TPU v7x, 32 devices: a whole 2x2x4 slice. The times are simulated.
32 devices in a mesh: dp: 16 (over z, x, core), blk: 2 (over y).
Axes of the slice: x: 2, y: 2, z: 4, core: 2. Of those that a mesh axis runs over, the one named last changes fastest.
Arguments:
- tokens: bfloat16 [32, 2048, 768], P('dp', 'blk'), may hold values from -6 to 6
- lengths: int32 [32], P('dp'), may hold values from 8 to 2048, as said below
- w_qkv: bfloat16 [768, 2304], P(('dp', 'blk')), may hold values from -0.21875 to 0.21875
- w_out: bfloat16 [768, 768], P(('dp', 'blk')), may hold values from -1.5 to 1.5
- w_gate: bfloat16 [768, 3072], P(('dp', 'blk')), may hold values from -0.21875 to 0.21875
- w_up: bfloat16 [768, 3072], P(('dp', 'blk')), may hold values from -0.21875 to 0.21875
- w_down: bfloat16 [3072, 768], P(('dp', 'blk')), may hold values from -0.109375 to 0.109375
- gain_one: bfloat16 [768], P(('dp', 'blk')), may hold values from 0.25 to 1.75
- gain_two: bfloat16 [768], P(('dp', 'blk')), may hold values from 0.25 to 1.75
- cotangent: bfloat16 [32, 2048, 768], P('dp', 'blk'), may hold values from -6 to 6
Outputs:
- output: bfloat16 [32, 2048, 768], P('dp', 'blk')
- grad_tokens: bfloat16 [32, 2048, 768], P('dp', 'blk')
- grad_w_qkv: float32 [768, 2304], P(('dp', 'blk'))
- grad_w_out: float32 [768, 768], P(('dp', 'blk'))
- grad_w_gate: float32 [768, 3072], P('dp', 'blk')
- grad_w_up: float32 [768, 3072], P('dp', 'blk')
- grad_w_down: float32 [3072, 768], P('blk', 'dp')
- grad_gain_one: float32 [768], P(('dp', 'blk'))
- grad_gain_two: float32 [768], P(('dp', 'blk'))
Inputs may be any that keep to these rules, and one draw needn't show every extreme that they name: `lengths`: among the 2 rows of each index of dp, one has length 2048; a row's positions from its length on are padding.
All inputs are finite; a program needn't handle non-finite values.
Results may differ from a plain program's by a relative error of at most 0.02.
Values may be sent and summed in bfloat16 or wider, within the bound.
A program may use at most 512 MiB of HBM per device.

v0:
```python
import jax
import jax.numpy as jnp
from jax import lax
from jax.sharding import PartitionSpec as P

HEADS = 12
HEAD = 64


epsilon = 1e-05
negative = -1e30


def passed_along(array, axis, by):
    devices = lax.axis_size(axis)
    return lax.ppermute(array, axis, [(i, (i + by) % devices) for i in range(devices)])


def tables(positions, head_size):
    half_size = head_size // 2
    index = jnp.arange(half_size, dtype=jnp.float32)
    inverse = jnp.power(1000.0, -2.0 * index / head_size)
    angles = positions.astype(jnp.float32)[:, None] * inverse[None, :]
    cosine = jnp.cos(angles)
    sine_part = jnp.sin(angles)
    return (jnp.concatenate([cosine, cosine], -1), jnp.concatenate([sine_part, sine_part], -1))


def rope(vector, cosine, sine_part):
    half_size = vector.shape[-1] // 2
    turned = jnp.concatenate([-vector[..., half_size:], vector[..., :half_size]], -1)
    return vector * cosine[:, None, :] + turned * sine_part[:, None, :]


def rope_back(grad_in, cosine, sine_part):
    half_size = grad_in.shape[-1] // 2
    sined = grad_in * sine_part[:, None, :]
    turned = jnp.concatenate([sined[..., half_size:], -sined[..., :half_size]], -1)
    return grad_in * cosine[:, None, :] + turned


def normalize(values, gain):
    mean_part = jnp.mean(values, axis=-1, keepdims=True)
    centered = values - mean_part
    variance = jnp.mean(centered * centered, axis=-1, keepdims=True)
    scale = lax.rsqrt(variance + epsilon)
    normed = centered * scale
    return (normed * gain, normed, scale)


def norm_back(grad_out, normed, scale, gain):
    inner = grad_out * gain
    grad_gain = jnp.sum(grad_out * normed, axis=0)
    centered = inner - jnp.mean(inner, axis=-1, keepdims=True)
    grad_in = scale * (centered - normed * jnp.mean(inner * normed, axis=-1, keepdims=True))
    return (grad_in, grad_gain)


def outer_sum(left, right):
    return lax.dot_general(
        left, right, (((0,), (0,)), ((), ())), preferred_element_type=jnp.float32
    )


def back_dot(grad_rows, weight):
    return lax.dot_general(
        grad_rows, weight, (((1,), (1,)), ((), ())), preferred_element_type=jnp.float32
    )


def body(tokens, lengths, w_qkv, w_out, w_gate, w_up, w_down, gain_one, gain_two, cotangent):
    full_qkv, full_out, full_gate, full_up, full_down, full_one, full_two = (
        lax.all_gather(w_qkv, ("dp", "blk"), axis=0, tiled=True),
        lax.all_gather(w_out, ("dp", "blk"), axis=0, tiled=True),
        lax.all_gather(w_gate, ("dp", "blk"), axis=0, tiled=True),
        lax.all_gather(w_up, ("dp", "blk"), axis=0, tiled=True),
        lax.all_gather(w_down, ("dp", "blk"), axis=0, tiled=True),
        lax.all_gather(gain_one, ("dp", "blk"), axis=0, tiled=True),
        lax.all_gather(gain_two, ("dp", "blk"), axis=0, tiled=True),
    )
    batch_rows, span_len, model_width = tokens.shape
    row_tokens = batch_rows * span_len
    gain_first = full_one.astype(jnp.float32)
    gain_second = full_two.astype(jnp.float32)
    cycle_size = lax.axis_size("blk")
    cycle_index = lax.axis_index("blk")
    hidden_width = full_gate.shape[1]
    unit_count = hidden_width // cycle_size
    unit_start = cycle_index * unit_count
    gate_slice = lax.dynamic_slice_in_dim(full_gate, unit_start, unit_count, 1)
    up_slice = lax.dynamic_slice_in_dim(full_up, unit_start, unit_count, 1)
    down_slice = lax.dynamic_slice_in_dim(full_down, unit_start, unit_count, 0)
    positions = cycle_index * span_len + jnp.arange(span_len, dtype=jnp.int32)
    cosine, sine_part = tables(positions, HEAD)
    flat = tokens.reshape(row_tokens, model_width)
    projected = jnp.dot(flat, full_qkv, preferred_element_type=jnp.float32).reshape(
        batch_rows, span_len, 3, HEADS, HEAD
    )
    queries = rope(projected[:, :, 0], cosine, sine_part).astype(jnp.bfloat16)
    key_side = rope(projected[:, :, 1], cosine, sine_part).astype(jnp.bfloat16)
    value_side = projected[:, :, 2].astype(jnp.bfloat16)

    def key_mask(start, count):
        key_pos = start + jnp.arange(count, dtype=jnp.int32)
        return (key_pos[None, :] < lengths[:, None])[:, None, None, :]

    start_max = jnp.full((batch_rows, HEADS, span_len), negative, jnp.float32)
    row_max = start_max
    key_piece = lax.all_gather(key_side, "blk", axis=1, tiled=True)
    value_piece = lax.all_gather(value_side, "blk", axis=1, tiled=True)
    allowed = key_mask(jnp.int32(0), key_piece.shape[1])
    scores = (
        jnp.einsum("rqhd,rkhd->rhqk", queries, key_piece, preferred_element_type=jnp.float32)
        * 0.125
    )
    scores = jnp.where(allowed, scores, negative)
    new_max = jnp.maximum(row_max, jnp.max(scores, axis=-1))
    weights = jnp.where(allowed, jnp.exp(scores - new_max[..., None]), 0.0)
    row_sum = jnp.sum(weights, axis=-1)
    update = jnp.einsum(
        "rhqk,rkhd->rqhd",
        weights.astype(jnp.bfloat16),
        value_piece,
        preferred_element_type=jnp.float32,
    )
    summed = update
    row_max, row_sum, summed = (new_max, row_sum, summed)
    attended = summed / jnp.transpose(row_sum, (0, 2, 1))[..., None]
    log_total = row_max + jnp.log(row_sum)
    attended_low = attended.astype(jnp.bfloat16).reshape(row_tokens, model_width)
    first = flat.astype(jnp.float32) + jnp.dot(
        attended_low, full_out, preferred_element_type=jnp.float32
    )
    hidden, normed_one, scale_one = normalize(first, gain_first)
    hidden_low = hidden.astype(jnp.bfloat16)
    whole_hidden = lax.all_gather(
        hidden_low.reshape(batch_rows, span_len, model_width), "blk", axis=1, tiled=True
    )
    group_tokens = whole_hidden.shape[0] * whole_hidden.shape[1]
    whole_hidden = whole_hidden.reshape(group_tokens, model_width)
    gate = jnp.dot(whole_hidden, gate_slice, preferred_element_type=jnp.float32)
    up_part = jnp.dot(whole_hidden, up_slice, preferred_element_type=jnp.float32)
    sigma = jax.nn.sigmoid(gate)
    silu_gate = gate * sigma
    active = (silu_gate * up_part).astype(jnp.bfloat16)
    active_local = lax.all_to_all(
        active.reshape(batch_rows, group_tokens // batch_rows, unit_count),
        "blk",
        split_axis=1,
        concat_axis=2,
        tiled=True,
    )
    second = hidden + jnp.dot(
        active_local.reshape(row_tokens, hidden_width),
        full_down,
        preferred_element_type=jnp.float32,
    )
    result, normed_two, scale_two = normalize(second, gain_second)
    output = result.astype(jnp.bfloat16).reshape(tokens.shape)
    grad_result = cotangent.reshape(row_tokens, model_width).astype(jnp.float32)
    grad_second, grad_gain_two = norm_back(grad_result, normed_two, scale_two, gain_second)
    grad_ffn = grad_second.astype(jnp.bfloat16)
    whole_grad = lax.all_gather(
        grad_ffn.reshape(batch_rows, span_len, model_width), "blk", axis=1, tiled=True
    ).reshape(group_tokens, model_width)
    grad_w_down = outer_sum(active, whole_grad)
    grad_active = back_dot(whole_grad, down_slice)
    grad_gate = (grad_active * up_part * sigma * (1.0 + gate * (1.0 - sigma))).astype(jnp.bfloat16)
    grad_up = (grad_active * silu_gate).astype(jnp.bfloat16)
    grad_w_gate = outer_sum(whole_hidden, grad_gate)
    grad_w_up = outer_sum(whole_hidden, grad_up)
    local_gate, local_up = (
        lax.all_to_all(
            grad_gate.reshape(batch_rows, group_tokens // batch_rows, unit_count),
            "blk",
            split_axis=1,
            concat_axis=2,
            tiled=True,
        ),
        lax.all_to_all(
            grad_up.reshape(batch_rows, group_tokens // batch_rows, unit_count),
            "blk",
            split_axis=1,
            concat_axis=2,
            tiled=True,
        ),
    )
    grad_hidden = (
        grad_second
        + back_dot(local_gate.reshape(row_tokens, hidden_width), full_gate)
        + back_dot(local_up.reshape(row_tokens, hidden_width), full_up)
    )
    grad_first, grad_gain_one = norm_back(grad_hidden, normed_one, scale_one, gain_first)
    grad_attn = grad_first.astype(jnp.bfloat16)
    grad_w_out = outer_sum(attended_low, grad_attn)
    grad_attended = (
        back_dot(grad_attn, full_out)
        .astype(jnp.bfloat16)
        .reshape(batch_rows, span_len, HEADS, HEAD)
    )
    delta = jnp.transpose(jnp.sum(grad_attended * attended, axis=-1), (0, 2, 1))

    def block_grads(key_piece, value_piece, anchor):
        allowed = key_mask(anchor * span_len, span_len)
        scores = (
            jnp.einsum("rqhd,rkhd->rhqk", queries, key_piece, preferred_element_type=jnp.float32)
            * 0.125
        )
        probs = jnp.where(allowed, jnp.exp(scores - log_total[..., None]), 0.0)
        part_values = jnp.einsum(
            "rhqk,rqhd->rkhd",
            probs.astype(jnp.bfloat16),
            grad_attended,
            preferred_element_type=jnp.float32,
        )
        grad_probs = jnp.einsum(
            "rqhd,rkhd->rhqk", grad_attended, value_piece, preferred_element_type=jnp.float32
        )
        grad_scores = (probs * (grad_probs - delta[..., None])).astype(jnp.bfloat16)
        part_queries = (
            jnp.einsum(
                "rhqk,rkhd->rqhd", grad_scores, key_piece, preferred_element_type=jnp.float32
            )
            * 0.125
        )
        part_keys = (
            jnp.einsum("rhqk,rqhd->rkhd", grad_scores, queries, preferred_element_type=jnp.float32)
            * 0.125
        )
        return (part_keys, part_values, part_queries)

    zero_block = jnp.zeros((batch_rows, span_len, HEADS, HEAD), jnp.float32)

    def cycle_step(step, carry):
        key_piece, value_piece, grad_keys, grad_values, grad_queries = carry
        anchor = (cycle_index - step) % cycle_size
        part_keys, part_values, part_queries = block_grads(key_piece, value_piece, anchor)
        grad_keys = grad_keys + part_keys
        grad_values = grad_values + part_values
        grad_queries = grad_queries + part_queries
        key_piece, value_piece = passed_along((key_piece, value_piece), "blk", 1)
        grad_keys, grad_values = (
            passed_along(grad_keys.astype(jnp.bfloat16), "blk", 1).astype(grad_keys.dtype),
            passed_along(grad_values.astype(jnp.bfloat16), "blk", 1).astype(grad_values.dtype),
        )
        return (key_piece, value_piece, grad_keys, grad_values, grad_queries)

    final_state = lax.fori_loop(
        0, cycle_size, cycle_step, (key_side, value_side, zero_block, zero_block, zero_block)
    )
    grad_keys, grad_values, grad_queries = (final_state[2], final_state[3], final_state[4])
    grad_projected = jnp.stack(
        [
            rope_back(grad_queries, cosine, sine_part),
            rope_back(grad_keys, cosine, sine_part),
            grad_values,
        ],
        axis=2,
    )
    grad_projected = grad_projected.astype(jnp.bfloat16).reshape(row_tokens, 3 * model_width)
    grad_w_qkv = outer_sum(flat, grad_projected)
    grad_tokens = (
        (grad_first + back_dot(grad_projected, full_qkv)).astype(jnp.bfloat16).reshape(tokens.shape)
    )
    sum_qkv, sum_out, sum_one, sum_two = (
        lax.psum_scatter(grad_w_qkv, ("dp", "blk"), scatter_dimension=0, tiled=True),
        lax.psum_scatter(grad_w_out, ("dp", "blk"), scatter_dimension=0, tiled=True),
        lax.psum_scatter(grad_gain_one, ("dp", "blk"), scatter_dimension=0, tiled=True),
        lax.psum_scatter(grad_gain_two, ("dp", "blk"), scatter_dimension=0, tiled=True),
    )
    sum_gate, sum_up, sum_down = (
        lax.psum_scatter(
            grad_w_gate.astype(jnp.bfloat16), "dp", scatter_dimension=0, tiled=True
        ).astype(jnp.float32),
        lax.psum_scatter(
            grad_w_up.astype(jnp.bfloat16), "dp", scatter_dimension=0, tiled=True
        ).astype(jnp.float32),
        lax.psum_scatter(
            grad_w_down.astype(jnp.bfloat16), "dp", scatter_dimension=1, tiled=True
        ).astype(jnp.float32),
    )
    return (output, grad_tokens, sum_qkv, sum_out, sum_gate, sum_up, sum_down, sum_one, sum_two)


def solution(mesh):
    return jax.shard_map(
        body,
        mesh=mesh,
        in_specs=(
            P("dp", "blk", None),
            P("dp"),
            P(("dp", "blk"), None),
            P(("dp", "blk"), None),
            P(("dp", "blk"), None),
            P(("dp", "blk"), None),
            P(("dp", "blk"), None),
            P(("dp", "blk")),
            P(("dp", "blk")),
            P("dp", "blk", None),
        ),
        out_specs=(
            P("dp", "blk", None),
            P("dp", "blk", None),
            P(("dp", "blk"), None),
            P(("dp", "blk"), None),
            P("dp", "blk"),
            P("dp", "blk"),
            P("blk", "dp"),
            P(("dp", "blk")),
            P(("dp", "blk")),
        ),
        check_vma=False,
    )
```

profile of v0, /device:TPU:0, one launch (start us, length us, event | category | flops | bytes accessed | tf_op | source)
XLA Modules:
  0.0 2495.5 jit_solution(5714352352352366496)
XLA Ops:
  9.4 64.5 %all-gather.11.cloned.1.call-done = bf16[768,2304]{1,0:T(8,128)(2,1)} async-done(((bf16[24,2304]{1,0:T(8,128)(2,1)}), bf16[768,2304]{1,0:T(8,128)(2,1)}) %all-gather.11.cloned.1.call-update) | async-done | bytes 3538960 | tf_op jit(solution)/shard_map/all_gather | solution.py:73
  128.8 39.5 %all-reduce.5 = (bf16[768]{0:T(1024)(128)(2,1)S(1)}, bf16[768]{0:T(1024)(128)(2,1)}) all-reduce(bf16[768]{0:T(1024)(128)(2,1)S(1)} %dynamic-update-slice, bf16[768]{0:T(1024)(128)(2,1)S(1)} %dynamic-update-slice.1), channel_id=1, replica_groups=mesh['dp'=16,'blk'=2] {'dp','blk'}, use_global_device_ids=true, to_apply=%add | all-reduce | flops 1536 | bytes 6144
  168.9 32.7 %all-gather.13.cloned.1.call-done = bf16[2,2048,12,64]{1,3,2,0:T(8,128)(2,1)} async-done(((bf16[2,1024,12,64]{1,3,2,0:T(8,128)(2,1)}), bf16[2,2048,12,64]{1,3,2,0:T(8,128)(2,1)}) %all-gather.13.cloned.1.call-update) | async-done | bytes 6291472 | tf_op jit(solution)/shard_map/all_gather | solution.py:109
  201.6 71.0 %fusion.10 = (f32[2,12,1024]{2,1,0:T(8,128)S(1)}, f32[2,12,1024,2048]{3,2,1,0:T(8,128)}) fusion(pred[2,2048]{1,0:T(4,128)(4,1)S(1)} %iota_compare_fusion, bf16[2,1024,12,64]{1,3,2,0:T(8,128)(2,1)S(1)} %get-tuple-element.564, bf16[2,2048,12,64]{1,3,2,0:T(8,128)(2,1)} %all-gather.13.cloned.1.call-done), kind=kOutput, calls=%fused_computation.16 | convolution fusion | flops 6593421312 | bytes 210866176 | tf_op jit(solution)/shard_map/rqhd,rkhd->rhqk/dot_general | solution.py:113
  273.3 61.1 %fusion.11 = f32[2,12,1024]{2,1,0:T(8,128)S(1)} fusion(f32[2,12,1024,2048]{3,2,1,0:T(8,128)} %get-tuple-element.469, f32[2,12,1024]{2,1,0:T(8,128)S(1)} %broadcast_maximum_fusion, pred[2,2048]{1,0:T(4,128)(4,1)S(1)} %iota_compare_fusion), kind=kLoop, calls=%fused_computation.17 | loop fusion | flops 251633664 | bytes 201527296 | tf_op jit(solution)/shard_map/reduce_sum | solution.py:119
  334.4 68.6 %fusion.33 = (bf16[2,1024,12,64]{1,3,2,0:T(8,128)(2,1)S(1)}, f32[2,12,64,1024]{3,2,1,0:T(8,128)}) fusion(f32[2,1024,12]{1,2,0:T(8,128)S(1)} %bitcast.198, f32[2,12,1024,2048]{3,2,1,0:T(8,128)} %get-tuple-element.469, f32[2,12,1024]{2,1,0:T(8,128)S(1)} %broadcast_maximum_fusion, pred[2,2048]{1,0:T(4,128)(4,1)S(1)} %iota_compare_fusion, ...), kind=kOutput, calls=%fused_computation.80 | convolution fusion | flops 6697254912 | bytes 217255936 | tf_op jit(solution)/shard_map/rhqk,rkhd->rqhd/dot_general | solution.py:120
  418.9 79.1 %all-gather.17.cloned.1.call-done = bf16[2,2048,768]{2,1,0:T(8,128)(2,1)} async-done(((bf16[2,1024,768]{2,1,0:T(8,128)(2,1)}), bf16[2,2048,768]{2,1,0:T(8,128)(2,1)}) %all-gather.17.cloned.1.call-update) | async-done | bytes 6291472 | tf_op jit(solution)/shard_map/all_gather | solution.py:136
  515.4 49.1 %all-gather.21.cloned.1.call-done = bf16[768,3072]{1,0:T(8,128)(2,1)} async-done(((bf16[24,3072]{1,0:T(8,128)(2,1)}), bf16[768,3072]{1,0:T(8,128)(2,1)}) %all-gather.21.cloned.1.call-update) | async-done | bytes 4718608 | tf_op jit(solution)/shard_map/all_gather | solution.py:76
  564.6 28.8 %multiply_convert_fusion.3 = (bf16[4096,1536]{1,0:T(8,128)(2,1)}, f32[4096,1536]{1,0:T(8,128)}) fusion(f32[4096,1536]{1,0:T(8,128)} %fusion.38, bf16[4096,768]{1,0:T(8,128)(2,1)} %bitcast.203, bf16[768,3072]{1,0:T(8,128)(2,1)} %all-gather.21.cloned.1.call-done, s32[]{:T(128)S(6)} %select_n.45), kind=kOutput, calls=%fused_computation.23 | convolution fusion | flops 9701425152 | bytes 71565312 | tf_op jit(solution)/shard_map/dot_general | solution.py:142
  626.7 137.2 %all-to-all-done = bf16[2,2048,1536]{2,0,1:T(2,128)(2,1)} async-done(((bf16[2,2048,1536]{2,0,1:T(2,128)(2,1)}), bf16[2,2048,1536]{2,0,1:T(2,128)(2,1)}, u32[]{:S(2)}, u32[]{:S(2)}) %all-to-all-start) | async-done | bytes 12582944 | tf_op jit(solution)/shard_map/all_to_all | solution.py:146
  772.2 70.2 %copy.46 = bf16[2,1024,2,1536]{3,2,1,0:T(2,128)(2,1)S(1)} copy(bf16[2,1024,2,1536]{3,1,2,0:T(8,128)(2,1)S(1)} %bitcast.172) | data formatting | bytes 25165824 | tf_op jit(solution)/shard_map/all_to_all | solution.py:146
  875.7 79.2 %all-gather.25.cloned.1.call-done = bf16[2,2048,768]{2,1,0:T(8,128)(2,1)} async-done(((bf16[2,1024,768]{2,1,0:T(8,128)(2,1)}), bf16[2,2048,768]{2,1,0:T(8,128)(2,1)}) %all-gather.25.cloned.1.call-update) | async-done | bytes 6291472 | tf_op jit(solution)/shard_map/all_gather | solution.py:163
  954.9 33.0 %multiply_convert_fusion.1 = (bf16[4096,1536]{1,0:T(8,128)(2,1)}, bf16[4096,1536]{1,0:T(8,128)(2,1)}) fusion(f32[4096,1536]{1,0:T(8,128)} %fusion.38, f32[4096,1536]{1,0:T(8,128)} %get-tuple-element.475, bf16[4096,768]{1,0:T(8,128)(2,1)} %bitcast.206, bf16[3072,768]{1,0:T(8,128)(2,1)} %all-gather.23.cloned.1.call-done, s32[]{:T(128)S(6)} %select_n.45), kind=kOutput, calls=%fused_computation.21 | convolution fusion | flops 9745465344 | bytes 84148224 | tf_op jit(solution)/shard_map/dot_general | solution.py:66
  1059.9 97.7 %all-to-all-done.1 = bf16[2,2048,1536]{2,0,1:T(2,128)(2,1)} async-done(((bf16[2,2048,1536]{2,0,1:T(2,128)(2,1)}), bf16[2,2048,1536]{2,0,1:T(2,128)(2,1)}, u32[]{:S(2)}, u32[]{:S(2)}) %all-to-all-start.1) | async-done | bytes 12582944 | tf_op jit(solution)/shard_map/all_to_all | solution.py:173
  1212.9 70.2 %copy.49 = bf16[2,1024,2,1536]{3,2,1,0:T(2,128)(2,1)S(1)} copy(bf16[2,1024,2,1536]{3,1,2,0:T(8,128)(2,1)S(1)} %bitcast.174) | data formatting | bytes 25165824 | tf_op jit(solution)/shard_map/all_to_all | solution.py:173
  1311.0 70.2 %copy.52 = bf16[2,1024,2,1536]{3,2,1,0:T(2,128)(2,1)S(1)} copy(bf16[2,1024,2,1536]{3,1,2,0:T(8,128)(2,1)S(1)} %bitcast.176) | data formatting | bytes 25165824 | tf_op jit(solution)/shard_map/all_to_all | solution.py:180
  1453.4 784.5 %while.24 = (s32[]{:T(128)}, bf16[2,1024,12,64]{1,3,2,0:T(8,128)(2,1)}, bf16[2,1024,12,64]{1,3,2,0:T(8,128)(2,1)}, f32[2,1024,12,64]{1,3,2,0:T(8,128)}, f32[2,10...) while((s32[]{:T(128)}, ...), condition=%wide.region_12.13_spmd.clone, body=%wide.region_11.12_spmd.clone.sunk | while | flops 16376663040 | bytes 588560896 | solution.py:248
  1459.6 36.4 %fusion.115 = f32[2,12,1024,1024]{3,2,1,0:T(8,128)} fusion(bf16[2,1024,12,64]{1,3,2,0:T(8,128)(2,1)} %get-tuple-element.596, bf16[2,1024,12,64]{1,3,2,0:T(8,128)(2,1)S(1)} %copy.80), kind=kOutput, calls=%fused_computation.120.clone.1 | convolution fusion | flops 3221225472 | bytes 106954752 | tf_op jit(solution)/shard_map/while/body/eval_jaxpr/rqhd,rkhd->rhqk/dot_general | solution.py:206
  1496.1 58.0 %multiply_convert_fusion.7 = bf16[2,12,1024,1024]{3,2,1,0:T(8,128)(2,1)} fusion(f32[2,12,1024,1024]{3,2,1,0:T(8,128)} %fusion.115, f32[2,12,1024]{2,1,0:T(8,128)S(1)} %get-tuple-element.599, f32[2,12,1024]{2,1,0:T(8,128)} %get-tuple-element.597, pred[2,1024]{1,0:T(4,128)(4,1)S(1)} %broadcast_compare_fusion.2, ...), kind=kOutput, calls=%fused_computation.clone.1 | convolution fusion | flops 3372220416 | bytes 157485056 | tf_op jit(solution)/shard_map/while/body/eval_jaxpr/rqhd,rkhd->rhqk/dot_general | solution.py:216
  1574.9 36.0 %fusion.117 = bf16[2,1024,12,64]{1,3,2,0:T(8,128)(2,1)} fusion(f32[2,1024,12,64]{1,3,2,0:T(8,128)} %get-tuple-element.576, pred[]{:T(512)S(6)} %compare.4, bf16[2,1024,12,64]{1,3,2,0:T(8,128)(2,1)} %get-tuple-element.598, f32[2,12,1024,1024]{3,2,1,0:T(8,128)} %fusion.115, f32[2,12,1024]{2,1,0:T(8,128)} %get-tuple-element.597, ...), kind=kOutput, calls=%fused_computation.7.clone.1 | convolution fusion | flops 3326607360 | bytes 113346560 | tf_op jit(solution)/shard_map/while/body/eval_jaxpr/rhqk,rqhd->rkhd/dot_general | solution.py:210
  1651.2 62.1 %collective-permute-done.3 = bf16[2,1024,12,64]{1,3,2,0:T(8,128)(2,1)} collective-permute-done((bf16[2,1024,12,64]{1,3,2,0:T(8,128)(2,1)}, bf16[2,1024,12,64]{1,3,2,0:T(8,128)(2,1)}, u32[]{:S(2)}, u32[]{:S(2)}) %collective-permute-start.3) | collective-permute-done | bytes 3145760 | tf_op jit(solution)/shard_map/while/body/eval_jaxpr/ppermute | solution.py:16
  1718.6 62.1 %collective-permute-done = bf16[2,1024,12,64]{1,3,2,0:T(8,128)(2,1)} collective-permute-done((bf16[2,1024,12,64]{1,3,2,0:T(8,128)(2,1)S(1)}, bf16[2,1024,12,64]{1,3,2,0:T(8,128)(2,1)}, u32[]{:S(2)}, u32[]{:S(2)}) %collective-permute-start) | collective-permute-done | bytes 3145760 | tf_op jit(solution)/shard_map/while/body/eval_jaxpr/ppermute | solution.py:16
  1780.7 64.4 %collective-permute-done.1 = bf16[2,1024,12,64]{1,3,2,0:T(8,128)(2,1)} collective-permute-done((bf16[2,1024,12,64]{1,3,2,0:T(8,128)(2,1)}, bf16[2,1024,12,64]{1,3,2,0:T(8,128)(2,1)}, u32[]{:S(2)}, u32[]{:S(2)}) %collective-permute-start.1) | collective-permute-done | bytes 3145760 | tf_op jit(solution)/shard_map/while/body/eval_jaxpr/ppermute | solution.py:16
  1851.1 36.4 %fusion.115 = f32[2,12,1024,1024]{3,2,1,0:T(8,128)} fusion(bf16[2,1024,12,64]{1,3,2,0:T(8,128)(2,1)} %get-tuple-element.596, bf16[2,1024,12,64]{1,3,2,0:T(8,128)(2,1)S(1)} %copy.80), kind=kOutput, calls=%fused_computation.120.clone.1 | convolution fusion | flops 3221225472 | bytes 106954752 | tf_op jit(solution)/shard_map/while/body/eval_jaxpr/rqhd,rkhd->rhqk/dot_general | solution.py:206
  1887.6 58.0 %multiply_convert_fusion.7 = bf16[2,12,1024,1024]{3,2,1,0:T(8,128)(2,1)} fusion(f32[2,12,1024,1024]{3,2,1,0:T(8,128)} %fusion.115, f32[2,12,1024]{2,1,0:T(8,128)S(1)} %get-tuple-element.599, f32[2,12,1024]{2,1,0:T(8,128)} %get-tuple-element.597, pred[2,1024]{1,0:T(4,128)(4,1)S(1)} %broadcast_compare_fusion.2, ...), kind=kOutput, calls=%fused_computation.clone.1 | convolution fusion | flops 3372220416 | bytes 157485056 | tf_op jit(solution)/shard_map/while/body/eval_jaxpr/rqhd,rkhd->rhqk/dot_general | solution.py:216
  1968.5 37.7 %fusion.117 = bf16[2,1024,12,64]{1,3,2,0:T(8,128)(2,1)} fusion(f32[2,1024,12,64]{1,3,2,0:T(8,128)} %get-tuple-element.576, pred[]{:T(512)S(6)} %compare.4, bf16[2,1024,12,64]{1,3,2,0:T(8,128)(2,1)} %get-tuple-element.598, f32[2,12,1024,1024]{3,2,1,0:T(8,128)} %fusion.115, f32[2,12,1024]{2,1,0:T(8,128)} %get-tuple-element.597, ...), kind=kOutput, calls=%fused_computation.7.clone.1 | convolution fusion | flops 3326607360 | bytes 113346560 | tf_op jit(solution)/shard_map/while/body/eval_jaxpr/rhqk,rqhd->rkhd/dot_general | solution.py:210
  2009.7 24.5 bitcast_add_fusion.4
  2044.6 62.1 %collective-permute-done.3 = bf16[2,1024,12,64]{1,3,2,0:T(8,128)(2,1)} collective-permute-done((bf16[2,1024,12,64]{1,3,2,0:T(8,128)(2,1)}, bf16[2,1024,12,64]{1,3,2,0:T(8,128)(2,1)}, u32[]{:S(2)}, u32[]{:S(2)}) %collective-permute-start.3) | collective-permute-done | bytes 3145760 | tf_op jit(solution)/shard_map/while/body/eval_jaxpr/ppermute | solution.py:16
  2111.9 62.1 %collective-permute-done = bf16[2,1024,12,64]{1,3,2,0:T(8,128)(2,1)} collective-permute-done((bf16[2,1024,12,64]{1,3,2,0:T(8,128)(2,1)S(1)}, bf16[2,1024,12,64]{1,3,2,0:T(8,128)(2,1)}, u32[]{:S(2)}, u32[]{:S(2)}) %collective-permute-start) | collective-permute-done | bytes 3145760 | tf_op jit(solution)/shard_map/while/body/eval_jaxpr/ppermute | solution.py:16
  2174.1 63.5 %collective-permute-done.1 = bf16[2,1024,12,64]{1,3,2,0:T(8,128)(2,1)} collective-permute-done((bf16[2,1024,12,64]{1,3,2,0:T(8,128)(2,1)}, bf16[2,1024,12,64]{1,3,2,0:T(8,128)(2,1)}, u32[]{:S(2)}, u32[]{:S(2)}) %collective-permute-start.1) | collective-permute-done | bytes 3145760 | tf_op jit(solution)/shard_map/while/body/eval_jaxpr/ppermute | solution.py:16
  2341.8 39.6 %all-reduce.4 = (f32[768]{0:T(1024)S(1)}, f32[768]{0:T(1024)S(1)}) all-reduce(f32[768]{0:T(1024)S(1)} %copy-done.25, f32[768]{0:T(1024)S(1)} %copy-done.24), channel_id=8, replica_groups=mesh['dp'=16,'blk'=2] {'dp','blk'}, use_global_device_ids=true, to_apply=%region_19.20.clone | all-reduce | flops 1536 | bytes 12288
  2396.8 92.0 %reduce-scatter.16.cloned.1.call-done = f32[24,2304]{1,0:T(8,128)} async-done(((f32[768,2304]{1,0:T(8,128)}), f32[24,2304]{1,0:T(8,128)}) %reduce-scatter.16.cloned.1.call-update) | async-done | bytes 221200
  (213 shorter events, 632.9 us)
Async XLA Ops:
  7.2 66.7 %all-gather.11.cloned.1.call-start = ((), (), s32[]{:S(2)}) async-start(), calls=%async_computation.8 | async-start | bytes 3649536 | tf_op jit(solution)/shard_map/all_gather | solution.py:73
  7.9 193.7 %all-gather.13.cloned.1.call-start = ((), (), s32[]{:S(2)}) async-start(), calls=%async_computation.9 | async-start | bytes 9437184 | tf_op jit(solution)/shard_map/all_gather | solution.py:109
  120.8 80.8 %copy-start = (bf16[2,1024,12,64]{1,3,2,0:T(8,128)(2,1)}, bf16[2,1024,12,64]{1,3,2,0:T(8,128)(2,1)S(1)}, u32[]{:S(2)}) copy-start(bf16[2,1024,12,64]{1,3,2,0:T(8,128)(2,1)S(1)} %get-tuple-element.564) | copy-start | bytes 9437188
  120.9 213.5 %all-gather.27.cloned.1.call-start = ((), (), s32[]{:S(2)}) async-start(), calls=%async_computation.20 | async-start | bytes 9437184 | tf_op jit(solution)/shard_map/all_gather | solution.py:110
  127.0 280.3 %all-gather.15.cloned.1.call-start = ((), (), s32[]{:S(2)}) async-start(), calls=%async_computation.10 | async-start | bytes 1216512 | tf_op jit(solution)/shard_map/all_gather | solution.py:74
  127.6 291.3 %all-gather.19.cloned.1.call-start = ((), (), s32[]{:S(2)}) async-start(), calls=%async_computation.12 | async-start | bytes 4866048 | tf_op jit(solution)/shard_map/all_gather | solution.py:75
  128.2 369.8 %all-gather.17.cloned.1.call-start = ((), (), s32[]{:S(2)}) async-start(), calls=%async_computation.11 | async-start | bytes 9437184 | tf_op jit(solution)/shard_map/all_gather | solution.py:136
  334.4 68.6 %copy-start.11 = (f32[2,12,1024]{2,1,0:T(8,128)}, f32[2,12,1024]{2,1,0:T(8,128)S(1)}, u32[]{:S(2)}) copy-start(f32[2,12,1024]{2,1,0:T(8,128)S(1)} %fusion.11) | copy-start | bytes 294916
  413.8 436.5 %copy-start.15 = (f32[2048]{0:T(1024)}, f32[2048]{0:T(1024)S(1)}, u32[]{:S(2)}) copy-start(f32[2048]{0:T(1024)S(1)} %broadcast_multiply_fusion.6) | copy-start | bytes 24580
  414.7 435.6 %copy-start.17 = (f32[2048]{0:T(1024)}, f32[2048]{0:T(1024)S(1)}, u32[]{:S(2)}) copy-start(f32[2048]{0:T(1024)S(1)} %add_rsqrt_fusion.1) | copy-start | bytes 24580
  417.4 147.2 %all-gather.21.cloned.1.call-start = ((), (), s32[]{:S(2)}) async-start(), calls=%async_computation.13 | async-start | bytes 4866048 | tf_op jit(solution)/shard_map/all_gather | solution.py:76
  418.1 432.2 %all-gather.23.cloned.1.call-start = ((), (), s32[]{:S(2)}) async-start(), calls=%async_computation.14 | async-start | bytes 4866048 | tf_op jit(solution)/shard_map/all_gather | solution.py:77
  617.2 146.7 %all-to-all-start = ((bf16[2,2048,1536]{2,0,1:T(2,128)(2,1)}), bf16[2,2048,1536]{2,0,1:T(2,128)(2,1)}, u32[]{:S(2)}, u32[]{:S(2)}) async-start(bf16[2,2048,1536]{2,0,1:T(2,128)(2,1)} %copy.44), calls=%async_computation | async-start | bytes 25165824 | tf_op jit(solution)/shard_map/all_to_all | solution.py:146
  625.9 329.0 %all-gather.25.cloned.1.call-start = ((), (), s32[]{:S(2)}) async-start(), calls=%async_computation.15 | async-start | bytes 9437184 | tf_op jit(solution)/shard_map/all_gather | solution.py:163
  1011.7 146.0 %all-to-all-start.1 = ((bf16[2,2048,1536]{2,0,1:T(2,128)(2,1)}), bf16[2,2048,1536]{2,0,1:T(2,128)(2,1)}, u32[]{:S(2)}, u32[]{:S(2)}) async-start(bf16[2,2048,1536]{2,0,1:T(2,128)(2,1)} %copy.47), calls=%async_computation.1 | async-start | bytes 25165824 | tf_op jit(solution)/shard_map/all_to_all | solution.py:173
  1020.1 1316.5 %reduce-scatter.14.cloned.1.call-start = ((), (), s32[]{:S(2)}) async-start(), calls=%async_computation.19 | async-start | bytes 2506752 | tf_op jit(solution)/shard_map/reduce_scatter | solution.py:278
  1157.7 145.1 %all-to-all-start.2 = ((bf16[2,2048,1536]{2,0,1:T(2,128)(2,1)}), bf16[2,2048,1536]{2,0,1:T(2,128)(2,1)}, u32[]{:S(2)}, u32[]{:S(2)}) async-start(bf16[2,2048,1536]{2,0,1:T(2,128)(2,1)} %copy.50), calls=%async_computation.2 | async-start | bytes 25165824 | tf_op jit(solution)/shard_map/all_to_all | solution.py:180
  1166.1 1172.3 %reduce-scatter.12.cloned.1.call-start = ((), (), s32[]{:S(2)}) async-start(), calls=%async_computation.18 | async-start | bytes 2506752 | tf_op jit(solution)/shard_map/reduce_scatter | solution.py:275
  1182.3 1157.8 %reduce-scatter.10.cloned.1.call-start = ((), (), s32[]{:S(2)}) async-start(), calls=%async_computation.17 | async-start | bytes 2506752 | tf_op jit(solution)/shard_map/reduce_scatter | solution.py:272
  1204.5 1192.4 %reduce-scatter.8.cloned.1.call-start = ((), (), s32[]{:S(2)}) async-start(), calls=%async_computation.16 | async-start | bytes 2433024 | tf_op jit(solution)/shard_map/reduce_scatter | solution.py:267
  1453.4 784.5 %copy-start.10 = (f32[1024,64]{0,1:T(8,128)S(1)}, f32[1024,64]{0,1:T(8,128)}, u32[]{:S(2)}) copy-start(f32[1024,64]{0,1:T(8,128)} %get-tuple-element.482) | copy-start | bytes 786436
  1574.6 71.4 %collective-permute-start.2 = (bf16[2,1024,12,64]{1,3,2,0:T(8,128)(2,1)}, bf16[2,1024,12,64]{1,3,2,0:T(8,128)(2,1)}, u32[]{:S(2)}, u32[]{:S(2)}) collective-permute-start(bf16[2,1024,12,64]{1,3,2,0:T(8,128)(2,1)} %fusion.116), channel_id=1, source_target_pairs={{0,1},{1,0},{2,3},{3,2},{4,5},{5,4},{6,7},{7,6},{8,9},{9,8},{10,11... | collective-permute-start | bytes 9437192 | tf_op jit(solution)/shard_map/while/body/eval_jaxpr/ppermute | solution.py:16
  1610.8 102.5 %collective-permute-start.3 = (bf16[2,1024,12,64]{1,3,2,0:T(8,128)(2,1)}, bf16[2,1024,12,64]{1,3,2,0:T(8,128)(2,1)}, u32[]{:S(2)}, u32[]{:S(2)}) collective-permute-start(bf16[2,1024,12,64]{1,3,2,0:T(8,128)(2,1)} %fusion.117), channel_id=1, source_target_pairs={{0,1},{1,0},{2,3},{3,2},{4,5},{5,4},{6,7},{7,6},{8,9},{9,8},{10,11... | collective-permute-start | bytes 9437192 | tf_op jit(solution)/shard_map/while/body/eval_jaxpr/ppermute | solution.py:16
  1612.5 168.2 %collective-permute-start = (bf16[2,1024,12,64]{1,3,2,0:T(8,128)(2,1)S(1)}, bf16[2,1024,12,64]{1,3,2,0:T(8,128)(2,1)}, u32[]{:S(2)}, u32[]{:S(2)}) collective-permute-start(bf16[2,1024,12,64]{1,3,2,0:T(8,128)(2,1)S(1)} %copy.80), channel_id=1, source_target_pairs={{0,1},{1,0},{2,3},{3,2},{4,5},{5,4},{6,7},{7,6},{8,9},{9,8},{10,11... | collective-permute-start | bytes 9437192 | tf_op jit(solution)/shard_map/while/body/eval_jaxpr/ppermute | solution.py:16
  1612.9 232.3 %collective-permute-start.1 = (bf16[2,1024,12,64]{1,3,2,0:T(8,128)(2,1)}, bf16[2,1024,12,64]{1,3,2,0:T(8,128)(2,1)}, u32[]{:S(2)}, u32[]{:S(2)}) collective-permute-start(bf16[2,1024,12,64]{1,3,2,0:T(8,128)(2,1)} %copy.81), channel_id=1, source_target_pairs={{0,1},{1,0},{2,3},{3,2},{4,5},{5,4},{6,7},{7,6},{8,9},{9,8},{10,11... | collective-permute-start | bytes 9437192 | tf_op jit(solution)/shard_map/while/body/eval_jaxpr/ppermute | solution.py:16
  1651.2 193.9 %copy-start.23 = (s32[2]{0:T(128)S(1)}, s32[2]{0:T(128)}, u32[]{:S(2)}) copy-start(s32[2]{0:T(128)} %get-tuple-element.673) | copy-start | bytes 28 | tf_op jit(solution)/shard_map/while
  1967.9 71.4 %collective-permute-start.2 = (bf16[2,1024,12,64]{1,3,2,0:T(8,128)(2,1)}, bf16[2,1024,12,64]{1,3,2,0:T(8,128)(2,1)}, u32[]{:S(2)}, u32[]{:S(2)}) collective-permute-start(bf16[2,1024,12,64]{1,3,2,0:T(8,128)(2,1)} %fusion.116), channel_id=1, source_target_pairs={{0,1},{1,0},{2,3},{3,2},{4,5},{5,4},{6,7},{7,6},{8,9},{9,8},{10,11... | collective-permute-start | bytes 9437192 | tf_op jit(solution)/shard_map/while/body/eval_jaxpr/ppermute | solution.py:16
  2006.2 100.4 %collective-permute-start.3 = (bf16[2,1024,12,64]{1,3,2,0:T(8,128)(2,1)}, bf16[2,1024,12,64]{1,3,2,0:T(8,128)(2,1)}, u32[]{:S(2)}, u32[]{:S(2)}) collective-permute-start(bf16[2,1024,12,64]{1,3,2,0:T(8,128)(2,1)} %fusion.117), channel_id=1, source_target_pairs={{0,1},{1,0},{2,3},{3,2},{4,5},{5,4},{6,7},{7,6},{8,9},{9,8},{10,11... | collective-permute-start | bytes 9437192 | tf_op jit(solution)/shard_map/while/body/eval_jaxpr/ppermute | solution.py:16
  2007.7 166.4 %collective-permute-start = (bf16[2,1024,12,64]{1,3,2,0:T(8,128)(2,1)S(1)}, bf16[2,1024,12,64]{1,3,2,0:T(8,128)(2,1)}, u32[]{:S(2)}, u32[]{:S(2)}) collective-permute-start(bf16[2,1024,12,64]{1,3,2,0:T(8,128)(2,1)S(1)} %copy.80), channel_id=1, source_target_pairs={{0,1},{1,0},{2,3},{3,2},{4,5},{5,4},{6,7},{7,6},{8,9},{9,8},{10,11... | collective-permute-start | bytes 9437192 | tf_op jit(solution)/shard_map/while/body/eval_jaxpr/ppermute | solution.py:16
  2008.2 229.3 %collective-permute-start.1 = (bf16[2,1024,12,64]{1,3,2,0:T(8,128)(2,1)}, bf16[2,1024,12,64]{1,3,2,0:T(8,128)(2,1)}, u32[]{:S(2)}, u32[]{:S(2)}) collective-permute-start(bf16[2,1024,12,64]{1,3,2,0:T(8,128)(2,1)} %copy.81), channel_id=1, source_target_pairs={{0,1},{1,0},{2,3},{3,2},{4,5},{5,4},{6,7},{7,6},{8,9},{9,8},{10,11... | collective-permute-start | bytes 9437192 | tf_op jit(solution)/shard_map/while/body/eval_jaxpr/ppermute | solution.py:16
  2044.6 193.0 %copy-start.23 = (s32[2]{0:T(128)S(1)}, s32[2]{0:T(128)}, u32[]{:S(2)}) copy-start(s32[2]{0:T(128)} %get-tuple-element.673) | copy-start | bytes 28 | tf_op jit(solution)/shard_map/while
  2265.2 223.6 %reduce-scatter.16.cloned.1.call-start = ((), (), s32[]{:S(2)}) async-start(), calls=%async_computation.21 | async-start | bytes 7299072
  (27 other events, 230.7 us)
Sparse Core Ops, SparseCore 0:
  10.9 62.8 all-gather.10
  121.0 80.5 all-gather.12
  203.8 80.3 all-gather.26
  286.9 54.1 all-gather.14
  343.9 62.5 all-gather.18
  417.5 80.4 all-gather.16
  500.9 63.6 all-gather.20
  567.5 62.4 all-gather.22
  875.8 79.0 all-gather.24
  1036.2 64.3 reduce-scatter.13
  1182.5 64.3 reduce-scatter.11
  1250.4 61.9 reduce-scatter.9
  2265.3 99.2 reduce-scatter.7
  2370.7 118.0 reduce-scatter.15
where the time goes:
time: 2500 us
  waiting for transfers between devices  1040 us (42%)
  matrix products  726 us (29%)
  local copies, waits for them, and re-layouts  426 us (17%)
  other arithmetic  178 us (7%)
  blocking collectives  79.1 us (3%)
  starting transfers between devices  34.2 us (1%)
    ppermute x8, waiting for transfers between devices, passed_along(): lax.ppermute(array, axis, [(i, (i + by) % devices) for i in range(devices)])  390 us
    all_to_all x1, waiting for transfers between devices, body(): lax.all_to_all(active.reshape(batch_rows, group_tokens // batch_rows, uni...  137 us
    dot_general x2, matrix products, block_grads(): jnp.einsum('rqhd,rkhd->rhqk', grad_attended, value_piece, preferred_eleme...  116 us
    all_to_all x1, waiting for transfers between devices, body(): lax.all_to_all(grad_gate.reshape(batch_rows, group_tokens // batch_rows,...  97.7 us
    unnamed x15, waiting for transfers between devices  95.2 us
    dot_general x5, matrix products, back_dot(): lax.dot_general(grad_rows, weight, (((1,), (1,)), ((), ())), preferred_el...  88 us
    all_gather x1, waiting for transfers between devices, body(): lax.all_gather(grad_ffn.reshape(batch_rows, span_len, model_width), 'blk'...  79.2 us
    unnamed x2, blocking collectives  79.1 us
  transfers between devices with their start and end apart: 25, of which 17 were waited for; matrix products, arithmetic and copies ran while one was open for 48% of the time, Pallas kernels for 0%

commit v1 on v0

v1 whole, which is shorter than its diff:
```python
import functools

import jax
import jax.numpy as jnp
import numpy as np
from jax import lax
from jax.experimental import pallas as pl
from jax.experimental.pallas import tpu as pltpu
from jax.sharding import PartitionSpec as P

HEADS = 12
HEAD = 64
PAIR = 2 * HEAD
EPS = 1e-05
NEG = -1e30
LOG2E = 1.4426950408889634
LN2 = 0.6931471805599453
VMEM_LIMIT = 60 * 1024 * 1024

BF = jnp.bfloat16
F32 = jnp.float32


def dot(a, b):
    return lax.dot_general(a, b, (((1,), (0,)), ((), ())), preferred_element_type=F32)


def dot_nt(a, b):
    return lax.dot_general(a, b, (((1,), (1,)), ((), ())), preferred_element_type=F32)


def params(limit=VMEM_LIMIT):
    return pltpu.CompilerParams(vmem_limit_bytes=limit)


def lanes(shape):
    return lax.broadcasted_iota(jnp.int32, shape, 1)


def turn(u):
    low_half = (lanes(u.shape) % HEAD) < HEAD // 2
    return jnp.where(low_half, -pltpu.roll(u, PAIR - HEAD // 2, 1), pltpu.roll(u, HEAD // 2, 1))


def qkv_kernel(x_ref, w_ref, cos_ref, sin_ref, q_ref, k_ref, v_ref, xt_ref):
    x = x_ref[...]
    width = x.shape[1]
    cosine, sine = cos_ref[...], sin_ref[...]
    for part, out in ((0, q_ref), (1, k_ref), (2, v_ref)):
        for pair in range(width // PAIR):
            at = part * width + pair * PAIR
            if pair % 2 == 0:
                u2 = dot(x, w_ref[:, at : at + 2 * PAIR])
            u = u2[:, (pair % 2) * PAIR : (pair % 2 + 1) * PAIR]
            if part < 2:
                u = u * cosine + turn(u) * sine
            if part == 0:
                u = u * (0.125 * LOG2E)
            out[:, pair * PAIR : (pair + 1) * PAIR] = u.astype(BF)
    xt_ref[...] = x.T


def qkv_call(x, w, cosine, sine, tile=512):
    tokens, width = x.shape
    span = cosine.shape[0]
    tile = min(tile, span)
    row = pl.BlockSpec((tile, width), lambda i: (i, 0))
    table = pl.BlockSpec((tile, PAIR), lambda i: (i % (span // tile), 0))
    return pl.pallas_call(
        qkv_kernel,
        grid=(tokens // tile,),
        in_specs=[
            row,
            pl.BlockSpec(w.shape, lambda i: (0, 0), pipeline_mode=pl.Buffered(1)),
            table,
            table,
        ],
        out_specs=[row, row, row, pl.BlockSpec((width, tile), lambda i: (0, i))],
        out_shape=[jax.ShapeDtypeStruct((tokens, width), BF)] * 3
        + [jax.ShapeDtypeStruct((width, tokens), BF)],
        compiler_params=params(),
        name="qkv",
    )(x, w, cosine, sine)


def attend_kernel(q_ref, k_ref, v_ref, bias_ref, o_ref, aug_ref, ka, va):
    keys = k_ref.shape[1]

    @pl.when(pl.program_id(2) == 0)
    def _():
        lane = lanes((keys, PAIR))
        k, v = k_ref[0], v_ref[0]
        zero = jnp.zeros_like(k)
        for h in range(2):
            mine = (lane // HEAD) == h
            ka[h, :, :PAIR] = jnp.where(mine, k, zero)
            ka[h, :, PAIR:] = bias_ref[0]
            va[h, :, :PAIR] = jnp.where(mine, v, zero)
            va[h, :, PAIR:] = mine.astype(F32).astype(BF)

    q = q_ref[0]
    lane = lanes(q.shape)
    qa = jnp.concatenate([q, (lane == 3).astype(F32).astype(BF)], axis=1)
    acc = None
    tops = []
    for h in range(2):
        s = dot_nt(qa, ka[h])
        top = jnp.max(s, axis=1, keepdims=True)
        p = jnp.exp2(s - top).astype(BF)
        part = dot(p, va[h])
        acc = part if acc is None else acc + part
        tops.append(top)
    total = acc[:, PAIR:]
    o_ref[0] = (acc[:, :PAIR] / total).astype(BF)
    lse = jnp.where(lane < HEAD, tops[0], tops[1]) + jnp.log2(total)
    aug_ref[0] = spread(lse, jnp.where(lane == 3, 1.0, 0.0))


def spread(value, other):
    high = value.astype(BF).astype(F32)
    rest = value - high
    mid = rest.astype(BF).astype(F32)
    low = rest - mid
    sub = lanes(value.shape) % HEAD
    return jnp.where(
        sub == 0, high, jnp.where(sub == 1, mid, jnp.where(sub == 2, low, other))
    ).astype(BF)


def attend_call(q, k, v, bias, tile=256):
    rows, span, width = q.shape
    keys = k.shape[1]
    tile = min(tile, span)
    qs = pl.BlockSpec((1, tile, PAIR), lambda r, p, i: (r, i, p))
    ks = pl.BlockSpec((1, keys, PAIR), lambda r, p, i: (r, 0, p))
    return pl.pallas_call(
        attend_kernel,
        grid=(rows, width // PAIR, span // tile),
        in_specs=[qs, ks, ks, pl.BlockSpec((1, keys, PAIR), lambda r, p, i: (r, 0, 0))],
        out_specs=[qs, qs],
        out_shape=[jax.ShapeDtypeStruct(q.shape, BF)] * 2,
        scratch_shapes=[
            pltpu.VMEM((2, keys, 2 * PAIR), BF),
            pltpu.VMEM((2, keys, 2 * PAIR), BF),
        ],
        compiler_params=params(),
        name="attend",
    )(q, k, v, bias)


def attend_back_kernel(
    tk, tq, q_ref, k_ref, v_ref, bias_ref, o_ref, do_ref, aug_ref, cq_ref, sq_ref, ck_ref, sk_ref,
    dq_ref, dk_ref, dv_ref, qa, ka, va, da, qm, dm, kt, dqt, dk_acc, dv_acc,
):
    keys, span = k_ref.shape[1], q_ref.shape[1]

    lane_k = lanes((keys, PAIR))
    lane_q = lanes((span, PAIR))
    q, k, v, do = q_ref[0], k_ref[0], v_ref[0], do_ref[0]
    bias = bias_ref[0].astype(F32)
    prod = do.astype(F32) * o_ref[0].astype(F32)
    first = prod.astype(BF)
    second = (prod - first.astype(F32)).astype(BF)
    block = (
        (lax.broadcasted_iota(jnp.int32, (PAIR, PAIR), 0) // HEAD)
        == (lax.broadcasted_iota(jnp.int32, (PAIR, PAIR), 1) // HEAD)
    ).astype(F32).astype(BF)
    delta = dot(first, block) + dot(second, block)
    qa[:, :PAIR] = q
    qa[:, PAIR:] = aug_ref[0]
    da[:, :PAIR] = do
    da[:, PAIR:] = spread(delta, jnp.zeros_like(delta))
    for h in range(2):
        mine_k = (lane_k // HEAD) == h
        mine_q = (lane_q // HEAD) == h
        minus = jnp.where(mine_k & (lane_k % HEAD < 3), -1.0, 0.0)
        ka[h, :, :PAIR] = jnp.where(mine_k, k, jnp.zeros_like(k))
        ka[h, :, PAIR:] = (minus + bias).astype(BF)
        va[h, :, :PAIR] = jnp.where(mine_k, v, jnp.zeros_like(v))
        va[h, :, PAIR:] = minus.astype(BF)
        qm[h] = jnp.where(mine_q, q, jnp.zeros_like(q))
        dm[h] = jnp.where(mine_q, do, jnp.zeros_like(do))
    kt[...] = k.T
    dqt[...] = jnp.zeros_like(dqt)

    nq, nk = span // tq, keys // tk

    def key_step(j, _):
        at_k = pl.ds(pl.multiple_of(j * tk, tk), tk)
        dk_acc[...] = jnp.zeros_like(dk_acc)
        dv_acc[...] = jnp.zeros_like(dv_acc)

        def query_step(i, _):
            at_q = pl.ds(pl.multiple_of(i * tq, tq), tq)
            dv, dk = None, None
            for h in range(2):
                st = dot_nt(ka[h, at_k, :], qa[at_q, :])
                dpt = dot_nt(va[h, at_k, :], da[at_q, :])
                p = jnp.exp2(st)
                ds = (p * dpt).astype(BF)
                pv = dot(p.astype(BF), dm[h, at_q, :])
                pk = dot(ds, qm[h, at_q, :])
                dv = pv if dv is None else dv + pv
                dk = pk if dk is None else dk + pk
                head = slice(h * HEAD, (h + 1) * HEAD)
                dqt[head, at_q] += dot(kt[head, at_k], ds)
            dv_acc[...] += dv
            dk_acc[...] += dk
            return 0

        lax.fori_loop(0, nq, query_step, 0, unroll=True)
        dv_ref[0, at_k, :] = dv_acc[...].astype(dv_ref.dtype)
        g = dk_acc[...] * LN2
        if dk_ref.dtype == BF:
            g = back_turn(g, ck_ref[at_k, :], sk_ref[at_k, :])
        dk_ref[0, at_k, :] = g.astype(dk_ref.dtype)
        return 0

    lax.fori_loop(0, nk, key_step, 0)
    g = dqt[...].T * 0.125
    dq_ref[0] = back_turn(g, cq_ref[...], sq_ref[...]).astype(BF)


def back_turn(g, cosine, sine):
    return g * cosine - turn(g * sine)


def attend_back_call(q, k, v, bias, o, do, aug, cq, sq, ck, sk, whole, tk=512, tq=512):
    rows, span, width = q.shape
    keys = k.shape[1]
    tq = min(tq, span)
    tk = min(tk, keys)
    qs = pl.BlockSpec((1, span, PAIR), lambda r, p: (r, 0, p))
    ks = pl.BlockSpec((1, keys, PAIR), lambda r, p: (r, 0, p))
    tq_s = pl.BlockSpec((span, PAIR), lambda r, p: (0, 0))
    tk_s = pl.BlockSpec((keys, PAIR), lambda r, p: (0, 0))
    kv_type = BF if whole else F32
    return pl.pallas_call(
        functools.partial(attend_back_kernel, tk, tq),
        grid=(rows, width // PAIR),
        in_specs=[
            qs, ks, ks, pl.BlockSpec((1, keys, PAIR), lambda r, p: (r, 0, 0)), qs, qs, qs,
            tq_s, tq_s, tk_s, tk_s,
        ],
        out_specs=[qs, ks, ks],
        out_shape=[
            jax.ShapeDtypeStruct(q.shape, BF),
            jax.ShapeDtypeStruct(k.shape, kv_type),
            jax.ShapeDtypeStruct(k.shape, kv_type),
        ],
        scratch_shapes=[
            pltpu.VMEM((span, 2 * PAIR), BF),
            pltpu.VMEM((2, keys, 2 * PAIR), BF),
            pltpu.VMEM((2, keys, 2 * PAIR), BF),
            pltpu.VMEM((span, 2 * PAIR), BF),
            pltpu.VMEM((2, span, PAIR), BF),
            pltpu.VMEM((2, span, PAIR), BF),
            pltpu.VMEM((PAIR, keys), BF),
            pltpu.VMEM((PAIR, span), F32),
            pltpu.VMEM((tk, PAIR), F32),
            pltpu.VMEM((tk, PAIR), F32),
        ],
        compiler_params=params(),
        name="attend_back",
    )(q, k, v, bias, o, do, aug, cq, sq, ck, sk)


def middle_kernel(
    chunk, x_ref, att_ref, cot_ref, wo_ref, wg_ref, wu_ref, wd_ref, g1_ref, g2_ref,
    out_ref, dfirst_ref, datt_ref, act_ref, dg_ref, du_ref, ht_ref, dft_ref, at_ref, gg1_ref, gg2_ref,
    ca, cb,
):
    @pl.when(pl.program_id(0) == 0)
    def _():
        gg1_ref[...] = jnp.zeros_like(gg1_ref)
        gg2_ref[...] = jnp.zeros_like(gg2_ref)

    gain1, gain2 = g1_ref[...], g2_ref[...]
    att = att_ref[...]
    at_ref[...] = att.T
    first = x_ref[...].astype(F32) + dot(att, wo_ref[...])
    centered = first - jnp.mean(first, axis=1, keepdims=True)
    s1 = lax.rsqrt(jnp.mean(centered * centered, axis=1, keepdims=True) + EPS)
    n1 = centered * s1
    hidden = n1 * gain1
    low = hidden.astype(BF)
    ht_ref[...] = low.T
    hidden_width = wg_ref.shape[1]
    second = hidden
    for c in range(hidden_width // chunk):
        at = slice(c * chunk, (c + 1) * chunk)
        g = dot(low, wg_ref[:, at])
        u = dot(low, wu_ref[:, at])
        sig = jax.nn.sigmoid(g)
        silu = g * sig
        act = (silu * u).astype(BF)
        act_ref[:, at] = act
        ca[:, at] = (u * (sig + silu * (1.0 - sig))).astype(ca.dtype)
        cb[:, at] = silu.astype(cb.dtype)
        second = second + dot(act, wd_ref[at, :])
    centered = second - jnp.mean(second, axis=1, keepdims=True)
    s2 = lax.rsqrt(jnp.mean(centered * centered, axis=1, keepdims=True) + EPS)
    n2 = centered * s2
    out_ref[...] = (n2 * gain2).astype(BF)
    dy = cot_ref[...].astype(F32)
    gg2_ref[...] += jnp.sum(dy * n2, axis=0, keepdims=True)
    inner = dy * gain2
    d_second = s2 * (
        inner - jnp.mean(inner, axis=1, keepdims=True) - n2 * jnp.mean(inner * n2, axis=1, keepdims=True)
    )
    d_ffn = d_second.astype(BF)
    dft_ref[...] = d_ffn.T
    d_hidden = d_second
    for c in range(hidden_width // chunk):
        at = slice(c * chunk, (c + 1) * chunk)
        d_act = dot_nt(d_ffn, wd_ref[at, :])
        dg = (d_act * ca[:, at]).astype(BF)
        du = (d_act * cb[:, at]).astype(BF)
        dg_ref[:, at] = dg
        du_ref[:, at] = du
        d_hidden = d_hidden + dot_nt(dg, wg_ref[:, at]) + dot_nt(du, wu_ref[:, at])
    gg1_ref[...] += jnp.sum(d_hidden * n1, axis=0, keepdims=True)
    inner = d_hidden * gain1
    d_first = s1 * (
        inner - jnp.mean(inner, axis=1, keepdims=True) - n1 * jnp.mean(inner * n1, axis=1, keepdims=True)
    )
    low = d_first.astype(BF)
    dfirst_ref[...] = low
    datt_ref[...] = dot_nt(low, wo_ref[...]).astype(BF)


def middle_call(x, att, cot, wo, wg, wu, wd, g1, g2, tile=256, chunk=768):
    tokens, width = x.shape
    hidden_width = wg.shape[1]
    tile = min(tile, tokens)
    row = pl.BlockSpec((tile, width), lambda i: (i, 0))
    wide = pl.BlockSpec((tile, hidden_width), lambda i: (i, 0))
    column = pl.BlockSpec((width, tile), lambda i: (0, i))

    def whole(a):
        return pl.BlockSpec(a.shape, lambda i: (0, 0), pipeline_mode=pl.Buffered(1))

    gain = pl.BlockSpec((1, width), lambda i: (0, 0))
    return pl.pallas_call(
        functools.partial(middle_kernel, chunk),
        grid=(tokens // tile,),
        in_specs=[row, row, row, whole(wo), whole(wg), whole(wu), whole(wd), gain, gain],
        out_specs=[row, row, row, wide, wide, wide, column, column, column, gain, gain],
        out_shape=[jax.ShapeDtypeStruct((tokens, width), BF)] * 3
        + [jax.ShapeDtypeStruct((tokens, hidden_width), BF)] * 3
        + [jax.ShapeDtypeStruct((width, tokens), BF)] * 3
        + [jax.ShapeDtypeStruct((1, width), F32)] * 2,
        scratch_shapes=[pltpu.VMEM((tile, hidden_width), F32)] * 2,
        compiler_params=params(),
        name="middle",
    )(x, att, cot, wo, wg, wu, wd, g1, g2)


def outer_kernel(a_ref, b_ref, o_ref):
    o_ref[...] = dot(a_ref[...], b_ref[...]).astype(o_ref.dtype)


def outer_call(a, b, out_type, tile=512):
    rows, tokens = a.shape
    columns = b.shape[1]
    tile = tile if columns % tile == 0 else 256
    return pl.pallas_call(
        outer_kernel,
        grid=(columns // tile,),
        in_specs=[
            pl.BlockSpec((rows, tokens), lambda i: (0, 0), pipeline_mode=pl.Buffered(1)),
            pl.BlockSpec((tokens, tile), lambda i: (0, i)),
        ],
        out_specs=pl.BlockSpec((rows, tile), lambda i: (0, i)),
        out_shape=jax.ShapeDtypeStruct((rows, columns), out_type),
        compiler_params=params(),
        name="outer",
    )(a, b)


def tokens_kernel(dq_ref, dk_ref, dv_ref, dfirst_ref, w_ref, o_ref):
    width = dq_ref.shape[1]
    total = dfirst_ref[...].astype(F32)
    total += dot_nt(dq_ref[...], w_ref[:, :width])
    total += dot_nt(dk_ref[...], w_ref[:, width : 2 * width])
    total += dot_nt(dv_ref[...], w_ref[:, 2 * width :])
    o_ref[...] = total.astype(BF)


def tokens_call(dq, dk, dv, dfirst, w, tile=512):
    tokens, width = dq.shape
    tile = min(tile, tokens)
    row = pl.BlockSpec((tile, width), lambda i: (i, 0))
    return pl.pallas_call(
        tokens_kernel,
        grid=(tokens // tile,),
        in_specs=[row] * 4 + [pl.BlockSpec(w.shape, lambda i: (0, 0), pipeline_mode=pl.Buffered(1))],
        out_specs=row,
        out_shape=jax.ShapeDtypeStruct((tokens, width), BF),
        compiler_params=params(),
        name="grad_tokens",
    )(dq, dk, dv, dfirst, w)


def angle_tables(span):
    index = np.arange(HEAD // 2, dtype=np.float64)
    inverse = np.power(1000.0, -2.0 * index / HEAD)
    angles = np.arange(span, dtype=np.float64)[:, None] * inverse[None, :]
    repeat = (1, PAIR // (HEAD // 2))
    return (
        np.tile(np.cos(angles), repeat).astype(np.float32),
        np.tile(np.sin(angles), repeat).astype(np.float32),
    )


def swap(a, mine):
    keep = lax.dynamic_index_in_dim(a, mine, 0, keepdims=False)
    give = lax.dynamic_index_in_dim(a, 1 - mine, 0, keepdims=False)
    got = lax.ppermute(give, "blk", [(0, 1), (1, 0)])
    low = jnp.where(mine == 0, keep, got)
    high = jnp.where(mine == 0, got, keep)
    return jnp.stack([low, high])


def body(tokens, lengths, w_qkv, w_out, w_gate, w_up, w_down, gain_one, gain_two, cotangent):
    axes = ("dp", "blk")
    blk = lax.axis_size("blk")
    mine = lax.axis_index("blk")
    rows, span, width = tokens.shape
    seq = span * blk
    own = blk == 2 and rows == 2

    def gather(a):
        return lax.all_gather(a, axes, axis=0, tiled=True)

    f_qkv, f_out, f_gate, f_up, f_down = map(gather, (w_qkv, w_out, w_gate, w_up, w_down))
    gains = jnp.stack([gain_one, gain_two], 1)
    f_gains = gather(gains).astype(F32)
    g1, g2 = f_gains[:, 0][None], f_gains[:, 1][None]
    cosine, sine = map(jnp.asarray, angle_tables(seq))
    if own:
        x = swap(tokens, mine).reshape(1, seq, width)
        cot = swap(cotangent, mine).reshape(1, seq, width)
        length = lax.dynamic_slice_in_dim(lengths, mine, 1, 0)
        cq, sq = cosine, sine
    else:
        x, cot, length = tokens, cotangent, lengths
        cq = lax.dynamic_slice_in_dim(cosine, mine * span, span, 0)
        sq = lax.dynamic_slice_in_dim(sine, mine * span, span, 0)
    n, t = x.shape[:2]
    flat = x.reshape(n * t, width)
    q, k, v, xt = qkv_call(flat, f_qkv, cq, sq)
    q, k, v = (a.reshape(n, t, width) for a in (q, k, v))
    if not own:
        k = lax.all_gather(k, "blk", axis=1, tiled=True)
        v = lax.all_gather(v, "blk", axis=1, tiled=True)
    position = jnp.arange(seq, dtype=jnp.int32)[None, :, None]
    lane = jnp.arange(PAIR, dtype=jnp.int32)[None, None, :]
    bias = jnp.where((lane == 3) & (position >= length[:, None, None]), NEG, 0.0).astype(BF)
    att, aug = attend_call(q, k, v, bias)
    out, d_first, d_att, act, d_gate, d_up, h_t, df_t, att_t, gg1, gg2 = middle_call(
        flat, att.reshape(n * t, width), cot.reshape(n * t, width), f_out, f_gate, f_up, f_down, g1, g2
    )
    gw_gate = outer_call(h_t, d_gate, BF)
    gw_up = outer_call(h_t, d_up, BF)
    gw_down_t = outer_call(df_t, act, BF)
    gw_out = outer_call(att_t, d_first, BF)

    def scatter_wide(g):
        g = lax.psum_scatter(g, "blk", scatter_dimension=1, tiled=True)
        return lax.psum_scatter(g, "dp", scatter_dimension=0, tiled=True).astype(F32)

    s_gate, s_up, s_down_t = map(scatter_wide, (gw_gate, gw_up, gw_down_t))
    s_down = s_down_t.T
    dq, dk, dv = attend_back_call(
        q, k, v, bias, att, d_att.reshape(n, t, width), aug, cq, sq, cosine, sine, own
    )
    if not own:
        dk = lax.psum_scatter(dk, "blk", scatter_dimension=1, tiled=True)
        dv = lax.psum_scatter(dv, "blk", scatter_dimension=1, tiled=True)
        heads = (dk * jnp.tile(sq, (1, width // PAIR))).reshape(n, t, HEADS, HEAD)
        half = jnp.concatenate([heads[..., HEAD // 2 :], -heads[..., : HEAD // 2]], -1)
        dk = dk * jnp.tile(cq, (1, width // PAIR)) + half.reshape(n, t, width)
        dk, dv = dk.astype(BF), dv.astype(BF)
    dq, dk, dv = (a.reshape(n * t, width) for a in (dq, dk, dv))
    gw_qkv = jnp.concatenate([outer_call(xt, a, BF, 256) for a in (dq, dk, dv)], 1)
    g_tokens = tokens_call(dq, dk, dv, d_first, f_qkv)
    s_qkv = lax.psum_scatter(gw_qkv, axes, scatter_dimension=0, tiled=True).astype(F32)
    s_out = lax.psum_scatter(gw_out, axes, scatter_dimension=0, tiled=True).astype(F32)
    gg = jnp.concatenate([gg1, gg2]).T
    s_gg = lax.psum_scatter(gg, axes, scatter_dimension=0, tiled=True)
    if own:
        out = swap(out.reshape(2, span, width), mine)
        g_tokens = swap(g_tokens.reshape(2, span, width), mine)
    else:
        out = out.reshape(tokens.shape)
        g_tokens = g_tokens.reshape(tokens.shape)
    return (out, g_tokens, s_qkv, s_out, s_gate, s_up, s_down, s_gg[:, 0], s_gg[:, 1])


def solution(mesh):
    both = ("dp", "blk")
    return jax.shard_map(
        body,
        mesh=mesh,
        in_specs=(
            P("dp", "blk", None),
            P("dp"),
            P(both, None),
            P(both, None),
            P(both, None),
            P(both, None),
            P(both, None),
            P(both),
            P(both),
            P("dp", "blk", None),
        ),
        out_specs=(
            P("dp", "blk", None),
            P("dp", "blk", None),
            P(both, None),
            P(both, None),
            P("dp", "blk"),
            P("dp", "blk"),
            P("blk", "dp"),
            P(both),
            P(both),
        ),
        check_vma=False,
    )
```

time: 2500 us -> 1040 us (0.42)
  waiting for transfers between devices: 1040 us -> 260 us
  matrix products: 726 us -> 0 us
  Pallas kernels: 0 us -> 484 us
  local copies, waits for them, and re-layouts: 426 us -> 13.8 us
  blocking collectives: 79.1 us -> 236 us
  other arithmetic: 178 us -> 27 us
  starting transfers between devices: 34.2 us -> 5.51 us
    dot_general x27 -> x0, matrix products: 726 us -> none  [the longest x2 116 us: block_grads(): jnp.einsum('rqhd,rkhd->rhqk', grad_attended, value_piece, preferred_eleme...]
    pallas_call x0 -> x12, Pallas kernels: none -> 484 us  [the longest x1 165 us: attend_back_call(): pl.pallas_call(functools.partial(attend_back_kernel, tk, tq), grid=(rows,...]
    ppermute x8 -> x4, waiting for transfers between devices: 390 us -> 0.01 us  [swap(): got = lax.ppermute(give, 'blk', [(0, 1), (1, 0)])]
    all_gather x9 -> x5, waiting for transfers between devices: 305 us -> 24.1 us  [gather(): return lax.all_gather(a, axes, axis=0, tiled=True)]
    all_to_all x3 -> x0, waiting for transfers between devices: 247 us -> none  [the longest x1 137 us: body(): lax.all_to_all(active.reshape(batch_rows, group_tokens // batch_rows, uni...]
    all_to_all x6 -> x0, local copies, waits for them, and re-layouts: 236 us -> none  [the longest x2 78.6 us: body(): lax.all_to_all(grad_gate.reshape(batch_rows, group_tokens // batch_rows,...]
    reduce_scatter x4 -> x8, waiting for transfers between devices: 0.03 us -> 231 us  [the longest x3 193 us: scatter_wide(): lax.psum_scatter(g, 'dp', scatter_dimension=0, tiled=True).astype(F32)]
    all_gather x0 -> x1, blocking collectives: none -> 135 us  [gather(): return lax.all_gather(a, axes, axis=0, tiled=True)]
  transfers between devices with their start and end apart: 25 -> 17, of which waited for: 17 -> 5; matrix products, arithmetic and copies ran while one was open for 48% -> 4% of each run, Pallas kernels for 0% -> 36%
where the time goes in v1:
time: 1040 us
  Pallas kernels  484 us (47%)
  waiting for transfers between devices  260 us (25%)
  blocking collectives  236 us (23%)
  other arithmetic  27 us (3%)
  between operations  14.1 us (1%)
  local copies, waits for them, and re-layouts  13.8 us (1%)
    reduce_scatter x3, waiting for transfers between devices, scatter_wide(): lax.psum_scatter(g, 'dp', scatter_dimension=0, tiled=True).astype(F32)  193 us
    pallas_call x1, Pallas kernels, attend_back_call(): pl.pallas_call(functools.partial(attend_back_kernel, tk, tq), grid=(rows,...  165 us
    all_gather x1, blocking collectives, gather(): return lax.all_gather(a, axes, axis=0, tiled=True)  135 us
    pallas_call x1, Pallas kernels, attend_call(): pl.pallas_call(attend_kernel, grid=(rows, width // PAIR, span // tile), i...  129 us
    unnamed x1, blocking collectives  102 us
    pallas_call x1, Pallas kernels, middle_call(): pl.pallas_call(functools.partial(middle_kernel, chunk), grid=(tokens // t...  93.3 us
    pallas_call x7, Pallas kernels, outer_call(): pl.pallas_call(outer_kernel, grid=(columns // tile,), in_specs=[pl.BlockS...  69.9 us
    reduce_scatter x1, waiting for transfers between devices, body(): lax.psum_scatter(gw_qkv, axes, scatter_dimension=0, tiled=True).astype(F32)  37.7 us
  transfers between devices with their start and end apart: 17, of which 5 were waited for; matrix products, arithmetic and copies ran while one was open for 4% of the time, Pallas kernels for 36%

profile of v1, /device:TPU:0, one launch (start us, length us, event | category | flops | bytes accessed | tf_op | source)
XLA Modules:
  0.0 1040.6 jit_solution(9756049344040983261)
XLA Ops:
  10.7 2.8 dynamic-slice_bitcast_fusion.3
  13.5 3.0 collective-permute-start
  16.4 2.7 dynamic-slice_bitcast_fusion.2
  19.1 134.6 %all-gather = bf16[32,24,2]{1,2,0:T(2,128)(2,1)S(1)} all-gather(bf16[1,24,2]{1,2,0:T(2,128)(2,1)S(1)} %maximum_bitcast_fusion.1), channel_id=1, replica_groups=mesh['dp'=16,'blk'=2] {'dp','blk'}, dimensions={0}, use_global_device_ids=true | all-gather | bytes 3168 | tf_op jit(solution)/shard_map/all_gather | solution.py:434
  158.7 1.9 pad_maximum_fusion.1
  163.3 1.9 pad_maximum_fusion.2
  165.3 13.3 %qkv.1 = (bf16[2048,768]{1,0:T(8,128)(2,1)}, bf16[2048,768]{1,0:T(8,128)(2,1)}, bf16[2048,768]{1,0:T(8,128)(2,1)}, bf16[768,2048]{1,0:T(8,128)(2,1)}) custom-call(bf16[2048,768]{1,0:T(8,128)(2,1)} %bitcast.85, bf16[768,2304]{1,0:T(8,128)(2,1)} %all-gather.7.cloned.1.call-done.w_ref, f32[2048,128]{1,0:T(8,128)} %constant.39.clone.cos_ref.cq_ref.ck_ref, ...), custom_call_target="tpu_custom_call" | custom-call | tf_op jit(solution)/shard_map/qkv/pallas_call | solution.py:69
  178.5 129.4 %attend.1 = (bf16[1,2048,768]{2,1,0:T(8,128)(2,1)}, bf16[1,2048,768]{2,1,0:T(8,128)(2,1)}) custom-call(bf16[1,2048,768]{2,1,0:T(8,128)(2,1)} %bitcast.95, bf16[1,2048,768]{2,1,0:T(8,128)(2,1)} %bitcast.97, bf16[1,2048,768]{2,1,0:T(8,128)(2,1)} %bitcast.99, bf16[1,2048,128]{2,1,0:T(8,128)(2,1)} %select_convert_fusion.bias_ref), custom_call_target="tpu_custom_call" | custom-call | tf_op jit(solution)/shard_map/attend/pallas_call | solution.py:136
  308.0 24.1 %all-gather.15.cloned.1.call-done.wd_ref = bf16[3072,768]{1,0:T(8,128)(2,1)} async-done(((bf16[96,768]{1,0:T(8,128)(2,1)}), bf16[3072,768]{1,0:T(8,128)(2,1)}) %all-gather.15.cloned.1.call-update) | async-done | bytes 4718608 | tf_op jit(solution)/shard_map/all_gather | solution.py:434
  332.1 93.3 %middle.1 = (bf16[2048,768]{1,0:T(8,128)(2,1)}, bf16[2048,768]{1,0:T(8,128)(2,1)}, bf16[2048,768]{1,0:T(8,128)(2,1)}, bf16[2048,3072]{1,0:T(8,128)(2,1)}, bf16[2...) custom-call(bf16[2048,768]{1,0:T(8,128)(2,1)} %bitcast.86, ...), custom_call_target="tpu_custom_call" | custom-call | tf_op jit(solution)/shard_map/middle/pallas_call | solution.py:344
  425.4 14.5 %outer.12 = bf16[768,3072]{1,0:T(8,128)(2,1)} custom-call(bf16[768,2048]{1,0:T(8,128)(2,1)} %get-tuple-element.42.a_ref, bf16[2048,3072]{1,0:T(8,128)(2,1)} %get-tuple-element.44.b_ref), custom_call_target="tpu_custom_call" | custom-call | tf_op jit(solution)/shard_map/outer/pallas_call | solution.py:367
  440.0 14.7 %outer.13 = bf16[768,3072]{1,0:T(8,128)(2,1)} custom-call(bf16[768,2048]{1,0:T(8,128)(2,1)} %get-tuple-element.45.a_ref, bf16[2048,3072]{1,0:T(8,128)(2,1)} %get-tuple-element.46.b_ref), custom_call_target="tpu_custom_call" | custom-call | tf_op jit(solution)/shard_map/outer/pallas_call | solution.py:367
  454.8 14.6 %outer.11 = bf16[768,3072]{1,0:T(8,128)(2,1)} custom-call(bf16[768,2048]{1,0:T(8,128)(2,1)} %get-tuple-element.42.a_ref, bf16[2048,3072]{1,0:T(8,128)(2,1)} %get-tuple-element.43.b_ref), custom_call_target="tpu_custom_call" | custom-call | tf_op jit(solution)/shard_map/outer/pallas_call | solution.py:367
  469.4 6.7 outer.10
  476.2 164.8 %attend_back.1 = (bf16[1,2048,768]{2,1,0:T(8,128)(2,1)}, bf16[1,2048,768]{2,1,0:T(8,128)(2,1)}, bf16[1,2048,768]{2,1,0:T(8,128)(2,1)}) custom-call(bf16[1,2048,768]{2,1,0:T(8,128)(2,1)} %bitcast.96, bf16[1,2048,768]{2,1,0:T(8,128)(2,1)} %bitcast.98, bf16[1,2048,768]{2,1,0:T(8,128)(2,1)} %bitcast.100, bf16[1,2048,128]{2,1,0:T(8,128)(2,1)} %select_convert_fusion.bias_ref, ...), custom_call_target="tpu_custom_call" | custom-call | tf_op jit(solution)/shard_map/attend_back/pallas_call | solution.py:238
  641.1 6.4 outer.7
  647.5 6.4 outer.8
  653.9 6.5 outer.9
  660.4 3.0 pad_maximum_fusion
  665.5 12.9 %grad_tokens.1 = bf16[2048,768]{1,0:T(8,128)(2,1)} custom-call(bf16[2048,768]{1,0:T(8,128)(2,1)} %bitcast.88, bf16[2048,768]{1,0:T(8,128)(2,1)} %bitcast.90, bf16[2048,768]{1,0:T(8,128)(2,1)} %bitcast.92, bf16[2048,768]{1,0:T(8,128)(2,1)} %get-tuple-element.39.dfirst_ref.b_ref, bf16[768,2304]{1,0:T(8,128)(2,1)} %all-gather.7.cloned.1.call-done.w_ref), custom_call_target="tpu_custom_call" | custom-call | tf_op jit(solution)/shard_map/grad_tokens/pallas_call | solution.py:394
  678.5 2.8 dynamic-slice_bitcast_fusion
  681.3 1.7 collective-permute-start.3
  684.5 101.7 %all-reduce = f32[768,2]{0,1:T(2,128)S(1)} all-reduce(f32[768,2]{0,1:T(2,128)S(1)} %maximum_bitcast_fusion), channel_id=10, replica_groups=mesh['dp'=16,'blk'=2] {'dp','blk'}, use_global_device_ids=true, to_apply=%region_8.9.clone | all-reduce | flops 1536 | bytes 12288
  789.9 1.9 pad_maximum_fusion.4
  794.6 1.9 pad_maximum_fusion.3
  796.6 37.7 %reduce-scatter.10.cloned.1.call-done = bf16[24,2304]{1,0:T(8,128)(2,1)} async-done(((bf16[768,2304]{1,0:T(8,128)(2,1)}), bf16[24,2304]{1,0:T(8,128)(2,1)}) %reduce-scatter.10.cloned.1.call-update) | async-done | bytes 110608 | tf_op jit(solution)/shard_map/reduce_scatter | solution.py:488
  835.9 64.6 %reduce-scatter.20.cloned.1.call-done = bf16[48,1536]{1,0:T(8,128)(2,1)} async-done(((bf16[768,1536]{1,0:T(8,128)(2,1)}), bf16[48,1536]{1,0:T(8,128)(2,1)}) %reduce-scatter.20.cloned.1.call-update) | async-done | bytes 147472 | tf_op jit(solution)/shard_map/reduce_scatter | solution.py:471
  900.5 1.6 convert_element_type.24
  902.1 64.0 %reduce-scatter.24.cloned.1.call-done = bf16[48,1536]{1,0:T(8,128)(2,1)} async-done(((bf16[768,1536]{1,0:T(8,128)(2,1)}), bf16[48,1536]{1,0:T(8,128)(2,1)}) %reduce-scatter.24.cloned.1.call-update) | async-done | bytes 147472 | tf_op jit(solution)/shard_map/reduce_scatter | solution.py:471
  966.1 1.6 convert_bitcast_fusion
  967.8 64.6 %reduce-scatter.16.cloned.1.call-done = bf16[48,1536]{1,0:T(8,128)(2,1)} async-done(((bf16[768,1536]{1,0:T(8,128)(2,1)}), bf16[48,1536]{1,0:T(8,128)(2,1)}) %reduce-scatter.16.cloned.1.call-update) | async-done | bytes 147472 | tf_op jit(solution)/shard_map/reduce_scatter | solution.py:471
  1032.4 1.6 convert_element_type.23
  (83 shorter events, 22.8 us)
Async XLA Ops:
  7.2 158.1 %all-gather.7.cloned.1.call-start = ((), (), s32[]{:S(2)}) async-start(), calls=%async_computation.8 | async-start | bytes 3649536 | tf_op jit(solution)/shard_map/all_gather | solution.py:434
  7.9 300.1 %all-gather.9.cloned.1.call-start = ((), (), s32[]{:S(2)}) async-start(), calls=%async_computation.9 | async-start | bytes 1216512 | tf_op jit(solution)/shard_map/all_gather | solution.py:434
  8.7 299.3 %all-gather.11.cloned.1.call-start = ((), (), s32[]{:S(2)}) async-start(), calls=%async_computation.10 | async-start | bytes 4866048 | tf_op jit(solution)/shard_map/all_gather | solution.py:434
  9.4 298.6 %all-gather.13.cloned.1.call-start = ((), (), s32[]{:S(2)}) async-start(), calls=%async_computation.11 | async-start | bytes 4866048 | tf_op jit(solution)/shard_map/all_gather | solution.py:434
  10.0 322.1 %all-gather.15.cloned.1.call-start = ((), (), s32[]{:S(2)}) async-start(), calls=%async_computation.12 | async-start | bytes 4866048 | tf_op jit(solution)/shard_map/all_gather | solution.py:434
  10.6 652.9 %reduce-scatter.18.cloned.1.call-start = ((), (), s32[]{:S(2)}) async-start(), calls=%async_computation.17 | async-start | bytes 7077888 | tf_op jit(solution)/shard_map/reduce_scatter | solution.py:470
  10.6 8.5 copy-start.9
  10.6 8.5 copy-start.10
  10.6 143.4 %copy-start.11 = (s32[2]{0:T(128)S(1)}, s32[2]{0:T(128)}, u32[]{:S(2)}) copy-start(s32[2]{0:T(128)} %param.13) | copy-start | bytes 28
  10.6 146.4 %copy-start.3 = (bf16[2,1024,768]{2,1,0:T(8,128)(2,1)S(1)}, bf16[2,1024,768]{2,1,0:T(8,128)(2,1)}, u32[]{:S(2)}) copy-start(bf16[2,1024,768]{2,1,0:T(8,128)(2,1)} %param.12) | copy-start | bytes 9437188
  13.5 143.6 %collective-permute-start = (bf16[1024,768]{1,0:T(8,128)(2,1)}, bf16[1024,768]{1,0:T(8,128)(2,1)}, u32[]{:S(2)}, u32[]{:S(2)}) collective-permute-start(bf16[1024,768]{1,0:T(8,128)(2,1)} %dynamic-slice_bitcast_fusion.3), channel_id=1, source_target_pairs={{0,1},{1,0},{2,3},{3,2},{4,5},{5,4},{6,7},{7,6},{8,9},{9,8},{10,11... | collective-permute-start | bytes 4718600 | tf_op jit(solution)/shard_map/ppermute | solution.py:419
  19.1 141.5 %collective-permute-start.1 = (bf16[1024,768]{1,0:T(8,128)(2,1)}, bf16[1024,768]{1,0:T(8,128)(2,1)}, u32[]{:S(2)}, u32[]{:S(2)}) collective-permute-start(bf16[1024,768]{1,0:T(8,128)(2,1)} %dynamic-slice_bitcast_fusion.2), channel_id=1, source_target_pairs={{0,1},{1,0},{2,3},{3,2},{4,5},{5,4},{6,7},{7,6},{8,9},{9,8},{10,11... | collective-permute-start | bytes 4718600 | tf_op jit(solution)/shard_map/ppermute | solution.py:419
  158.7 3.0 copy-start.4
  439.9 224.3 %reduce-scatter.22.cloned.1.call-start = ((), (), s32[]{:S(2)}) async-start(), calls=%async_computation.19 | async-start | bytes 7077888 | tf_op jit(solution)/shard_map/reduce_scatter | solution.py:470
  454.7 210.1 %reduce-scatter.14.cloned.1.call-start = ((), (), s32[]{:S(2)}) async-start(), calls=%async_computation.15 | async-start | bytes 7077888 | tf_op jit(solution)/shard_map/reduce_scatter | solution.py:470
  469.4 317.5 %reduce-scatter.12.cloned.1.call-start = ((), (), s32[]{:S(2)}) async-start(), calls=%async_computation.14 | async-start | bytes 1216512 | tf_op jit(solution)/shard_map/reduce_scatter | solution.py:489
  476.2 358.1 %reduce-scatter.10.cloned.1.call-start = ((), (), s32[]{:S(2)}) async-start(), calls=%async_computation.13 | async-start | bytes 3649536 | tf_op jit(solution)/shard_map/reduce_scatter | solution.py:488
  653.9 6.5 copy-start.1
  653.9 6.5 copy-start.2
  663.4 237.1 %reduce-scatter.20.cloned.1.call-start = ((), (), s32[]{:S(2)}) async-start(), calls=%async_computation.18 | async-start | bytes 2506752 | tf_op jit(solution)/shard_map/reduce_scatter | solution.py:471
  664.1 302.0 %reduce-scatter.24.cloned.1.call-start = ((), (), s32[]{:S(2)}) async-start(), calls=%async_computation.20 | async-start | bytes 2506752 | tf_op jit(solution)/shard_map/reduce_scatter | solution.py:471
  664.7 367.7 %reduce-scatter.16.cloned.1.call-start = ((), (), s32[]{:S(2)}) async-start(), calls=%async_computation.16 | async-start | bytes 2506752 | tf_op jit(solution)/shard_map/reduce_scatter | solution.py:471
  678.4 4.5 copy-start.5
  678.4 6.1 copy-start.7
  678.4 6.1 copy-start.8
  678.4 109.9 %copy-start = (bf16[2048,768]{1,0:T(8,128)(2,1)S(1)}, bf16[2048,768]{1,0:T(8,128)(2,1)}, u32[]{:S(2)}) copy-start(bf16[2048,768]{1,0:T(8,128)(2,1)} %grad_tokens.1) | copy-start | bytes 9437188
  681.3 107.0 %collective-permute-start.3 = (bf16[1024,768]{1,0:T(8,128)(2,1)}, bf16[1024,768]{1,0:T(8,128)(2,1)}, u32[]{:S(2)}, u32[]{:S(2)}) collective-permute-start(bf16[1024,768]{1,0:T(8,128)(2,1)} %dynamic-slice_bitcast_fusion), channel_id=1, source_target_pairs={{0,1},{1,0},{2,3},{3,2},{4,5},{5,4},{6,7},{7,6},{8,9},{9,8},{10,11... | collective-permute-start | bytes 4718600 | tf_op jit(solution)/shard_map/ppermute | solution.py:419
  684.2 107.7 %collective-permute-start.2 = (bf16[1024,768]{1,0:T(8,128)(2,1)}, bf16[1024,768]{1,0:T(8,128)(2,1)}, u32[]{:S(2)}, u32[]{:S(2)}) collective-permute-start(bf16[1024,768]{1,0:T(8,128)(2,1)} %dynamic-slice_bitcast_fusion.1), channel_id=1, source_target_pairs={{0,1},{1,0},{2,3},{3,2},{4,5},{5,4},{6,7},{7,6},{8,9},{9,8},{10,11... | collective-permute-start | bytes 4718600 | tf_op jit(solution)/shard_map/ppermute | solution.py:419
  789.9 3.1 copy-start.6
Sparse Core Ops, SparseCore 0:
  10.9 69.1 all-gather.6
  83.1 52.8 all-gather.8
  138.9 62.5 all-gather.10
  204.3 62.4 all-gather.12
  269.6 62.4 all-gather.14
  440.0 58.7 reduce-scatter.17
  501.2 59.9 reduce-scatter.21
  563.6 59.9 reduce-scatter.13
  629.5 96.2 reduce-scatter.11
  732.0 102.2 reduce-scatter.9
  838.5 61.9 reduce-scatter.19
  904.1 61.9 reduce-scatter.23
  970.3 61.9 reduce-scatter.15

commit v2 on v1

--- a/solution.py
+++ b/solution.py
@@ -40,6 +40,158 @@
 def turn(u):
     low_half = (lanes(u.shape) % HEAD) < HEAD // 2
     return jnp.where(low_half, -pltpu.roll(u, PAIR - HEAD // 2, 1), pltpu.roll(u, HEAD // 2, 1))
+
+
+MESH = pl.DeviceIdType.MESH
+AXES = "zxcy"
+SIZE = {"z": 4, "x": 2, "c": 2, "y": 2}
+
+
+def place():
+    dp, y = lax.axis_index("dp"), lax.axis_index("blk")
+    return {"z": dp // 4, "x": dp // 2 % 2, "c": dp % 2, "y": y}
+
+
+def moved(me, axis, by):
+    return {**me, axis: lax.rem(me[axis] + by, SIZE[axis])}
+
+
+def device(at):
+    return ((at["z"] * 2 + at["x"]) * 2 + at["c"], at["y"])
+
+
+def greet(me):
+    barrier = pltpu.get_barrier_semaphore()
+    peers = [moved(me, "y", 1), moved(me, "x", 1), moved(me, "c", 1)]
+    peers += [moved(me, "z", d) for d in range(1, 4)]
+    for peer in peers:
+        pl.semaphore_signal(barrier, inc=1, device_id=device(peer), device_id_type=MESH)
+    pl.semaphore_wait(barrier, len(peers))
+
+
+class Gather:
+    SEMS = 6
+
+    def __init__(self, me, shard, full, send, recv, local, base, order):
+        self.me, self.shard, self.full = me, shard, full
+        self.send, self.recv, self.local, self.base, self.order = send, recv, local, base, order
+
+    def view(self, at, got):
+        return self.full.at[tuple(slice(None) if a in got else at[a] for a in AXES)]
+
+    def copies(self, stage):
+        got = self.order[:stage]
+        axis = self.order[stage]
+        slot = self.base + sum(SIZE[a] - 1 for a in got)
+        out = []
+        for d in range(1, SIZE[axis]):
+            here = self.view(self.me, got)
+            out.append(
+                pltpu.make_async_remote_copy(
+                    src_ref=self.shard if stage == 0 else here,
+                    dst_ref=here,
+                    send_sem=self.send.at[slot + d - 1],
+                    recv_sem=self.recv.at[slot + d - 1],
+                    device_id=device(moved(self.me, axis, d)),
+                    device_id_type=MESH,
+                )
+            )
+        return out
+
+    def own(self):
+        return pltpu.make_async_copy(self.shard, self.view(self.me, ""), self.local)
+
+    def arrivals(self, stage):
+        got = self.order[:stage]
+        axis = self.order[stage]
+        slot = self.base + sum(SIZE[a] - 1 for a in got)
+        for d in range(1, SIZE[axis]):
+            there = self.view(moved(self.me, axis, SIZE[axis] - d), got)
+            pltpu.make_async_remote_copy(
+                src_ref=there,
+                dst_ref=there,
+                send_sem=self.send.at[slot + d - 1],
+                recv_sem=self.recv.at[slot + d - 1],
+                device_id=device(moved(self.me, axis, d)),
+                device_id_type=MESH,
+            ).wait_recv()
+
+    def start(self):
+        self.own().start()
+        for copy in self.copies(0):
+            copy.start()
+
+    def step(self, stage):
+        self.arrivals(stage - 1)
+        if stage == 1:
+            self.own().wait()
+        if stage < len(self.order):
+            for copy in self.copies(stage):
+                copy.start()
+
+    def finish(self):
+        for stage in range(len(self.order)):
+            for copy in self.copies(stage):
+                copy.wait_send()
+
+
+def swap_copies(me, source, target, send, recv, local, slot):
+    other = moved(me, "y", 1)
+    y = me["y"]
+    keep = pltpu.make_async_copy(source.at[y], target.at[y], local)
+    give = pltpu.make_async_remote_copy(
+        src_ref=source.at[1 - y],
+        dst_ref=target.at[y],
+        send_sem=send.at[slot],
+        recv_sem=recv.at[slot],
+        device_id=device(other),
+        device_id_type=MESH,
+    )
+    take = pltpu.make_async_remote_copy(
+        src_ref=target.at[1 - y],
+        dst_ref=target.at[1 - y],
+        send_sem=send.at[slot],
+        recv_sem=recv.at[slot],
+        device_id=device(other),
+        device_id_type=MESH,
+    )
+    return keep, give, take
+
+
+def opening_kernel(tok_ref, qkv_ref, x_ref, full_ref, send, recv, local):
+    me = place()
+    greet(me)
+    keep, give, take = swap_copies(me, tok_ref, x_ref, send, recv, local.at[0], 0)
+    gather = Gather(me, qkv_ref, full_ref, send, recv, local.at[1], 1, "yzxc")
+    gather.start()
+    give.start()
+    keep.start()
+    for stage in range(1, 5):
+        gather.step(stage)
+    gather.finish()
+    take.wait_recv()
+    give.wait_send()
+    keep.wait()
+
+
+def opening_call(tokens, w_qkv):
+    hbm = pl.BlockSpec(memory_space=pl.ANY)
+    return pl.pallas_call(
+        opening_kernel,
+        in_specs=[hbm, hbm],
+        out_specs=[hbm, hbm],
+        out_shape=[
+            jax.ShapeDtypeStruct(tokens.shape, BF),
+            jax.ShapeDtypeStruct((4, 2, 2, 2) + w_qkv.shape, BF),
+        ],
+        scratch_shapes=[
+            pltpu.SemaphoreType.DMA((1 + Gather.SEMS,)),
+            pltpu.SemaphoreType.DMA((1 + Gather.SEMS,)),
+            pltpu.SemaphoreType.DMA((2,)),
+        ],
+        compiler_params=pltpu.CompilerParams(collective_id=0, has_side_effects=True),
+        name="opening",
+    )(tokens, w_qkv)
 
 
 def qkv_kernel(x_ref, w_ref, cos_ref, sin_ref, q_ref, k_ref, v_ref, xt_ref):
@@ -83,37 +235,124 @@
     )(x, w, cosine, sine)
 
 
-def attend_kernel(q_ref, k_ref, v_ref, bias_ref, o_ref, aug_ref, ka, va):
-    keys = k_ref.shape[1]
-
-    @pl.when(pl.program_id(2) == 0)
-    def _():
-        lane = lanes((keys, PAIR))
-        k, v = k_ref[0], v_ref[0]
-        zero = jnp.zeros_like(k)
-        for h in range(2):
-            mine = (lane // HEAD) == h
-            ka[h, :, :PAIR] = jnp.where(mine, k, zero)
-            ka[h, :, PAIR:] = bias_ref[0]
-            va[h, :, :PAIR] = jnp.where(mine, v, zero)
-            va[h, :, PAIR:] = mine.astype(F32).astype(BF)
-
-    q = q_ref[0]
-    lane = lanes(q.shape)
-    qa = jnp.concatenate([q, (lane == 3).astype(F32).astype(BF)], axis=1)
-    acc = None
-    tops = []
+def attend_kernel(tile, chunk, moves, q_ref, k_ref, v_ref, bias_ref, *rest):
+    inputs, rest = rest[: moves], rest[moves:]
+    o_ref, aug_ref, rest = rest[0], rest[1], rest[2:]
+    outputs, rest = rest[: moves], rest[moves:]
+    ka, va, s_scr, m_scr = rest[:4]
+    keys, span = k_ref.shape[1], q_ref.shape[1]
+    tiles = span // tile
+    events = {}
+    if moves:
+        events = attend_events(inputs, outputs, tiles * pl.num_programs(1), *rest[4:])
+    lane = lanes((keys, PAIR))
+    k, v = k_ref[0], v_ref[0]
+    zero = jnp.zeros_like(k)
     for h in range(2):
-        s = dot_nt(qa, ka[h])
-        top = jnp.max(s, axis=1, keepdims=True)
-        p = jnp.exp2(s - top).astype(BF)
-        part = dot(p, va[h])
-        acc = part if acc is None else acc + part
-        tops.append(top)
-    total = acc[:, PAIR:]
-    o_ref[0] = (acc[:, :PAIR] / total).astype(BF)
-    lse = jnp.where(lane < HEAD, tops[0], tops[1]) + jnp.log2(total)
-    aug_ref[0] = spread(lse, jnp.where(lane == 3, 1.0, 0.0))
+        mine = (lane // HEAD) == h
+        ka[h, :, :PAIR] = jnp.where(mine, k, zero)
+        ka[h, :, PAIR:] = bias_ref[0]
+        va[h, :, :PAIR] = jnp.where(mine, v, zero)
+        va[h, :, PAIR:] = mine.astype(F32).astype(BF)
+    lane = lanes((tile, PAIR))
+    ones = (lane == 3).astype(F32).astype(BF)
+    chunks = keys // chunk
+
+    def score(i, h, c, top):
+        at = pl.ds(pl.multiple_of(i * tile, tile), tile)
+        qa = jnp.concatenate([q_ref[0, at, :], ones], axis=1)
+        s = dot_nt(qa, ka[h, c * chunk : (c + 1) * chunk, :])
+        s_scr[h, :, c * chunk : (c + 1) * chunk] = s
+        for b in range(chunk // PAIR):
+            part = s[:, b * PAIR : (b + 1) * PAIR]
+            top = part if top is None else jnp.maximum(top, part)
+        return top
+
+    def close(h, top):
+        m_scr[h] = jnp.broadcast_to(jnp.max(top, axis=1, keepdims=True), (tile, PAIR))
+
+    def unit(h, later, other):
+        m = m_scr[h]
+        wide = jnp.concatenate([m] * (chunk // PAIR), axis=1)
+        acc, top = None, None
+        for c in range(chunks):
+            top = score(later, other, c, top)
+            p = jnp.exp2(s_scr[h, :, c * chunk : (c + 1) * chunk] - wide).astype(BF)
+            part = dot(p, va[h, c * chunk : (c + 1) * chunk, :])
+            acc = part if acc is None else acc + part
+        return acc, top, m
+
+    top = None
+    for c in range(chunks):
+        top = score(0, 0, c, top)
+    close(0, top)
+
+    def step(i, _):
+        now = pl.program_id(1) * tiles + i
+        for at_step, act in events.items():
+            pl.when(now == at_step)(act)
+        acc0, top, m0 = unit(0, i, 1)
+        close(1, top)
+        acc1, top, m1 = unit(1, jnp.minimum(i + 1, tiles - 1), 0)
+        close(0, top)
+        acc = acc0 + acc1
+        total = acc[:, PAIR:]
+        at = pl.ds(pl.multiple_of(i * tile, tile), tile)
+        o_ref[0, at, :] = (acc[:, :PAIR] / total).astype(BF)
+        lse = jnp.where(lane < HEAD, m0, m1) + jnp.log2(total)
+        aug_ref[0, at, :] = spread(lse, jnp.where(lane == 3, 1.0, 0.0))
+        return 0
+
+    lax.fori_loop(0, tiles, step, 0)
+    if moves:
+        pl.when(pl.program_id(1) == pl.num_programs(1) - 1)(events.last)
+
+
+class Events(dict):
+    last = None
+
+
+def attend_events(inputs, outputs, steps, send, recv, local):
+    me = place()
+    cot_in, shards = inputs[0], inputs[1:]
+    cot_out, fulls = outputs[0], outputs[1:]
+    keep, give, take = swap_copies(me, cot_in, cot_out, send, recv, local.at[0], 0)
+    orders = ["zxyc", "zxyc", "zyxc", "yzxc"]
+    gathers = [
+        Gather(me, shard, full, send, recv, local.at[1 + i], 1 + i * Gather.SEMS, orders[i])
+        for i, (shard, full) in enumerate(zip(shards, fulls))
+    ]
+
+    def begin():
+        greet(me)
+        for g in gathers:
+            g.start()
+        give.start()
+        keep.start()
+
+    def stage(g, n):
+        return lambda: g.step(n)
+
+    def last():
+        for n, g in pending:
+            g.step(n)
+        for g in gathers:
+            g.finish()
+        take.wait_recv()
+        give.wait_send()
+        keep.wait()
+
+    events = Events()
+    events[0] = begin
+    todo = [(n, g) for n in (1, 2, 3, 4) for g in gathers]
+    times = [4, 6, 9, 5, 6, 9, 12, 11, 12, 16, 19, 20]
+    for at, (n, g) in zip(times, todo):
+        old = events.get(at)
+        new = stage(g, n)
+        events[at] = new if old is None else (lambda old=old, new=new: (old(), new(), None)[2])
+    pending = todo[len(times) :]
+    events.last = last
+    return events
 
 
 def spread(value, other):
@@ -127,25 +366,36 @@
     ).astype(BF)
 
 
-def attend_call(q, k, v, bias, tile=256):
+def attend_call(q, k, v, bias, moving=(), tile=512, chunk=512):
     rows, span, width = q.shape
     keys = k.shape[1]
     tile = min(tile, span)
-    qs = pl.BlockSpec((1, tile, PAIR), lambda r, p, i: (r, i, p))
-    ks = pl.BlockSpec((1, keys, PAIR), lambda r, p, i: (r, 0, p))
+    moves = len(moving)
+    qs = pl.BlockSpec((1, span, PAIR), lambda r, p: (r, 0, p))
+    ks = pl.BlockSpec((1, keys, PAIR), lambda r, p: (r, 0, p))
+    hbm = pl.BlockSpec(memory_space=pl.ANY)
+    moved_shapes = [jax.ShapeDtypeStruct(a.shape, a.dtype) for a in moving[:1]] + [
+        jax.ShapeDtypeStruct((4, 2, 2, 2) + a.shape, a.dtype) for a in moving[1:]
+    ]
+    sems = 1 + Gather.SEMS * max(moves - 1, 0)
+    extra = [pltpu.SemaphoreType.DMA((sems,))] * 2 + [pltpu.SemaphoreType.DMA((moves,))]
+    more = dict(collective_id=1, has_side_effects=True) if moves else {}
     return pl.pallas_call(
-        attend_kernel,
-        grid=(rows, width // PAIR, span // tile),
-        in_specs=[qs, ks, ks, pl.BlockSpec((1, keys, PAIR), lambda r, p, i: (r, 0, 0))],
-        out_specs=[qs, qs],
-        out_shape=[jax.ShapeDtypeStruct(q.shape, BF)] * 2,
+        functools.partial(attend_kernel, tile, chunk, moves),
+        grid=(rows, width // PAIR),
+        in_specs=[qs, ks, ks, pl.BlockSpec((1, keys, PAIR), lambda r, p: (r, 0, 0))] + [hbm] * moves,
+        out_specs=[qs, qs] + [hbm] * moves,
+        out_shape=[jax.ShapeDtypeStruct(q.shape, BF)] * 2 + moved_shapes,
         scratch_shapes=[
             pltpu.VMEM((2, keys, 2 * PAIR), BF),
             pltpu.VMEM((2, keys, 2 * PAIR), BF),
-        ],
-        compiler_params=params(),
+            pltpu.VMEM((2, tile, keys), F32),
+            pltpu.VMEM((2, tile, PAIR), F32),
+        ]
+        + (extra if moves else []),
+        compiler_params=pltpu.CompilerParams(vmem_limit_bytes=VMEM_LIMIT, **more),
         name="attend",
-    )(q, k, v, bias)
+    )(q, k, v, bias, *moving)
 
 
 def attend_back_kernel(
@@ -225,7 +475,7 @@
     return g * cosine - turn(g * sine)
 
 
-def attend_back_call(q, k, v, bias, o, do, aug, cq, sq, ck, sk, whole, tk=512, tq=512):
+def attend_back_call(q, k, v, bias, o, do, aug, cq, sq, ck, sk, whole, tk=1024, tq=512):
     rows, span, width = q.shape
     keys = k.shape[1]
     tq = min(tq, span)
@@ -428,22 +678,22 @@
     mine = lax.axis_index("blk")
     rows, span, width = tokens.shape
     seq = span * blk
-    own = blk == 2 and rows == 2
+    own = blk == 2 and rows == 2 and lax.axis_size("dp") == 16
 
     def gather(a):
         return lax.all_gather(a, axes, axis=0, tiled=True)
 
-    f_qkv, f_out, f_gate, f_up, f_down = map(gather, (w_qkv, w_out, w_gate, w_up, w_down))
+    cosine, sine = map(jnp.asarray, angle_tables(seq))
     gains = jnp.stack([gain_one, gain_two], 1)
-    f_gains = gather(gains).astype(F32)
-    g1, g2 = f_gains[:, 0][None], f_gains[:, 1][None]
-    cosine, sine = map(jnp.asarray, angle_tables(seq))
     if own:
-        x = swap(tokens, mine).reshape(1, seq, width)
-        cot = swap(cotangent, mine).reshape(1, seq, width)
+        x, f_qkv = opening_call(tokens, w_qkv)
+        x = x.reshape(1, seq, width)
+        f_qkv = f_qkv.reshape(width, -1)
         length = lax.dynamic_slice_in_dim(lengths, mine, 1, 0)
         cq, sq = cosine, sine
     else:
+        f_qkv, f_out, f_gate, f_up, f_down = map(gather, (w_qkv, w_out, w_gate, w_up, w_down))
+        f_gains = gather(gains).astype(F32)
         x, cot, length = tokens, cotangent, lengths
         cq = lax.dynamic_slice_in_dim(cosine, mine * span, span, 0)
         sq = lax.dynamic_slice_in_dim(sine, mine * span, span, 0)
@@ -457,7 +707,18 @@
     position = jnp.arange(seq, dtype=jnp.int32)[None, :, None]
     lane = jnp.arange(PAIR, dtype=jnp.int32)[None, None, :]
     bias = jnp.where((lane == 3) & (position >= length[:, None, None]), NEG, 0.0).astype(BF)
-    att, aug = attend_call(q, k, v, bias)
+    if own:
+        w_out = jnp.pad(jnp.concatenate([w_out, gains], 1), ((0, 0), (0, PAIR - 2)))
+        att, aug, cot, f_out, f_gate, f_up, f_down = attend_call(
+            q, k, v, bias, (cotangent, w_out, w_gate, w_up, w_down)
+        )
+        f_out = f_out.reshape(width, -1)
+        f_out, f_gains = f_out[:, :width], f_out[:, width : width + 2].astype(F32)
+        f_gate, f_up = f_gate.reshape(width, -1), f_up.reshape(width, -1)
+        f_down = f_down.reshape(-1, width)
+    else:
+        att, aug = attend_call(q, k, v, bias)
+    g1, g2 = f_gains[:, 0][None], f_gains[:, 1][None]
     out, d_first, d_att, act, d_gate, d_up, h_t, df_t, att_t, gg1, gg2 = middle_call(
         flat, att.reshape(n * t, width), cot.reshape(n * t, width), f_out, f_gate, f_up, f_down, g1, g2
     )

time: 1040 us -> 934 us (0.90)
  blocking collectives: 236 us -> 106 us
  Pallas kernels: 484 us -> 520 us
  waiting for transfers between devices: 260 us -> 249 us
    all_gather x1 -> x0, blocking collectives: 135 us -> none  [gather(): return lax.all_gather(a, axes, axis=0, tiled=True)]
    pallas_call x1 -> x2, Pallas kernels: 129 us -> 181 us  [the longest x1 123 us: attend_call(): pl.pallas_call(functools.partial(attend_kernel, tile, chunk, moves), grid...]
    all_gather x5 -> x0, waiting for transfers between devices: 24.1 us -> none  [gather(): return lax.all_gather(a, axes, axis=0, tiled=True)]
    reduce_scatter x1, waiting for transfers between devices: 37.7 us -> 53.9 us  [body(): lax.psum_scatter(gw_qkv, axes, scatter_dimension=0, tiled=True).astype(F32)]
    pallas_call x1, Pallas kernels: 165 us -> 150 us  [attend_back_call(): pl.pallas_call(functools.partial(attend_back_kernel, tk, tq), grid=(rows,...]
  transfers between devices with their start and end apart: 17 -> 10, of which waited for: 5 -> 4; matrix products, arithmetic and copies ran while one was open for 4% -> 2% of each run, Pallas kernels for 36% -> 24%
where the time goes in v2:
time: 934 us; the launch traced here: 927 us
  Pallas kernels  520 us (56%)
  waiting for transfers between devices  249 us (27%)
  blocking collectives  106 us (11%)
  other arithmetic  21.4 us (2%)
  between operations  14.7 us (2%)
  local copies, waits for them, and re-layouts  13.8 us (1%)
    reduce_scatter x3, waiting for transfers between devices, scatter_wide(): lax.psum_scatter(g, 'dp', scatter_dimension=0, tiled=True).astype(F32)  193 us
    pallas_call x1, Pallas kernels, attend_back_call(): pl.pallas_call(functools.partial(attend_back_kernel, tk, tq), grid=(rows,...  150 us
    pallas_call x1, Pallas kernels, attend_call(): pl.pallas_call(functools.partial(attend_kernel, tile, chunk, moves), grid...  123 us
    unnamed x1, blocking collectives  106 us
    pallas_call x1, Pallas kernels, middle_call(): pl.pallas_call(functools.partial(middle_kernel, chunk), grid=(tokens // t...  93.2 us
    pallas_call x7, Pallas kernels, outer_call(): pl.pallas_call(outer_kernel, grid=(columns // tile,), in_specs=[pl.BlockS...  70 us
    pallas_call x1, Pallas kernels, opening_call(): pl.pallas_call(opening_kernel, in_specs=[hbm, hbm], out_specs=[hbm, hbm],...  57.3 us
    reduce_scatter x1, waiting for transfers between devices, body(): lax.psum_scatter(gw_qkv, axes, scatter_dimension=0, tiled=True).astype(F32)  53.9 us
  transfers between devices with their start and end apart: 10, of which 4 were waited for; matrix products, arithmetic and copies ran while one was open for 2% of the time, Pallas kernels for 24%

profile of v2, /device:TPU:0, one launch (start us, length us, event | category | flops | bytes accessed | tf_op | source)
XLA Modules:
  0.0 926.9 jit_solution(8669256938652530732)
XLA Ops:
  11.8 57.3 %opening.1 = (bf16[2,1024,768]{2,1,0:T(8,128)(2,1)}, bf16[4,2,2,2,24,2304]{5,4,3,2,1,0:T(8,128)(2,1)}) custom-call(bf16[2,1024,768]{2,1,0:T(8,128)(2,1)} %tok_ref.1, bf16[24,2304]{1,0:T(8,128)(2,1)} %qkv_ref.1), custom_call_target="tpu_custom_call" | custom-call | tf_op jit(solution)/shard_map/opening/pallas_call | solution.py:179
  69.8 13.2 %qkv.1 = (bf16[2048,768]{1,0:T(8,128)(2,1)}, bf16[2048,768]{1,0:T(8,128)(2,1)}, bf16[2048,768]{1,0:T(8,128)(2,1)}, bf16[768,2048]{1,0:T(8,128)(2,1)}) custom-call(bf16[2048,768]{1,0:T(8,128)(2,1)} %bitcast.66, bf16[768,2304]{1,0:T(8,128)(2,1)} %bitcast.56, f32[2048,128]{1,0:T(8,128)} %constant.33.clone.cos_ref.cq_ref.ck_ref, ...), custom_call_target="tpu_custom_call" | custom-call | tf_op jit(solution)/shard_map/qkv/pallas_call | solution.py:221
  83.0 123.4 %attend.1 = (bf16[1,2048,768]{2,1,0:T(8,128)(2,1)}, bf16[1,2048,768]{2,1,0:T(8,128)(2,1)}, bf16[2,1024,768]{2,1,0:T(8,128)(2,1)}, bf16[4,2,2,2,24,896]{5,4,3,2,1...) custom-call(bf16[1,2048,768]{2,1,0:T(8,128)(2,1)} %bitcast.68, ...), custom_call_target="tpu_custom_call" | custom-call | tf_op jit(solution)/shard_map/attend/pallas_call | solution.py:383
  207.4 2.4 slice.24.wo_ref
  211.3 93.2 %middle.1 = (bf16[2048,768]{1,0:T(8,128)(2,1)}, bf16[2048,768]{1,0:T(8,128)(2,1)}, bf16[2048,768]{1,0:T(8,128)(2,1)}, bf16[2048,3072]{1,0:T(8,128)(2,1)}, bf16[2...) custom-call(bf16[2048,768]{1,0:T(8,128)(2,1)} %bitcast.67, ...), custom_call_target="tpu_custom_call" | custom-call | tf_op jit(solution)/shard_map/middle/pallas_call | solution.py:594
  304.5 14.5 %outer.12 = bf16[768,3072]{1,0:T(8,128)(2,1)} custom-call(bf16[768,2048]{1,0:T(8,128)(2,1)} %get-tuple-element.56.a_ref, bf16[2048,3072]{1,0:T(8,128)(2,1)} %get-tuple-element.58.b_ref), custom_call_target="tpu_custom_call" | custom-call | tf_op jit(solution)/shard_map/outer/pallas_call | solution.py:617
  319.1 14.8 %outer.13 = bf16[768,3072]{1,0:T(8,128)(2,1)} custom-call(bf16[768,2048]{1,0:T(8,128)(2,1)} %get-tuple-element.59.a_ref, bf16[2048,3072]{1,0:T(8,128)(2,1)} %get-tuple-element.60.b_ref), custom_call_target="tpu_custom_call" | custom-call | tf_op jit(solution)/shard_map/outer/pallas_call | solution.py:617
  333.9 14.7 %outer.11 = bf16[768,3072]{1,0:T(8,128)(2,1)} custom-call(bf16[768,2048]{1,0:T(8,128)(2,1)} %get-tuple-element.56.a_ref, bf16[2048,3072]{1,0:T(8,128)(2,1)} %get-tuple-element.57.b_ref), custom_call_target="tpu_custom_call" | custom-call | tf_op jit(solution)/shard_map/outer/pallas_call | solution.py:617
  348.7 6.6 outer.10
  355.4 150.0 %attend_back.1 = (bf16[1,2048,768]{2,1,0:T(8,128)(2,1)}, bf16[1,2048,768]{2,1,0:T(8,128)(2,1)}, bf16[1,2048,768]{2,1,0:T(8,128)(2,1)}) custom-call(bf16[1,2048,768]{2,1,0:T(8,128)(2,1)} %bitcast.69, bf16[1,2048,768]{2,1,0:T(8,128)(2,1)} %bitcast.71, bf16[1,2048,768]{2,1,0:T(8,128)(2,1)} %bitcast.73, bf16[1,2048,128]{2,1,0:T(8,128)(2,1)} %select_convert_fusion.bias_ref, ...), custom_call_target="tpu_custom_call" | custom-call | tf_op jit(solution)/shard_map/attend_back/pallas_call | solution.py:488
  505.4 6.4 outer.7
  511.8 6.6 outer.8
  518.3 6.5 outer.9
  524.9 2.9 pad_maximum_fusion
  529.9 12.7 %grad_tokens.1 = bf16[2048,768]{1,0:T(8,128)(2,1)} custom-call(bf16[2048,768]{1,0:T(8,128)(2,1)} %bitcast.59, bf16[2048,768]{1,0:T(8,128)(2,1)} %bitcast.61, bf16[2048,768]{1,0:T(8,128)(2,1)} %bitcast.63, bf16[2048,768]{1,0:T(8,128)(2,1)} %get-tuple-element.53.dfirst_ref.b_ref, bf16[768,2304]{1,0:T(8,128)(2,1)} %bitcast.57), custom_call_target="tpu_custom_call" | custom-call | tf_op jit(solution)/shard_map/grad_tokens/pallas_call | solution.py:644
  542.6 2.8 dynamic-slice_bitcast_fusion
  545.5 1.7 collective-permute-start.1
  547.2 2.7 dynamic-slice_bitcast_fusion.1
  550.2 105.7 %all-reduce.1 = f32[768,2]{0,1:T(2,128)S(1)} all-reduce(f32[768,2]{0,1:T(2,128)S(1)} %maximum_bitcast_fusion), channel_id=10, replica_groups=mesh['dp'=16,'blk'=2] {'dp','blk'}, use_global_device_ids=true, to_apply=%region_8.9.clone | all-reduce | flops 1536 | bytes 12288
  656.5 1.4 convert_element_type.24
  657.9 1.6 fusion
  659.5 1.9 pad_maximum_fusion.2
  662.5 1.6 fusion.2
  664.1 1.9 pad_maximum_fusion.1
  666.1 53.9 %reduce-scatter.10.cloned.1.call-done = bf16[24,2304]{1,0:T(8,128)(2,1)} async-done(((bf16[768,2304]{1,0:T(8,128)(2,1)}), bf16[24,2304]{1,0:T(8,128)(2,1)}) %reduce-scatter.10.cloned.1.call-update) | async-done | bytes 110608 | tf_op jit(solution)/shard_map/reduce_scatter | solution.py:749
  719.9 1.6 convert_element_type.23
  721.5 64.4 %reduce-scatter.20.cloned.1.call-done = bf16[48,1536]{1,0:T(8,128)(2,1)} async-done(((bf16[768,1536]{1,0:T(8,128)(2,1)}), bf16[48,1536]{1,0:T(8,128)(2,1)}) %reduce-scatter.20.cloned.1.call-update) | async-done | bytes 147472 | tf_op jit(solution)/shard_map/reduce_scatter | solution.py:732
  785.9 1.6 convert_element_type.26
  787.6 64.1 %reduce-scatter.24.cloned.1.call-done = bf16[48,1536]{1,0:T(8,128)(2,1)} async-done(((bf16[768,1536]{1,0:T(8,128)(2,1)}), bf16[48,1536]{1,0:T(8,128)(2,1)}) %reduce-scatter.24.cloned.1.call-update) | async-done | bytes 147472 | tf_op jit(solution)/shard_map/reduce_scatter | solution.py:732
  851.7 1.6 convert_bitcast_fusion
  853.4 64.6 %reduce-scatter.16.cloned.1.call-done = bf16[48,1536]{1,0:T(8,128)(2,1)} async-done(((bf16[768,1536]{1,0:T(8,128)(2,1)}), bf16[48,1536]{1,0:T(8,128)(2,1)}) %reduce-scatter.16.cloned.1.call-update) | async-done | bytes 147472 | tf_op jit(solution)/shard_map/reduce_scatter | solution.py:732
  918.0 1.6 convert_element_type.25
  (51 shorter events, 12.0 us)
Async XLA Ops:
  7.2 61.9 %copy-start.4 = (bf16[24,768]{1,0:T(8,128)(2,1)S(1)}, bf16[24,768]{1,0:T(8,128)(2,1)}, u32[]{:S(2)}) copy-start(bf16[24,768]{1,0:T(8,128)(2,1)} %param.15) | copy-start | bytes 110596
  7.2 520.7 %reduce-scatter.18.cloned.1.call-start = ((), (), s32[]{:S(2)}) async-start(), calls=%async_computation.12 | async-start | bytes 7077888 | tf_op jit(solution)/shard_map/reduce_scatter | solution.py:731
  319.0 209.4 %reduce-scatter.22.cloned.1.call-start = ((), (), s32[]{:S(2)}) async-start(), calls=%async_computation.14 | async-start | bytes 7077888 | tf_op jit(solution)/shard_map/reduce_scatter | solution.py:731
  333.9 195.3 %reduce-scatter.14.cloned.1.call-start = ((), (), s32[]{:S(2)}) async-start(), calls=%async_computation.10 | async-start | bytes 7077888 | tf_op jit(solution)/shard_map/reduce_scatter | solution.py:731
  348.6 307.8 %reduce-scatter.12.cloned.1.call-start = ((), (), s32[]{:S(2)}) async-start(), calls=%async_computation.9 | async-start | bytes 1216512 | tf_op jit(solution)/shard_map/reduce_scatter | solution.py:750
  355.3 364.6 %reduce-scatter.10.cloned.1.call-start = ((), (), s32[]{:S(2)}) async-start(), calls=%async_computation.8 | async-start | bytes 3649536 | tf_op jit(solution)/shard_map/reduce_scatter | solution.py:749
  518.3 6.5 copy-start.1
  518.3 6.5 copy-start.2
  527.8 258.1 %reduce-scatter.20.cloned.1.call-start = ((), (), s32[]{:S(2)}) async-start(), calls=%async_computation.13 | async-start | bytes 2506752 | tf_op jit(solution)/shard_map/reduce_scatter | solution.py:732
  528.4 323.3 %reduce-scatter.24.cloned.1.call-start = ((), (), s32[]{:S(2)}) async-start(), calls=%async_computation.15 | async-start | bytes 2506752 | tf_op jit(solution)/shard_map/reduce_scatter | solution.py:732
  529.1 388.8 %reduce-scatter.16.cloned.1.call-start = ((), (), s32[]{:S(2)}) async-start(), calls=%async_computation.11 | async-start | bytes 2506752 | tf_op jit(solution)/shard_map/reduce_scatter | solution.py:732
  542.6 7.5 copy-start.5
  542.6 7.5 copy-start.6
  542.6 115.2 %copy-start = (bf16[2048,768]{1,0:T(8,128)(2,1)S(1)}, bf16[2048,768]{1,0:T(8,128)(2,1)}, u32[]{:S(2)}) copy-start(bf16[2048,768]{1,0:T(8,128)(2,1)} %grad_tokens.1) | copy-start | bytes 9437188
  545.5 112.4 %collective-permute-start.1 = (bf16[1024,768]{1,0:T(8,128)(2,1)}, bf16[1024,768]{1,0:T(8,128)(2,1)}, u32[]{:S(2)}, u32[]{:S(2)}) collective-permute-start(bf16[1024,768]{1,0:T(8,128)(2,1)} %dynamic-slice_bitcast_fusion), channel_id=1, source_target_pairs={{0,1},{1,0},{2,3},{3,2},{4,5},{5,4},{6,7},{7,6},{8,9},{9,8},{10,11... | collective-permute-start | bytes 4718600 | tf_op jit(solution)/shard_map/ppermute | solution.py:669
  549.9 111.6 %collective-permute-start = (bf16[1024,768]{1,0:T(8,128)(2,1)}, bf16[1024,768]{1,0:T(8,128)(2,1)}, u32[]{:S(2)}, u32[]{:S(2)}) collective-permute-start(bf16[1024,768]{1,0:T(8,128)(2,1)} %dynamic-slice_bitcast_fusion.1), channel_id=1, source_target_pairs={{0,1},{1,0},{2,3},{3,2},{4,5},{5,4},{6,7},{7,6},{8,9},{9,8},{10,11... | collective-permute-start | bytes 4718600 | tf_op jit(solution)/shard_map/ppermute | solution.py:669
  659.5 3.0 copy-start.3
Sparse Core Ops, SparseCore 0:
  319.2 64.2 reduce-scatter.17
  385.8 59.9 reduce-scatter.21
  448.2 59.9 reduce-scatter.13
  514.0 97.8 reduce-scatter.11
  618.0 101.9 reduce-scatter.9
  724.0 61.8 reduce-scatter.19
  789.7 61.9 reduce-scatter.23
  856.0 61.9 reduce-scatter.15

commit v3 on v2

--- a/solution.py
+++ b/solution.py
@@ -133,6 +133,107 @@
         for stage in range(len(self.order)):
             for copy in self.copies(stage):
                 copy.wait_send()
+
+
+class Reduce:
+    SEMS = 7
+
+    def __init__(self, me, piece, bufs, out, send, recv, local, base, order):
+        self.me, self.piece, self.out, self.order = me, piece, out, order
+        self.b, self.r0, self.r1, self.r2, self.r3 = bufs
+        self.send, self.recv, self.local, self.base = send, recv, local, base
+
+    def copy(self, source, target, slot, axis, by=1):
+        return pltpu.make_async_remote_copy(
+            src_ref=source,
+            dst_ref=target,
+            send_sem=self.send.at[self.base + slot],
+            recv_sem=self.recv.at[self.base + slot],
+            device_id=device(moved(self.me, axis, by)),
+            device_id_type=MESH,
+        )
+
+    def mine(self):
+        c = self.me["c"]
+        return [
+            pltpu.make_async_copy(self.piece(c, y), self.b.at[y], self.local.at[y]) for y in range(2)
+        ]
+
+    def copies(self, stage):
+        x, y, z = self.me["x"], self.me["y"], self.me["z"]
+        if stage == 0:
+            other = 1 - self.me["c"]
+            return [self.copy(self.piece(other, i), self.r0.at[i], i, "c") for i in range(2)]
+        if stage == 1:
+            source = self.b.at[1 - y] if self.order[0] == "y" else self.b.at[:, :, 1 - x]
+            return [self.copy(source, self.r1, 2, self.order[0])]
+        if stage == 2:
+            source = self.b.at[y, :, 1 - x] if self.order[0] == "y" else self.b.at[1 - y, :, x]
+            return [self.copy(source, self.r2, 3, self.order[1])]
+        return [
+            self.copy(self.b.at[y, lax.rem(z + d, 4), x], self.r3.at[d - 1], 3 + d, "z", d)
+            for d in range(1, 4)
+        ]
+
+    def start(self):
+        for copy in self.copies(0) + self.mine():
+            copy.start()
+
+    def step(self, stage):
+        x, y, z = self.me["x"], self.me["y"], self.me["z"]
+        for copy in self.copies(stage - 1):
+            copy.wait_recv()
+        b, kind = self.b, self.b.dtype
+        if stage == 1:
+            for copy in self.mine():
+                copy.wait()
+
+            def add(i, _):
+                at = (i // 4, i % 4)
+                b[at] = (b[at].astype(F32) + self.r0[at].astype(F32)).astype(kind)
+                return 0
+
+            lax.fori_loop(0, 8, add, 0)
+        if stage == 2:
+
+            def add(i, _):
+                if self.order[0] == "y":
+                    for j in range(2):
+                        b[y, i, j] = (b[y, i, j].astype(F32) + self.r1[i, j].astype(F32)).astype(kind)
+                else:
+                    for j in range(2):
+                        b[j, i, x] = (b[j, i, x].astype(F32) + self.r1[j, i].astype(F32)).astype(kind)
+                return 0
+
+            lax.fori_loop(0, 4, add, 0)
+        if stage == 3:
+
+            def add(i, _):
+                b[y, i, x] = (b[y, i, x].astype(F32) + self.r2[i].astype(F32)).astype(kind)
+                return 0
+
+            lax.fori_loop(0, 4, add, 0)
+        if stage == 4:
+            total = b[y, z, x].astype(F32)
+            for d in range(3):
+                total = total + self.r3[d].astype(F32)
+            self.out[...] = total
+            return
+        for copy in self.copies(stage):
+            copy.start()
+
+    def finish(self):
+        for stage in range(4):
+            for copy in self.copies(stage):
+                copy.wait_send()
+
+    @staticmethod
+    def scratch(rows, columns, kind, order):
+        lead = (4, 2) if order[0] == "y" else (2, 4)
+        return [
+            pltpu.VMEM(shape + (rows, columns), kind)
+            for shape in ((2, 4, 2), (2, 4, 2), lead, (4,), (3,))
+        ]
 
 
 def swap_copies(me, source, target, send, recv, local, slot):
@@ -399,10 +500,17 @@
 
 
 def attend_back_kernel(
-    tk, tq, q_ref, k_ref, v_ref, bias_ref, o_ref, do_ref, aug_ref, cq_ref, sq_ref, ck_ref, sk_ref,
-    dq_ref, dk_ref, dv_ref, qa, ka, va, da, qm, dm, kt, dqt, dk_acc, dv_acc,
+    tk, tq, moves, q_ref, k_ref, v_ref, bias_ref, o_ref, do_ref, aug_ref, cos_ref, sin_ref, *rest
 ):
+    inputs, rest = rest[:moves], rest[moves:]
+    dq_ref, dk_ref, dv_ref, rest = rest[0], rest[1], rest[2], rest[3:]
+    outputs, rest = rest[:moves], rest[moves:]
+    qa, ka, va, da, qm, dm, kt, dqt, dk_acc, dv_acc = rest[:10]
     keys, span = k_ref.shape[1], q_ref.shape[1]
+    nq, nk = span // tq, keys // tk
+    events = {}
+    if moves:
+        events = back_events(inputs, outputs, *rest[10:])
 
     lane_k = lanes((keys, PAIR))
     lane_q = lanes((span, PAIR))
@@ -433,14 +541,15 @@
     kt[...] = k.T
     dqt[...] = jnp.zeros_like(dqt)
 
-    nq, nk = span // tq, keys // tk
-
     def key_step(j, _):
         at_k = pl.ds(pl.multiple_of(j * tk, tk), tk)
         dk_acc[...] = jnp.zeros_like(dk_acc)
         dv_acc[...] = jnp.zeros_like(dv_acc)
 
         def query_step(i, _):
+            now = (pl.program_id(1) * nk + j) * nq + i
+            for at_step, act in events.items():
+                pl.when(now == at_step)(act)
             at_q = pl.ds(pl.multiple_of(i * tq, tq), tq)
             dv, dk = None, None
             for h in range(2):
@@ -458,46 +567,115 @@
             dk_acc[...] += dk
             return 0
 
-        lax.fori_loop(0, nq, query_step, 0, unroll=True)
+        lax.fori_loop(0, nq, query_step, 0)
         dv_ref[0, at_k, :] = dv_acc[...].astype(dv_ref.dtype)
         g = dk_acc[...] * LN2
         if dk_ref.dtype == BF:
-            g = back_turn(g, ck_ref[at_k, :], sk_ref[at_k, :])
+            g = back_turn(g, cos_ref[at_k, :], sin_ref[at_k, :])
         dk_ref[0, at_k, :] = g.astype(dk_ref.dtype)
         return 0
 
     lax.fori_loop(0, nk, key_step, 0)
     g = dqt[...].T * 0.125
-    dq_ref[0] = back_turn(g, cq_ref[...], sq_ref[...]).astype(BF)
+    dq_ref[0] = back_turn(g, cos_ref[...], sin_ref[...]).astype(BF)
+    if moves:
+        pl.when(pl.program_id(1) == pl.num_programs(1) - 1)(events.last)
 
 
 def back_turn(g, cosine, sine):
     return g * cosine - turn(g * sine)
 
 
-def attend_back_call(q, k, v, bias, o, do, aug, cq, sq, ck, sk, whole, tk=1024, tq=512):
+def wide_piece(source, columns):
+    return lambda c, y: source.at[:, :, c, :, pl.ds(y * columns, columns)]
+
+
+def tall_piece(source):
+    return lambda c, y: source.at[:, :, c, y]
+
+
+BACK_ORDERS = ("yx", "xy", "xy", "yx")
+
+
+def back_events(inputs, outputs, send, recv, local, *bufs):
+    me = place()
+    keep, give, take = swap_copies(me, inputs[0], outputs[0], send, recv, local.at[0], 0)
+    reduces = []
+    for i, (source, out) in enumerate(zip(inputs[1:], outputs[1:])):
+        piece = wide_piece(source, source.shape[-1] // 2) if len(source.shape) == 5 else tall_piece(source)
+        reduces.append(
+            Reduce(
+                me, piece, bufs[5 * i : 5 * i + 5], out, send, recv,
+                local.at[pl.ds(1 + 2 * i, 2)], 1 + i * Reduce.SEMS, BACK_ORDERS[i],
+            )
+        )
+
+    def begin():
+        greet(me)
+        for r in reduces:
+            r.start()
+        give.start()
+        keep.start()
+
+    def last():
+        for r in reduces:
+            r.step(4)
+        for r in reduces:
+            r.finish()
+        take.wait_recv()
+        give.wait_send()
+        keep.wait()
+
+    events = Events()
+    events[0] = begin
+    todo = [(n, r) for n in (1, 2, 3) for r in reduces]
+    for at, (n, r) in zip(BACK_TIMES, todo):
+        assert at not in events
+        events[at] = functools.partial(r.step, n)
+    events.last = last
+    return events
+
+
+BACK_TIMES = (5, 6, 7, 8, 16, 17, 21, 18, 24, 28, 32, 25)
+
+
+def attend_back_call(q, k, v, bias, o, do, aug, cosine, sine, whole, moving=(), tk=1024, tq=512):
     rows, span, width = q.shape
     keys = k.shape[1]
     tq = min(tq, span)
     tk = min(tk, keys)
+    moves = len(moving)
     qs = pl.BlockSpec((1, span, PAIR), lambda r, p: (r, 0, p))
     ks = pl.BlockSpec((1, keys, PAIR), lambda r, p: (r, 0, p))
-    tq_s = pl.BlockSpec((span, PAIR), lambda r, p: (0, 0))
-    tk_s = pl.BlockSpec((keys, PAIR), lambda r, p: (0, 0))
+    table = pl.BlockSpec((span, PAIR), lambda r, p: (0, 0), pipeline_mode=pl.Buffered(1))
+    hbm = pl.BlockSpec(memory_space=pl.ANY)
     kv_type = BF if whole else F32
+    results, result_specs, extra, more = [], [], [], {}
+    if moves:
+        results.append(jax.ShapeDtypeStruct(moving[0].shape, BF))
+        result_specs.append(hbm)
+        sems = 1 + Reduce.SEMS * (moves - 1)
+        extra = [pltpu.SemaphoreType.DMA((sems,))] * 2 + [pltpu.SemaphoreType.DMA((2 * moves - 1,))]
+        for a, order in zip(moving[1:], BACK_ORDERS):
+            block = (a.shape[-2], a.shape[-1] // (2 if a.ndim == 5 else 1))
+            results.append(jax.ShapeDtypeStruct(block, F32))
+            result_specs.append(pl.BlockSpec(block, lambda r, p: (0, 0)))
+            extra += Reduce.scratch(*block, a.dtype, order)
+        more = dict(collective_id=2, has_side_effects=True)
     return pl.pallas_call(
-        functools.partial(attend_back_kernel, tk, tq),
+        functools.partial(attend_back_kernel, tk, tq, moves),
         grid=(rows, width // PAIR),
         in_specs=[
-            qs, ks, ks, pl.BlockSpec((1, keys, PAIR), lambda r, p: (r, 0, 0)), qs, qs, qs,
-            tq_s, tq_s, tk_s, tk_s,
-        ],
-        out_specs=[qs, ks, ks],
+            qs, ks, ks, pl.BlockSpec((1, keys, PAIR), lambda r, p: (r, 0, 0)), qs, qs, qs, table, table,
+        ]
+        + [hbm] * moves,
+        out_specs=[qs, ks, ks] + result_specs,
         out_shape=[
             jax.ShapeDtypeStruct(q.shape, BF),
             jax.ShapeDtypeStruct(k.shape, kv_type),
             jax.ShapeDtypeStruct(k.shape, kv_type),
-        ],
+        ]
+        + results,
         scratch_shapes=[
             pltpu.VMEM((span, 2 * PAIR), BF),
             pltpu.VMEM((2, keys, 2 * PAIR), BF),
@@ -509,10 +687,11 @@
             pltpu.VMEM((PAIR, span), F32),
             pltpu.VMEM((tk, PAIR), F32),
             pltpu.VMEM((tk, PAIR), F32),
-        ],
-        compiler_params=params(),
+        ]
+        + extra,
+        compiler_params=pltpu.CompilerParams(vmem_limit_bytes=VMEM_LIMIT, **more),
         name="attend_back",
-    )(q, k, v, bias, o, do, aug, cq, sq, ck, sk)
+    )(q, k, v, bias, o, do, aug, cosine, sine, *moving)
 
 
 def middle_kernel(
@@ -725,33 +904,38 @@
     gw_gate = outer_call(h_t, d_gate, BF)
     gw_up = outer_call(h_t, d_up, BF)
     gw_down_t = outer_call(df_t, act, BF)
-    gw_out = outer_call(att_t, d_first, BF)
-
-    def scatter_wide(g):
-        g = lax.psum_scatter(g, "blk", scatter_dimension=1, tiled=True)
-        return lax.psum_scatter(g, "dp", scatter_dimension=0, tiled=True).astype(F32)
-
-    s_gate, s_up, s_down_t = map(scatter_wide, (gw_gate, gw_up, gw_down_t))
-    s_down = s_down_t.T
-    dq, dk, dv = attend_back_call(
-        q, k, v, bias, att, d_att.reshape(n, t, width), aug, cq, sq, cosine, sine, own
-    )
-    if not own:
+    gw_out = outer_call(att_t, d_first, F32)
+    gains = jnp.pad(jnp.concatenate([gg1, gg2]).T, ((0, 0), (0, PAIR - 2)))
+    gw_out = jnp.concatenate([gw_out, gains], 1)
+    d_att = d_att.reshape(n, t, width)
+    if own:
+        wide = tuple(g.reshape(4, 2, 2, width // 16, -1) for g in (gw_gate, gw_up, gw_down_t))
+        dq, dk, dv, out, s_gate, s_up, s_down_t, s_out = attend_back_call(
+            q, k, v, bias, att, d_att, aug, cq, sq, True,
+            (out.reshape(2, span, width),) + wide + (gw_out.reshape(4, 2, 2, 2, width // 32, -1),),
+        )
+    else:
+
+        def scatter_wide(g):
+            g = lax.psum_scatter(g, "blk", scatter_dimension=1, tiled=True)
+            return lax.psum_scatter(g, "dp", scatter_dimension=0, tiled=True).astype(F32)
+
+        s_gate, s_up, s_down_t = map(scatter_wide, (gw_gate, gw_up, gw_down_t))
+        s_out = lax.psum_scatter(gw_out, axes, scatter_dimension=0, tiled=True)
+        dq, dk, dv = attend_back_call(q, k, v, bias, att, d_att, aug, cq, sq, False)
         dk = lax.psum_scatter(dk, "blk", scatter_dimension=1, tiled=True)
         dv = lax.psum_scatter(dv, "blk", scatter_dimension=1, tiled=True)
         heads = (dk * jnp.tile(sq, (1, width // PAIR))).reshape(n, t, HEADS, HEAD)
         half = jnp.concatenate([heads[..., HEAD // 2 :], -heads[..., : HEAD // 2]], -1)
         dk = dk * jnp.tile(cq, (1, width // PAIR)) + half.reshape(n, t, width)
         dk, dv = dk.astype(BF), dv.astype(BF)
+    s_down = s_down_t.T
+    s_out, s_gg = s_out[:, :width], s_out[:, width : width + 2]
     dq, dk, dv = (a.reshape(n * t, width) for a in (dq, dk, dv))
     gw_qkv = jnp.concatenate([outer_call(xt, a, BF, 256) for a in (dq, dk, dv)], 1)
     g_tokens = tokens_call(dq, dk, dv, d_first, f_qkv)
     s_qkv = lax.psum_scatter(gw_qkv, axes, scatter_dimension=0, tiled=True).astype(F32)
-    s_out = lax.psum_scatter(gw_out, axes, scatter_dimension=0, tiled=True).astype(F32)
-    gg = jnp.concatenate([gg1, gg2]).T
-    s_gg = lax.psum_scatter(gg, axes, scatter_dimension=0, tiled=True)
     if own:
-        out = swap(out.reshape(2, span, width), mine)
         g_tokens = swap(g_tokens.reshape(2, span, width), mine)
     else:
         out = out.reshape(tokens.shape)

time: 934 us -> 688 us (0.74)
  waiting for transfers between devices: 249 us -> 79.8 us
  blocking collectives: 106 us -> 0 us
  Pallas kernels: 520 us -> 562 us
    reduce_scatter x7 -> x0, waiting for transfers between devices: 193 us -> none  [the longest x3 193 us: scatter_wide(): lax.psum_scatter(g, 'dp', scatter_dimension=0, tiled=True).astype(F32)]
    unnamed x1 -> x0, blocking collectives: 106 us -> none
    pallas_call x1, Pallas kernels: 150 us -> 192 us  [attend_back_call(): pl.pallas_call(functools.partial(attend_back_kernel, tk, tq, moves), grid...]
    ppermute x2 -> x1, waiting for transfers between devices: 0.01 us -> 29.4 us  [swap(): got = lax.ppermute(give, 'blk', [(0, 1), (1, 0)])]
  transfers between devices with their start and end apart: 10 -> 2, of which waited for: 4 -> 2; matrix products, arithmetic and copies ran while one was open for 2% -> 1% of each run, Pallas kernels for 24% -> 2%
where the time goes in v3:
time: 688 us; the launch traced here: 687 us
  Pallas kernels  562 us (82%)
  waiting for transfers between devices  79.8 us (12%)
  other arithmetic  15.7 us (2%)
  local copies, waits for them, and re-layouts  14.9 us (2%)
  between operations  14.2 us (2%)
    pallas_call x1, Pallas kernels, attend_back_call(): pl.pallas_call(functools.partial(attend_back_kernel, tk, tq, moves), grid...  192 us
    pallas_call x1, Pallas kernels, attend_call(): pl.pallas_call(functools.partial(attend_kernel, tile, chunk, moves), grid...  123 us
    pallas_call x1, Pallas kernels, middle_call(): pl.pallas_call(functools.partial(middle_kernel, chunk), grid=(tokens // t...  93.3 us
    pallas_call x7, Pallas kernels, outer_call(): pl.pallas_call(outer_kernel, grid=(columns // tile,), in_specs=[pl.BlockS...  69.2 us
    pallas_call x1, Pallas kernels, opening_call(): pl.pallas_call(opening_kernel, in_specs=[hbm, hbm], out_specs=[hbm, hbm],...  57.3 us
    reduce_scatter x1, waiting for transfers between devices, body(): lax.psum_scatter(gw_qkv, axes, scatter_dimension=0, tiled=True).astype(F32)  50.5 us
    ppermute x1, waiting for transfers between devices, swap(): got = lax.ppermute(give, 'blk', [(0, 1), (1, 0)])  29.4 us
  transfers between devices with their start and end apart: 2, of which 2 were waited for; matrix products, arithmetic and copies ran while one was open for 1% of the time, Pallas kernels for 2%

profile of v3, /device:TPU:0, one launch (start us, length us, event | category | flops | bytes accessed | tf_op | source)
XLA Modules:
  0.0 686.6 jit_solution(16166554057306713206)
XLA Ops:
  7.3 1.2 dynamic_slice.10
  9.2 0.7 copy.29
  9.9 0.7 copy.30
  10.6 1.2 select_convert_fusion.bias_ref
  11.8 57.3 %opening.1 = (bf16[2,1024,768]{2,1,0:T(8,128)(2,1)}, bf16[4,2,2,2,24,2304]{5,4,3,2,1,0:T(8,128)(2,1)}) custom-call(bf16[2,1024,768]{2,1,0:T(8,128)(2,1)} %tok_ref.1, bf16[24,2304]{1,0:T(8,128)(2,1)} %qkv_ref.1), custom_call_target="tpu_custom_call" | custom-call | tf_op jit(solution)/shard_map/opening/pallas_call | solution.py:280
  69.8 13.3 %qkv.1 = (bf16[2048,768]{1,0:T(8,128)(2,1)}, bf16[2048,768]{1,0:T(8,128)(2,1)}, bf16[2048,768]{1,0:T(8,128)(2,1)}, bf16[768,2048]{1,0:T(8,128)(2,1)}) custom-call(bf16[2048,768]{1,0:T(8,128)(2,1)} %bitcast.59, bf16[768,2304]{1,0:T(8,128)(2,1)} %bitcast.42, f32[2048,128]{1,0:T(8,128)} %constant.30.clone.cos_ref, f32[2048,128]{1,0:T(8,128)} %constant.31.clone.sin_ref), custom_call_target="tpu_custom_call" | custom-call | tf_op jit(solution)/shard_map/qkv/pallas_call | solution.py:322
  83.1 123.3 %attend.1 = (bf16[1,2048,768]{2,1,0:T(8,128)(2,1)}, bf16[1,2048,768]{2,1,0:T(8,128)(2,1)}, bf16[2,1024,768]{2,1,0:T(8,128)(2,1)}, bf16[4,2,2,2,24,896]{5,4,3,2,1...) custom-call(bf16[1,2048,768]{2,1,0:T(8,128)(2,1)} %bitcast.50, ...), custom_call_target="tpu_custom_call" | custom-call | tf_op jit(solution)/shard_map/attend/pallas_call | solution.py:484
  206.4 1.0 slice_convert_fusion
  207.4 2.4 slice.31.wo_ref
  211.3 93.3 %middle.1 = (bf16[2048,768]{1,0:T(8,128)(2,1)}, bf16[2048,768]{1,0:T(8,128)(2,1)}, bf16[2048,768]{1,0:T(8,128)(2,1)}, bf16[2048,3072]{1,0:T(8,128)(2,1)}, bf16[2...) custom-call(bf16[2048,768]{1,0:T(8,128)(2,1)} %bitcast.60, ...), custom_call_target="tpu_custom_call" | custom-call | tf_op jit(solution)/shard_map/middle/pallas_call | solution.py:773
  304.6 0.7 pad_maximum_fusion.2
  305.5 14.5 %outer.8 = bf16[768,3072]{1,0:T(8,128)(2,1)} custom-call(bf16[768,2048]{1,0:T(8,128)(2,1)} %get-tuple-element.55.a_ref, bf16[2048,3072]{1,0:T(8,128)(2,1)} %get-tuple-element.57.b_ref), custom_call_target="tpu_custom_call" | custom-call | tf_op jit(solution)/shard_map/outer/pallas_call | solution.py:796
  320.0 14.4 %outer.7 = bf16[768,3072]{1,0:T(8,128)(2,1)} custom-call(bf16[768,2048]{1,0:T(8,128)(2,1)} %get-tuple-element.55.a_ref, bf16[2048,3072]{1,0:T(8,128)(2,1)} %get-tuple-element.56.b_ref), custom_call_target="tpu_custom_call" | custom-call | tf_op jit(solution)/shard_map/outer/pallas_call | solution.py:796
  334.4 6.7 outer.10
  341.1 3.5 select_maximum_fusion
  344.6 14.4 %outer.9 = bf16[768,3072]{1,0:T(8,128)(2,1)} custom-call(bf16[768,2048]{1,0:T(8,128)(2,1)} %get-tuple-element.58.a_ref, bf16[2048,3072]{1,0:T(8,128)(2,1)} %get-tuple-element.59.b_ref), custom_call_target="tpu_custom_call" | custom-call | tf_op jit(solution)/shard_map/outer/pallas_call | solution.py:796
  359.0 192.5 %attend_back.1 = (bf16[1,2048,768]{2,1,0:T(8,128)(2,1)}, bf16[1,2048,768]{2,1,0:T(8,128)(2,1)}, bf16[1,2048,768]{2,1,0:T(8,128)(2,1)}, bf16[2,1024,768]{2,1,0:T(...) custom-call(bf16[1,2048,768]{2,1,0:T(8,128)(2,1)} %bitcast.51, ...), custom_call_target="tpu_custom_call" | custom-call | tf_op jit(solution)/shard_map/attend_back/pallas_call | solution.py:665
  551.5 6.4 outer.11
  557.9 6.3 outer.12
  564.2 6.5 outer.13
  570.7 2.9 pad_maximum_fusion
  573.6 12.8 %grad_tokens.1 = bf16[2048,768]{1,0:T(8,128)(2,1)} custom-call(bf16[2048,768]{1,0:T(8,128)(2,1)} %bitcast.45, bf16[2048,768]{1,0:T(8,128)(2,1)} %bitcast.47, bf16[2048,768]{1,0:T(8,128)(2,1)} %bitcast.49, bf16[2048,768]{1,0:T(8,128)(2,1)} %get-tuple-element.61.b_ref.dfirst_ref, bf16[768,2304]{1,0:T(8,128)(2,1)} %bitcast.43), custom_call_target="tpu_custom_call" | custom-call | tf_op jit(solution)/shard_map/grad_tokens/pallas_call | solution.py:823
  586.4 2.8 dynamic-slice_bitcast_fusion
  590.9 29.4 %collective-permute-done = bf16[1024,768]{1,0:T(8,128)(2,1)} collective-permute-done((bf16[1024,768]{1,0:T(8,128)(2,1)}, bf16[1024,768]{1,0:T(8,128)(2,1)}, u32[]{:S(2)}, u32[]{:S(2)}) %collective-permute-start) | collective-permute-done | bytes 1572896 | tf_op jit(solution)/shard_map/ppermute | solution.py:848
  620.3 1.6 fusion
  621.9 1.9 pad_maximum_fusion.1
  623.8 50.5 %reduce-scatter.2.cloned.1.call-done = bf16[24,2304]{1,0:T(8,128)(2,1)} async-done(((bf16[768,2304]{1,0:T(8,128)(2,1)}), bf16[24,2304]{1,0:T(8,128)(2,1)}) %reduce-scatter.2.cloned.1.call-update) | async-done | bytes 110608 | tf_op jit(solution)/shard_map/reduce_scatter | solution.py:937
  674.3 1.6 convert_element_type.15
  675.9 1.7 copy.36
  677.6 0.7 copy.37
  678.3 0.7 copy.38
  679.0 0.7 copy.39
  (30 shorter events, 4.8 us)
Async XLA Ops:
  7.2 61.9 %copy-start.8 = (bf16[24,768]{1,0:T(8,128)(2,1)S(1)}, bf16[24,768]{1,0:T(8,128)(2,1)}, u32[]{:S(2)}) copy-start(bf16[24,768]{1,0:T(8,128)(2,1)} %param.15) | copy-start | bytes 110596
  7.2 667.1 %reduce-scatter.2.cloned.1.call-start = ((), (), s32[]{:S(2)}) async-start(), calls=%async_computation.1 | async-start | bytes 3649536 | tf_op jit(solution)/shard_map/reduce_scatter | solution.py:937
  564.2 6.5 copy-start.1
  564.2 6.5 copy-start.2
  573.6 15.9 %copy-start.7 = (f32[24,896]{1,0:T(8,128)S(1)}, f32[24,896]{1,0:T(8,128)}, u32[]{:S(2)}) copy-start(f32[24,896]{1,0:T(8,128)} %get-tuple-element.69) | copy-start | bytes 258052
  586.4 33.8 %copy-start = (bf16[2048,768]{1,0:T(8,128)(2,1)S(1)}, bf16[2048,768]{1,0:T(8,128)(2,1)}, u32[]{:S(2)}) copy-start(bf16[2048,768]{1,0:T(8,128)(2,1)} %grad_tokens.1) | copy-start | bytes 9437188
  589.3 31.0 %collective-permute-start = (bf16[1024,768]{1,0:T(8,128)(2,1)}, bf16[1024,768]{1,0:T(8,128)(2,1)}, u32[]{:S(2)}, u32[]{:S(2)}) collective-permute-start(bf16[1024,768]{1,0:T(8,128)(2,1)} %dynamic-slice_bitcast_fusion), channel_id=1, source_target_pairs={{0,1},{1,0},{2,3},{3,2},{4,5},{5,4},{6,7},{7,6},{8,9},{9,8},{10,11... | collective-permute-start | bytes 4718600 | tf_op jit(solution)/shard_map/ppermute | solution.py:848
  621.9 54.0 %copy-start.3 = (bf16[2,1024,768]{2,1,0:T(8,128)(2,1)S(1)}, bf16[2,1024,768]{2,1,0:T(8,128)(2,1)}, u32[]{:S(2)}) copy-start(bf16[2,1024,768]{2,1,0:T(8,128)(2,1)} %get-tuple-element.88) | copy-start | bytes 9437188
  675.9 1.7 copy-start.6
  675.9 2.4 copy-start.5
  675.9 3.1 copy-start.4
Sparse Core Ops, SparseCore 0:
  573.7 100.5 reduce-scatter.1

commit v4 on v3

--- a/solution.py
+++ b/solution.py
@@ -70,41 +70,47 @@
 
 
 class Gather:
-    SEMS = 6
-
-    def __init__(self, me, shard, full, send, recv, local, base, order):
-        self.me, self.shard, self.full = me, shard, full
+    def __init__(self, me, shard, full, send, recv, local, base, order, held="", columns=None):
+        self.me, self.full, self.held = me, full, held
+        self.part = () if columns is None else (slice(None), pl.ds(*columns))
+        lead = (slice(None),) * len(held)
+        self.shard = shard.at[lead + self.part] if self.part else shard
         self.send, self.recv, self.local, self.base, self.order = send, recv, local, base, order
 
+    @staticmethod
+    def sems(order):
+        return sum(SIZE[a] - 1 for a in order)
+
     def view(self, at, got):
-        return self.full.at[tuple(slice(None) if a in got else at[a] for a in AXES)]
+        return self.full.at[tuple(slice(None) if a in got else at[a] for a in AXES if a in self.axes()) + self.part]
+
+    def axes(self):
+        return AXES if len(self.full.shape) == 6 else "z"
+
+    def at_stage(self, stage):
+        got = self.held + self.order[:stage]
+        return got, self.order[stage], self.base + self.sems(self.order[:stage])
 
     def copies(self, stage):
-        got = self.order[:stage]
-        axis = self.order[stage]
-        slot = self.base + sum(SIZE[a] - 1 for a in got)
-        out = []
-        for d in range(1, SIZE[axis]):
-            here = self.view(self.me, got)
-            out.append(
-                pltpu.make_async_remote_copy(
-                    src_ref=self.shard if stage == 0 else here,
-                    dst_ref=here,
-                    send_sem=self.send.at[slot + d - 1],
-                    recv_sem=self.recv.at[slot + d - 1],
-                    device_id=device(moved(self.me, axis, d)),
-                    device_id_type=MESH,
-                )
+        got, axis, slot = self.at_stage(stage)
+        here = self.view(self.me, got)
+        return [
+            pltpu.make_async_remote_copy(
+                src_ref=self.shard if stage == 0 else here,
+                dst_ref=here,
+                send_sem=self.send.at[slot + d - 1],
+                recv_sem=self.recv.at[slot + d - 1],
+                device_id=device(moved(self.me, axis, d)),
+                device_id_type=MESH,
             )
-        return out
+            for d in range(1, SIZE[axis])
+        ]
 
     def own(self):
-        return pltpu.make_async_copy(self.shard, self.view(self.me, ""), self.local)
+        return pltpu.make_async_copy(self.shard, self.view(self.me, self.held), self.local)
 
     def arrivals(self, stage):
-        got = self.order[:stage]
-        axis = self.order[stage]
-        slot = self.base + sum(SIZE[a] - 1 for a in got)
+        got, axis, slot = self.at_stage(stage)
         for d in range(1, SIZE[axis]):
             there = self.view(moved(self.me, axis, SIZE[axis] - d), got)
             pltpu.make_async_remote_copy(
@@ -259,40 +265,70 @@
     return keep, give, take
 
 
-def opening_kernel(tok_ref, qkv_ref, x_ref, full_ref, send, recv, local):
+OPENING_ORDERS = ("yzxc", "zyxc", "z", "z", "z")
+
+
+def opening_kernel(tok_ref, qkv_ref, *rest):
+    early, rest = rest[:3], rest[3:]
+    x_ref, full_ref, rest = rest[0], rest[1], rest[2:]
+    early_out, (send, recv, local) = rest[:3], rest[3:]
     me = place()
     greet(me)
     keep, give, take = swap_copies(me, tok_ref, x_ref, send, recv, local.at[0], 0)
-    gather = Gather(me, qkv_ref, full_ref, send, recv, local.at[1], 1, "yzxc")
-    gather.start()
+    half = qkv_ref.shape[-1] // 2
+    sources = [(qkv_ref, full_ref, (0, half)), (qkv_ref, full_ref, (half, half))]
+    sources += [(a, b, None) for a, b in zip(early, early_out)]
+    gathers, base = [], 1
+    for i, (source, full, columns) in enumerate(sources):
+        order = OPENING_ORDERS[i]
+        gathers.append(
+            Gather(me, source, full, send, recv, local.at[1 + i], base, order, "", columns)
+        )
+        base += Gather.sems(order)
+    first, second, later = gathers[0], gathers[1], gathers[2:]
+    first.start()
+    second.start()
     give.start()
     keep.start()
-    for stage in range(1, 5):
-        gather.step(stage)
-    gather.finish()
+    first.step(1)
+    second.step(1)
+    first.step(2)
+    for g in later:
+        g.start()
+    second.step(2)
+    first.step(3)
+    second.step(3)
+    first.step(4)
+    second.step(4)
+    for g in later:
+        g.step(1)
+    for g in gathers:
+        g.finish()
     take.wait_recv()
     give.wait_send()
     keep.wait()
 
 
-def opening_call(tokens, w_qkv):
+def opening_call(tokens, w_qkv, early):
     hbm = pl.BlockSpec(memory_space=pl.ANY)
+    sems = 1 + sum(map(Gather.sems, OPENING_ORDERS))
     return pl.pallas_call(
         opening_kernel,
-        in_specs=[hbm, hbm],
-        out_specs=[hbm, hbm],
+        in_specs=[hbm] * 5,
+        out_specs=[hbm] * 5,
         out_shape=[
             jax.ShapeDtypeStruct(tokens.shape, BF),
             jax.ShapeDtypeStruct((4, 2, 2, 2) + w_qkv.shape, BF),
-        ],
+        ]
+        + [jax.ShapeDtypeStruct((4,) + a.shape, BF) for a in early],
         scratch_shapes=[
-            pltpu.SemaphoreType.DMA((1 + Gather.SEMS,)),
-            pltpu.SemaphoreType.DMA((1 + Gather.SEMS,)),
-            pltpu.SemaphoreType.DMA((2,)),
+            pltpu.SemaphoreType.DMA((sems,)),
+            pltpu.SemaphoreType.DMA((sems,)),
+            pltpu.SemaphoreType.DMA((6,)),
         ],
         compiler_params=pltpu.CompilerParams(collective_id=0, has_side_effects=True),
         name="opening",
-    )(tokens, w_qkv)
+    )(tokens, w_qkv, *early)
 
 
 def qkv_kernel(x_ref, w_ref, cos_ref, sin_ref, q_ref, k_ref, v_ref, xt_ref):
@@ -345,24 +381,27 @@
     tiles = span // tile
     events = {}
     if moves:
-        events = attend_events(inputs, outputs, tiles * pl.num_programs(1), *rest[4:])
-    lane = lanes((keys, PAIR))
-    k, v = k_ref[0], v_ref[0]
-    zero = jnp.zeros_like(k)
-    for h in range(2):
-        mine = (lane // HEAD) == h
-        ka[h, :, :PAIR] = jnp.where(mine, k, zero)
-        ka[h, :, PAIR:] = bias_ref[0]
-        va[h, :, :PAIR] = jnp.where(mine, v, zero)
-        va[h, :, PAIR:] = mine.astype(F32).astype(BF)
+        events = attend_events(inputs, outputs, *rest[4:])
+
+    @pl.when(pl.program_id(1) == 0)
+    def _():
+        ka[:, PAIR:] = bias_ref[0]
+        va[:, PAIR:] = jnp.ones((keys, PAIR), BF)
+
+    ka[:, :PAIR] = k_ref[0]
+    va[:, :PAIR] = v_ref[0]
     lane = lanes((tile, PAIR))
-    ones = (lane == 3).astype(F32).astype(BF)
+    side = lanes((tile, 2 * PAIR)) // HEAD % 2
+    ones = (lane % HEAD == 3).astype(F32).astype(BF)
     chunks = keys // chunk
 
-    def score(i, h, c, top):
+    def query(i, h):
         at = pl.ds(pl.multiple_of(i * tile, tile), tile)
-        qa = jnp.concatenate([q_ref[0, at, :], ones], axis=1)
-        s = dot_nt(qa, ka[h, c * chunk : (c + 1) * chunk, :])
+        both = jnp.concatenate([q_ref[0, at, :], ones], axis=1)
+        return jnp.where(side == h, both, jnp.zeros_like(both))
+
+    def score(qa, h, c, top):
+        s = dot_nt(qa, ka[c * chunk : (c + 1) * chunk, :])
         s_scr[h, :, c * chunk : (c + 1) * chunk] = s
         for b in range(chunk // PAIR):
             part = s[:, b * PAIR : (b + 1) * PAIR]
@@ -375,84 +414,88 @@
     def unit(h, later, other):
         m = m_scr[h]
         wide = jnp.concatenate([m] * (chunk // PAIR), axis=1)
+        qa = query(later, other)
         acc, top = None, None
         for c in range(chunks):
-            top = score(later, other, c, top)
+            top = score(qa, other, c, top)
             p = jnp.exp2(s_scr[h, :, c * chunk : (c + 1) * chunk] - wide).astype(BF)
-            part = dot(p, va[h, c * chunk : (c + 1) * chunk, :])
+            part = dot(p, va[c * chunk : (c + 1) * chunk, :])
             acc = part if acc is None else acc + part
         return acc, top, m
 
     top = None
+    qa = query(0, 0)
     for c in range(chunks):
-        top = score(0, 0, c, top)
+        top = score(qa, 0, c, top)
     close(0, top)
 
     def step(i, _):
         now = pl.program_id(1) * tiles + i
-        for at_step, act in events.items():
-            pl.when(now == at_step)(act)
+        for at_step, acts in events.items():
+
+            @pl.when(now == at_step)
+            def _():
+                for act in acts:
+                    act()
+
         acc0, top, m0 = unit(0, i, 1)
         close(1, top)
         acc1, top, m1 = unit(1, jnp.minimum(i + 1, tiles - 1), 0)
         close(0, top)
-        acc = acc0 + acc1
-        total = acc[:, PAIR:]
+        mine = lane < HEAD
+        total = jnp.where(mine, acc0[:, PAIR:], acc1[:, PAIR:])
         at = pl.ds(pl.multiple_of(i * tile, tile), tile)
-        o_ref[0, at, :] = (acc[:, :PAIR] / total).astype(BF)
-        lse = jnp.where(lane < HEAD, m0, m1) + jnp.log2(total)
-        aug_ref[0, at, :] = spread(lse, jnp.where(lane == 3, 1.0, 0.0))
+        o_ref[0, at, :] = (jnp.where(mine, acc0[:, :PAIR], acc1[:, :PAIR]) / total).astype(BF)
+        lse = jnp.where(mine, m0, m1) + jnp.log2(total)
+        aug_ref[0, at, :] = spread(lse, jnp.where(lane % HEAD == 3, 1.0, 0.0))
         return 0
 
     lax.fori_loop(0, tiles, step, 0)
     if moves:
-        pl.when(pl.program_id(1) == pl.num_programs(1) - 1)(events.last)
+
+        @pl.when(pl.program_id(1) == pl.num_programs(1) - 1)
+        def _():
+            for act in events.last:
+                act()
 
 
 class Events(dict):
-    last = None
-
-
-def attend_events(inputs, outputs, steps, send, recv, local):
+    def __init__(self):
+        self.last = []
+
+    def put(self, at, *acts):
+        self.setdefault(at, []).extend(acts)
+
+
+ATTEND_ORDERS = ("xyc", "xyc", "yxc", "yzxc")
+ATTEND_PLAN = (
+    (3, 3, 1), (7, 1, 1), (7, 2, 1), (8, 0, 1), (13, 3, 2), (16, 0, 2), (17, 1, 2), (18, 2, 2),
+)
+ATTEND_SWAP = 9
+
+
+def attend_events(inputs, outputs, send, recv, local):
     me = place()
-    cot_in, shards = inputs[0], inputs[1:]
-    cot_out, fulls = outputs[0], outputs[1:]
-    keep, give, take = swap_copies(me, cot_in, cot_out, send, recv, local.at[0], 0)
-    orders = ["zxyc", "zxyc", "zyxc", "yzxc"]
-    gathers = [
-        Gather(me, shard, full, send, recv, local.at[1 + i], 1 + i * Gather.SEMS, orders[i])
-        for i, (shard, full) in enumerate(zip(shards, fulls))
-    ]
-
-    def begin():
-        greet(me)
-        for g in gathers:
-            g.start()
-        give.start()
-        keep.start()
-
-    def stage(g, n):
-        return lambda: g.step(n)
-
-    def last():
-        for n, g in pending:
-            g.step(n)
-        for g in gathers:
-            g.finish()
-        take.wait_recv()
-        give.wait_send()
-        keep.wait()
-
+    keep, give, take = swap_copies(me, inputs[0], outputs[0], send, recv, local.at[0], 0)
+    gathers, base = [], 1
+    for i, (shard, full) in enumerate(zip(inputs[1:], outputs[1:])):
+        held = "z" if i < 3 else ""
+        gathers.append(
+            Gather(me, shard, full, send, recv, local.at[1 + i], base, ATTEND_ORDERS[i], held)
+        )
+        base += Gather.sems(ATTEND_ORDERS[i])
     events = Events()
-    events[0] = begin
-    todo = [(n, g) for n in (1, 2, 3, 4) for g in gathers]
-    times = [4, 6, 9, 5, 6, 9, 12, 11, 12, 16, 19, 20]
-    for at, (n, g) in zip(times, todo):
-        old = events.get(at)
-        new = stage(g, n)
-        events[at] = new if old is None else (lambda old=old, new=new: (old(), new(), None)[2])
-    pending = todo[len(times) :]
-    events.last = last
+    events.put(0, functools.partial(greet, me), *(gathers[i].start for i in (3, 1, 2, 0)))
+    events.put(ATTEND_SWAP, give.start, keep.start)
+    done = [1] * len(gathers)
+    for at, i, stage in ATTEND_PLAN:
+        events.put(at, functools.partial(gathers[i].step, stage))
+        done[i] = stage + 1
+    for stage in range(1, 5):
+        for i, g in enumerate(gathers):
+            if done[i] <= stage <= len(ATTEND_ORDERS[i]):
+                events.last.append(functools.partial(g.step, stage))
+    events.last += [g.finish for g in gathers] + [take.wait_recv, give.wait_send, keep.wait]
     return events
 
 
@@ -476,9 +519,9 @@
     ks = pl.BlockSpec((1, keys, PAIR), lambda r, p: (r, 0, p))
     hbm = pl.BlockSpec(memory_space=pl.ANY)
     moved_shapes = [jax.ShapeDtypeStruct(a.shape, a.dtype) for a in moving[:1]] + [
-        jax.ShapeDtypeStruct((4, 2, 2, 2) + a.shape, a.dtype) for a in moving[1:]
+        jax.ShapeDtypeStruct((4, 2, 2, 2) + a.shape[-2:], a.dtype) for a in moving[1:]
     ]
-    sems = 1 + Gather.SEMS * max(moves - 1, 0)
+    sems = 1 + sum(map(Gather.sems, ATTEND_ORDERS))
     extra = [pltpu.SemaphoreType.DMA((sems,))] * 2 + [pltpu.SemaphoreType.DMA((moves,))]
     more = dict(collective_id=1, has_side_effects=True) if moves else {}
     return pl.pallas_call(
@@ -488,8 +531,8 @@
         out_specs=[qs, qs] + [hbm] * moves,
         out_shape=[jax.ShapeDtypeStruct(q.shape, BF)] * 2 + moved_shapes,
         scratch_shapes=[
-            pltpu.VMEM((2, keys, 2 * PAIR), BF),
-            pltpu.VMEM((2, keys, 2 * PAIR), BF),
+            pltpu.VMEM((keys, 2 * PAIR), BF),
+            pltpu.VMEM((keys, 2 * PAIR), BF),
             pltpu.VMEM((2, tile, keys), F32),
             pltpu.VMEM((2, tile, PAIR), F32),
         ]
@@ -505,17 +548,23 @@
     inputs, rest = rest[:moves], rest[moves:]
     dq_ref, dk_ref, dv_ref, rest = rest[0], rest[1], rest[2], rest[3:]
     outputs, rest = rest[:moves], rest[moves:]
-    qa, ka, va, da, qm, dm, kt, dqt, dk_acc, dv_acc = rest[:10]
+    qa, da, ka, va, kt, dqt, dk_acc, dv_acc = rest[:8]
     keys, span = k_ref.shape[1], q_ref.shape[1]
     nq, nk = span // tq, keys // tk
     events = {}
     if moves:
-        events = back_events(inputs, outputs, *rest[10:])
-
-    lane_k = lanes((keys, PAIR))
-    lane_q = lanes((span, PAIR))
-    q, k, v, do = q_ref[0], k_ref[0], v_ref[0], do_ref[0]
-    bias = bias_ref[0].astype(F32)
+        events = back_events(inputs, outputs, *rest[8:])
+
+    @pl.when(pl.program_id(1) == 0)
+    def _():
+        minus = jnp.where(lanes((keys, PAIR)) % HEAD < 3, -1.0, 0.0)
+        ka[:, PAIR:] = (minus + bias_ref[0].astype(F32)).astype(BF)
+        va[:, PAIR:] = minus.astype(BF)
+
+    k, do = k_ref[0], do_ref[0]
+    ka[:, :PAIR] = k
+    va[:, :PAIR] = v_ref[0]
+    kt[...] = k.T
     prod = do.astype(F32) * o_ref[0].astype(F32)
     first = prod.astype(BF)
     second = (prod - first.astype(F32)).astype(BF)
@@ -524,41 +573,37 @@
         == (lax.broadcasted_iota(jnp.int32, (PAIR, PAIR), 1) // HEAD)
     ).astype(F32).astype(BF)
     delta = dot(first, block) + dot(second, block)
-    qa[:, :PAIR] = q
-    qa[:, PAIR:] = aug_ref[0]
-    da[:, :PAIR] = do
-    da[:, PAIR:] = spread(delta, jnp.zeros_like(delta))
+    q_both = jnp.concatenate([q_ref[0], aug_ref[0]], axis=1)
+    d_both = jnp.concatenate([do, spread(delta, jnp.zeros_like(delta))], axis=1)
+    side = lanes(q_both.shape) // HEAD % 2
     for h in range(2):
-        mine_k = (lane_k // HEAD) == h
-        mine_q = (lane_q // HEAD) == h
-        minus = jnp.where(mine_k & (lane_k % HEAD < 3), -1.0, 0.0)
-        ka[h, :, :PAIR] = jnp.where(mine_k, k, jnp.zeros_like(k))
-        ka[h, :, PAIR:] = (minus + bias).astype(BF)
-        va[h, :, :PAIR] = jnp.where(mine_k, v, jnp.zeros_like(v))
-        va[h, :, PAIR:] = minus.astype(BF)
-        qm[h] = jnp.where(mine_q, q, jnp.zeros_like(q))
-        dm[h] = jnp.where(mine_q, do, jnp.zeros_like(do))
-    kt[...] = k.T
+        qa[h] = jnp.where(side == h, q_both, jnp.zeros_like(q_both))
+        da[h] = jnp.where(side == h, d_both, jnp.zeros_like(d_both))
     dqt[...] = jnp.zeros_like(dqt)
 
     def key_step(j, _):
+        now = pl.program_id(1) * nk + j
+        for at_step, acts in events.items():
+
+            @pl.when(now == at_step)
+            def _():
+                for act in acts:
+                    act()
+
         at_k = pl.ds(pl.multiple_of(j * tk, tk), tk)
         dk_acc[...] = jnp.zeros_like(dk_acc)
         dv_acc[...] = jnp.zeros_like(dv_acc)
 
         def query_step(i, _):
-            now = (pl.program_id(1) * nk + j) * nq + i
-            for at_step, act in events.items():
-                pl.when(now == at_step)(act)
             at_q = pl.ds(pl.multiple_of(i * tq, tq), tq)
             dv, dk = None, None
             for h in range(2):
-                st = dot_nt(ka[h, at_k, :], qa[at_q, :])
-                dpt = dot_nt(va[h, at_k, :], da[at_q, :])
+                st = dot_nt(ka[at_k, :], qa[h, at_q, :])
+                dpt = dot_nt(va[at_k, :], da[h, at_q, :])
                 p = jnp.exp2(st)
                 ds = (p * dpt).astype(BF)
-                pv = dot(p.astype(BF), dm[h, at_q, :])
-                pk = dot(ds, qm[h, at_q, :])
+                pv = dot(p.astype(BF), da[h, at_q, :PAIR])
+                pk = dot(ds, qa[h, at_q, :PAIR])
                 dv = pv if dv is None else dv + pv
                 dk = pk if dk is None else dk + pk
                 head = slice(h * HEAD, (h + 1) * HEAD)
@@ -567,7 +612,7 @@
             dk_acc[...] += dk
             return 0
 
-        lax.fori_loop(0, nq, query_step, 0)
+        lax.fori_loop(0, nq, query_step, 0, unroll=True)
         dv_ref[0, at_k, :] = dv_acc[...].astype(dv_ref.dtype)
         g = dk_acc[...] * LN2
         if dk_ref.dtype == BF:
@@ -579,7 +624,11 @@
     g = dqt[...].T * 0.125
     dq_ref[0] = back_turn(g, cos_ref[...], sin_ref[...]).astype(BF)
     if moves:
-        pl.when(pl.program_id(1) == pl.num_programs(1) - 1)(events.last)
+
+        @pl.when(pl.program_id(1) == pl.num_programs(1) - 1)
+        def _():
+            for act in events.last:
+                act()
 
 
 def back_turn(g, cosine, sine):
@@ -594,7 +643,12 @@
     return lambda c, y: source.at[:, :, c, y]
 
 
-BACK_ORDERS = ("yx", "xy", "xy", "yx")
+BACK_ORDERS = ("yx", "yx", "xy", "xy")
+BACK_PLAN = (
+    (1, 0, 1), (1, 2, 1), (4, 0, 2), (4, 1, 1), (5, 3, 1), (5, 0, 3), (7, 1, 2), (7, 2, 2),
+    (8, 3, 2), (9, 1, 3), (9, 2, 3), (10, 3, 3),
+)
+BACK_SWAP = 8
 
 
 def back_events(inputs, outputs, send, recv, local, *bufs):
@@ -609,34 +663,14 @@
                 local.at[pl.ds(1 + 2 * i, 2)], 1 + i * Reduce.SEMS, BACK_ORDERS[i],
             )
         )
-
-    def begin():
-        greet(me)
-        for r in reduces:
-            r.start()
-        give.start()
-        keep.start()
-
-    def last():
-        for r in reduces:
-            r.step(4)
-        for r in reduces:
-            r.finish()
-        take.wait_recv()
-        give.wait_send()
-        keep.wait()
-
     events = Events()
-    events[0] = begin
-    todo = [(n, r) for n in (1, 2, 3) for r in reduces]
-    for at, (n, r) in zip(BACK_TIMES, todo):
-        assert at not in events
-        events[at] = functools.partial(r.step, n)
-    events.last = last
+    events.put(0, functools.partial(greet, me), *(reduces[i].start for i in (0, 2, 1, 3)))
+    for at, i, stage in BACK_PLAN:
+        events.put(at, functools.partial(reduces[i].step, stage))
+    events.put(BACK_SWAP, give.start, keep.start)
+    events.last += [functools.partial(r.step, 4) for r in reduces] + [r.finish for r in reduces]
+    events.last += [take.wait_recv, give.wait_send, keep.wait]
     return events
-
-
-BACK_TIMES = (5, 6, 7, 8, 16, 17, 21, 18, 24, 28, 32, 25)
 
 
 def attend_back_call(q, k, v, bias, o, do, aug, cosine, sine, whole, moving=(), tk=1024, tq=512):
@@ -677,12 +711,10 @@
         ]
         + results,
         scratch_shapes=[
-            pltpu.VMEM((span, 2 * PAIR), BF),
-            pltpu.VMEM((2, keys, 2 * PAIR), BF),
-            pltpu.VMEM((2, keys, 2 * PAIR), BF),
-            pltpu.VMEM((span, 2 * PAIR), BF),
-            pltpu.VMEM((2, span, PAIR), BF),
-            pltpu.VMEM((2, span, PAIR), BF),
+            pltpu.VMEM((2, span, 2 * PAIR), BF),
+            pltpu.VMEM((2, span, 2 * PAIR), BF),
+            pltpu.VMEM((keys, 2 * PAIR), BF),
+            pltpu.VMEM((keys, 2 * PAIR), BF),
             pltpu.VMEM((PAIR, keys), BF),
             pltpu.VMEM((PAIR, span), F32),
             pltpu.VMEM((tk, PAIR), F32),
@@ -807,6 +839,187 @@
     )(a, b)
 
 
+def outers_kernel(steps, a1_ref, a2_ref, a3_ref, b1_ref, b2_ref, b3_ref, b4_ref, gains_ref, o1_ref, o2_ref, o3_ref, o4_ref):
+    now = pl.program_id(0)
+
+    @pl.when(now < steps)
+    def _():
+        o1_ref[...] = dot(a1_ref[...], b1_ref[...]).astype(BF)
+
+    @pl.when((now >= steps) & (now < 2 * steps))
+    def _():
+        o2_ref[...] = dot(a1_ref[...], b2_ref[...]).astype(BF)
+
+    @pl.when((now >= 2 * steps) & (now < 3 * steps))
+    def _():
+        o3_ref[...] = dot(a2_ref[...], b3_ref[...]).astype(BF)
+
+    @pl.when(now == 3 * steps)
+    def _():
+        width = b4_ref.shape[1]
+        o4_ref[:, :width] = dot(a3_ref[...], b4_ref[...])
+        o4_ref[:, width:] = gains_ref[...]
+
+
+def outers_call(h_t, df_t, att_t, d_gate, d_up, act, d_first, gains, tile=512):
+    width, tokens = h_t.shape
+    hidden = d_gate.shape[1]
+    steps = hidden // tile
+
+    def whole(a):
+        return pl.BlockSpec(a.shape, lambda i: (0, 0), pipeline_mode=pl.Buffered(1))
+
+    def part(rows, n):
+        return pl.BlockSpec((rows, tile), lambda i: (0, jnp.clip(i - n * steps, 0, steps - 1)))
+
+    return pl.pallas_call(
+        functools.partial(outers_kernel, steps),
+        grid=(3 * steps + 1,),
+        in_specs=[whole(h_t), whole(df_t), whole(att_t)]
+        + [part(tokens, n) for n in range(3)]
+        + [whole(d_first), whole(gains)],
+        out_specs=[part(width, n) for n in range(3)]
+        + [pl.BlockSpec((width, width + gains.shape[1]), lambda i: (0, 0), pipeline_mode=pl.Buffered(1))],
+        out_shape=[jax.ShapeDtypeStruct((width, hidden), BF)] * 3
+        + [jax.ShapeDtypeStruct((width, width + gains.shape[1]), F32)],
+        compiler_params=params(),
+        name="outers",
+    )(h_t, df_t, att_t, d_gate, d_up, act, d_first, gains)
+
+
+CLOSING_ORDERS = ("xy", "yx", "xy")
+
+
+def closing_kernel(
+    dq_hbm, dk_hbm, dv_hbm, first_hbm, xt_hbm, w_hbm, g_out, sum_ref,
+    dq, dk, dv, first, xt, w, g, w0, w1, w2, send, recv, local, mine_sem, *bufs,
+):
+    me = place()
+    y = me["y"]
+    loads = [
+        pltpu.make_async_copy(a, b, local.at[i])
+        for i, (a, b) in enumerate(
+            ((w_hbm, w), (dq_hbm, dq), (dk_hbm, dk), (dv_hbm, dv), (first_hbm, first), (xt_hbm, xt))
+        )
+    ]
+    for load in loads:
+        load.start()
+    greet(me)
+    width = dq.shape[1]
+    half = g.shape[1]
+    tile = half // 2
+
+    def rows_of(which, t):
+        at = pl.ds(pl.multiple_of(which * half + t * tile, tile), tile)
+        total = first[at, :].astype(F32)
+        for n, a in enumerate((dq, dk, dv)):
+            total += dot_nt(a[at, :], w[:, n * width : (n + 1) * width])
+        g[which, pl.ds(t * tile, tile), :] = total.astype(BF)
+
+    for load in loads[:5]:
+        load.wait()
+    gives = []
+    for t in range(2):
+        rows_of(1 - y, t)
+        part = pl.ds(t * tile, tile)
+        gives.append(
+            pltpu.make_async_remote_copy(
+                src_ref=g.at[1 - y, part],
+                dst_ref=g_out.at[y, part],
+                send_sem=send.at[t],
+                recv_sem=recv.at[t],
+                device_id=device(moved(me, "y", 1)),
+                device_id_type=MESH,
+            )
+        )
+        gives[-1].start()
+    for t in range(2):
+        rows_of(y, t)
+    keep = pltpu.make_async_copy(g.at[y], g_out.at[y], local.at[0])
+    keep.start()
+    loads[5].wait()
+    reduces = []
+    for n, (a, target) in enumerate(((dq, w0), (dk, w1), (dv, w2))):
+        reduces.append(
+            Reduce(
+                me, tall_piece(target), bufs[5 * n : 5 * n + 5], sum_ref.at[:, pl.ds(n * width, width)],
+                send, recv, mine_sem.at[pl.ds(2 * n, 2)], 2 + n * Reduce.SEMS, CLOSING_ORDERS[n],
+            )
+        )
+
+    def products(n, a, target):
+        step = 2 * PAIR
+
+        def part(i, _):
+            at = pl.ds(pl.multiple_of(i * step, step), step)
+            value = dot(xt[...], a[:, at])
+            target[:, :, :, :, :, at] = value.reshape(target.shape[:-1] + (step,)).astype(BF)
+            return 0
+
+        lax.fori_loop(0, width // step, part, 0)
+
+    products(0, dq, w0)
+    reduces[0].start()
+    products(1, dk, w1)
+    reduces[1].start()
+    reduces[0].step(1)
+    products(2, dv, w2)
+    reduces[2].start()
+    reduces[1].step(1)
+    reduces[0].step(2)
+    reduces[2].step(1)
+    reduces[1].step(2)
+    reduces[0].step(3)
+    reduces[2].step(2)
+    reduces[1].step(3)
+    reduces[0].step(4)
+    reduces[2].step(3)
+    reduces[1].step(4)
+    reduces[2].step(4)
+    for r in reduces:
+        r.finish()
+    for t in range(2):
+        part = pl.ds(t * tile, tile)
+        pltpu.make_async_remote_copy(
+            src_ref=g.at[1 - y, part],
+            dst_ref=g_out.at[1 - y, part],
+            send_sem=send.at[t],
+            recv_sem=recv.at[t],
+            device_id=device(moved(me, "y", 1)),
+            device_id_type=MESH,
+        ).wait_recv()
+        gives[t].wait_send()
+    keep.wait()
+
+
+def closing_call(dq, dk, dv, first, xt, w):
+    tokens, width = dq.shape
+    hbm = pl.BlockSpec(memory_space=pl.ANY)
+    block = (width // 32, width)
+    full = pltpu.VMEM((4, 2, 2, 2) + block, BF)
+    scratch = [pltpu.VMEM(a.shape, BF) for a in (dq, dk, dv, first, xt, w)]
+    scratch += [pltpu.VMEM((2, tokens // 2, width), BF), full, full, full]
+    sems = 2 + 3 * Reduce.SEMS
+    scratch += [pltpu.SemaphoreType.DMA((sems,))] * 2
+    scratch += [pltpu.SemaphoreType.DMA((6,)), pltpu.SemaphoreType.DMA((6,))]
+    for order in CLOSING_ORDERS:
+        scratch += Reduce.scratch(*block, BF, order)
+    return pl.pallas_call(
+        closing_kernel,
+        in_specs=[hbm] * 6,
+        out_specs=[hbm, pl.BlockSpec(memory_space=pltpu.VMEM)],
+        out_shape=[
+            jax.ShapeDtypeStruct((2, tokens // 2, width), BF),
+            jax.ShapeDtypeStruct((block[0], 3 * width), F32),
+        ],
+        scratch_shapes=scratch,
+        compiler_params=pltpu.CompilerParams(
+            vmem_limit_bytes=VMEM_LIMIT, collective_id=3, has_side_effects=True
+        ),
+        name="closing",
+    )(dq, dk, dv, first, xt, w)
+
+
 def tokens_kernel(dq_ref, dk_ref, dv_ref, dfirst_ref, w_ref, o_ref):
     width = dq_ref.shape[1]
     total = dfirst_ref[...].astype(F32)
@@ -842,15 +1055,6 @@
     )
 
 
-def swap(a, mine):
-    keep = lax.dynamic_index_in_dim(a, mine, 0, keepdims=False)
-    give = lax.dynamic_index_in_dim(a, 1 - mine, 0, keepdims=False)
-    got = lax.ppermute(give, "blk", [(0, 1), (1, 0)])
-    low = jnp.where(mine == 0, keep, got)
-    high = jnp.where(mine == 0, got, keep)
-    return jnp.stack([low, high])
-
-
 def body(tokens, lengths, w_qkv, w_out, w_gate, w_up, w_down, gain_one, gain_two, cotangent):
     axes = ("dp", "blk")
     blk = lax.axis_size("blk")
@@ -865,7 +1069,8 @@
     cosine, sine = map(jnp.asarray, angle_tables(seq))
     gains = jnp.stack([gain_one, gain_two], 1)
     if own:
-        x, f_qkv = opening_call(tokens, w_qkv)
+        w_out = jnp.pad(jnp.concatenate([w_out, gains], 1), ((0, 0), (0, PAIR - 2)))
+        x, f_qkv, w_out, w_gate, w_up = opening_call(tokens, w_qkv, (w_out, w_gate, w_up))
         x = x.reshape(1, seq, width)
         f_qkv = f_qkv.reshape(width, -1)
         length = lax.dynamic_slice_in_dim(lengths, mine, 1, 0)
@@ -885,9 +1090,8 @@
         v = lax.all_gather(v, "blk", axis=1, tiled=True)
     position = jnp.arange(seq, dtype=jnp.int32)[None, :, None]
     lane = jnp.arange(PAIR, dtype=jnp.int32)[None, None, :]
-    bias = jnp.where((lane == 3) & (position >= length[:, None, None]), NEG, 0.0).astype(BF)
+    bias = jnp.where((lane % HEAD == 3) & (position >= length[:, None, None]), NEG, 0.0).astype(BF)
     if own:
-        w_out = jnp.pad(jnp.concatenate([w_out, gains], 1), ((0, 0), (0, PAIR - 2)))
         att, aug, cot, f_out, f_gate, f_up, f_down = attend_call(
             q, k, v, bias, (cotangent, w_out, w_gate, w_up, w_down)
         )
@@ -901,12 +1105,8 @@
     out, d_first, d_att, act, d_gate, d_up, h_t, df_t, att_t, gg1, gg2 = middle_call(
         flat, att.reshape(n * t, width), cot.reshape(n * t, width), f_out, f_gate, f_up, f_down, g1, g2
     )
-    gw_gate = outer_call(h_t, d_gate, BF)
-    gw_up = outer_call(h_t, d_up, BF)
-    gw_down_t = outer_call(df_t, act, BF)
-    gw_out = outer_call(att_t, d_first, F32)
     gains = jnp.pad(jnp.concatenate([gg1, gg2]).T, ((0, 0), (0, PAIR - 2)))
-    gw_out = jnp.concatenate([gw_out, gains], 1)
+    gw_gate, gw_up, gw_down_t, gw_out = outers_call(h_t, df_t, att_t, d_gate, d_up, act, d_first, gains)
     d_att = d_att.reshape(n, t, width)
     if own:
         wide = tuple(g.reshape(4, 2, 2, width // 16, -1) for g in (gw_gate, gw_up, gw_down_t))
@@ -932,14 +1132,13 @@
     s_down = s_down_t.T
     s_out, s_gg = s_out[:, :width], s_out[:, width : width + 2]
     dq, dk, dv = (a.reshape(n * t, width) for a in (dq, dk, dv))
-    gw_qkv = jnp.concatenate([outer_call(xt, a, BF, 256) for a in (dq, dk, dv)], 1)
-    g_tokens = tokens_call(dq, dk, dv, d_first, f_qkv)
-    s_qkv = lax.psum_scatter(gw_qkv, axes, scatter_dimension=0, tiled=True).astype(F32)
     if own:
-        g_tokens = swap(g_tokens.reshape(2, span, width), mine)
+        g_tokens, s_qkv = closing_call(dq, dk, dv, d_first, xt, f_qkv)
     else:
+        gw_qkv = jnp.concatenate([outer_call(xt, a, BF, 256) for a in (dq, dk, dv)], 1)
+        s_qkv = lax.psum_scatter(gw_qkv, axes, scatter_dimension=0, tiled=True).astype(F32)
+        g_tokens = tokens_call(dq, dk, dv, d_first, f_qkv).reshape(tokens.shape)
         out = out.reshape(tokens.shape)
-        g_tokens = g_tokens.reshape(tokens.shape)
     return (out, g_tokens, s_qkv, s_out, s_gate, s_up, s_down, s_gg[:, 0], s_gg[:, 1])
 
 

time: 688 us -> 578 us (0.84)
  waiting for transfers between devices: 79.8 us -> 0 us
  between operations: 14.2 us -> 1.19 us
  Pallas kernels: 562 us -> 549 us
  other arithmetic: 15.7 us -> 4.94 us
    reduce_scatter x1 -> x0, waiting for transfers between devices: 50.5 us -> none  [body(): lax.psum_scatter(gw_qkv, axes, scatter_dimension=0, tiled=True).astype(F32)]
    pallas_call x9 -> x3, Pallas kernels: 139 us -> 179 us  [the longest x1 67.9 us: opening_call(): pl.pallas_call(opening_kernel, in_specs=[hbm] * 5, out_specs=[hbm] * 5, o...]
    pallas_call x1, Pallas kernels: 192 us -> 160 us  [attend_back_call(): pl.pallas_call(functools.partial(attend_back_kernel, tk, tq, moves), grid...]
    ppermute x1 -> x0, waiting for transfers between devices: 29.4 us -> none  [swap(): got = lax.ppermute(give, 'blk', [(0, 1), (1, 0)])]
    pallas_call x1, Pallas kernels: 123 us -> 104 us  [attend_call(): pl.pallas_call(functools.partial(attend_kernel, tile, chunk, moves), grid...]
  transfers between devices with their start and end apart: 2 -> 0, of which waited for: 2 -> 0; matrix products, arithmetic and copies ran while one was open for 1% -> 0% of each run, Pallas kernels for 2% -> 0%
where the time goes in v4:
time: 578 us; the launch traced here: 572 us
  Pallas kernels  549 us (95%)
  local copies, waits for them, and re-layouts  16.5 us (3%)
    pallas_call x1, Pallas kernels, attend_back_call(): pl.pallas_call(functools.partial(attend_back_kernel, tk, tq, moves), grid...  160 us
    pallas_call x1, Pallas kernels, attend_call(): pl.pallas_call(functools.partial(attend_kernel, tile, chunk, moves), grid...  104 us
    pallas_call x1, Pallas kernels, middle_call(): pl.pallas_call(functools.partial(middle_kernel, chunk), grid=(tokens // t...  93.2 us
    pallas_call x1, Pallas kernels, opening_call(): pl.pallas_call(opening_kernel, in_specs=[hbm] * 5, out_specs=[hbm] * 5, o...  67.9 us
    pallas_call x1, Pallas kernels, closing_call(): pl.pallas_call(closing_kernel, in_specs=[hbm] * 6, out_specs=[hbm, pl.Blo...  65.3 us
    pallas_call x1, Pallas kernels, outers_call(): pl.pallas_call(functools.partial(outers_kernel, steps), grid=(3 * steps +...  45.6 us
    pallas_call x1, Pallas kernels, qkv_call(): pl.pallas_call(qkv_kernel, grid=(tokens // tile,), in_specs=[row, pl.Bloc...  13.3 us

profile of v4, /device:TPU:0, one launch (start us, length us, event | category | flops | bytes accessed | tf_op | source)
XLA Modules:
  0.0 571.9 jit_solution(6503861752981646285)
XLA Ops:
  0.6 1.2 dynamic_slice.3
  1.9 0.7 iota_compare_fusion.1
  2.6 0.7 copy.29
  3.3 0.7 copy.30
  4.0 1.5 fusion.4.rest_0_
  5.5 1.2 select_convert_fusion.bias_ref
  6.7 67.9 %opening.1 = (bf16[2,1024,768]{2,1,0:T(8,128)(2,1)}, bf16[4,2,2,2,24,2304]{5,4,3,2,1,0:T(8,128)(2,1)}, bf16[4,24,896]{2,1,0:T(8,128)(2,1)}, bf16[4,24,3072]{2,1,0:T(8,128)(2,1)}, bf16[4,24,3072]{2,1,0:T(8,128)(2,1)}) custom-call(bf16[2,1024,768]{2,1,0:T(8,128)(2,1)} %tok_ref.1, bf16[24,2304]{1,0:T(8,128)(2,1)} %qkv_ref.1, bf16[24,896]{1,0:T(8,128)(2,1)} %fusion.4.rest_0_, ...), custom_call_target="tpu_custom_call" | custom-call | tf_op jit(solution)/shard_map/opening/pallas_call | solution.py:315
  74.5 13.3 %qkv.1 = (bf16[2048,768]{1,0:T(8,128)(2,1)}, bf16[2048,768]{1,0:T(8,128)(2,1)}, bf16[2048,768]{1,0:T(8,128)(2,1)}, bf16[768,2048]{1,0:T(8,128)(2,1)}) custom-call(bf16[2048,768]{1,0:T(8,128)(2,1)} %bitcast.34, bf16[768,2304]{1,0:T(8,128)(2,1)} %bitcast.25, f32[2048,128]{1,0:T(8,128)} %constant.36.clone.cos_ref, f32[2048,128]{1,0:T(8,128)} %constant.37.clone.sin_ref), custom_call_target="tpu_custom_call" | custom-call | tf_op jit(solution)/shard_map/qkv/pallas_call | solution.py:358
  87.8 104.4 %attend.1 = (bf16[1,2048,768]{2,1,0:T(8,128)(2,1)}, bf16[1,2048,768]{2,1,0:T(8,128)(2,1)}, bf16[2,1024,768]{2,1,0:T(8,128)(2,1)}, bf16[4,2,2,2,24,896]{5,4,3,2,1...) custom-call(bf16[1,2048,768]{2,1,0:T(8,128)(2,1)} %bitcast.27, ...), custom_call_target="tpu_custom_call" | custom-call | tf_op jit(solution)/shard_map/attend/pallas_call | solution.py:527
  192.3 1.0 slice_convert_fusion
  193.2 0.4 slice_reduce_fusion
  193.6 2.4 slice.31.wo_ref
  196.0 0.6 broadcast_in_dim_squeeze.7.g2_ref
  196.6 0.6 broadcast_in_dim_squeeze.6.g1_ref
  197.1 93.2 %middle.1 = (bf16[2048,768]{1,0:T(8,128)(2,1)}, bf16[2048,768]{1,0:T(8,128)(2,1)}, bf16[2048,768]{1,0:T(8,128)(2,1)}, bf16[2048,3072]{1,0:T(8,128)(2,1)}, bf16[2...) custom-call(bf16[2048,768]{1,0:T(8,128)(2,1)} %bitcast.35, ...), custom_call_target="tpu_custom_call" | custom-call | tf_op jit(solution)/shard_map/middle/pallas_call | solution.py:805
  290.4 0.7 pad_maximum_fusion
  291.1 0.2 copy.31
  291.3 0.8 pad.9.gains_ref
  292.1 45.6 %outers.1 = (bf16[768,3072]{1,0:T(8,128)(2,1)}, bf16[768,3072]{1,0:T(8,128)(2,1)}, bf16[768,3072]{1,0:T(8,128)(2,1)}, f32[768,896]{1,0:T(8,128)}) custom-call(bf16[768,2048]{1,0:T(8,128)(2,1)} %get-tuple-element.67.a1_ref, bf16[768,2048]{1,0:T(8,128)(2,1)} %get-tuple-element.68.a2_ref, bf16[768,2048]{1,0:T(8,128)(2,1)} %get-tuple-element.69.a3_ref, ...), custom_call_target="tpu_custom_call" | custom-call | tf_op jit(solution)/shard_map/outers/pallas_call | solution.py:875
  337.7 159.6 %attend_back.1 = (bf16[1,2048,768]{2,1,0:T(8,128)(2,1)}, bf16[1,2048,768]{2,1,0:T(8,128)(2,1)}, bf16[1,2048,768]{2,1,0:T(8,128)(2,1)}, bf16[2,1024,768]{2,1,0:T(...) custom-call(bf16[1,2048,768]{2,1,0:T(8,128)(2,1)} %bitcast.28, ...), custom_call_target="tpu_custom_call" | custom-call | tf_op jit(solution)/shard_map/attend_back/pallas_call | solution.py:699
  497.3 65.3 %closing.1 = (bf16[2,1024,768]{2,1,0:T(8,128)(2,1)}, f32[24,2304]{1,0:T(8,128)}) custom-call(bf16[2048,768]{1,0:T(8,128)(2,1)} %bitcast.44, bf16[2048,768]{1,0:T(8,128)(2,1)} %bitcast.45, bf16[2048,768]{1,0:T(8,128)(2,1)} %bitcast.46, bf16[2048,768]{1,0:T(8,128)(2,1)} %get-tuple-element.73.b4_ref.first_hbm, bf16[768,2048]{1,0:T(8,128)(2,1)} %get-tuple-element.84.xt_hbm, ...), custom_call_target="tpu_custom_call" | custom-call | tf_op jit(solution)/shard_map/closing/pallas_call | solution.py:1007
  562.6 0.7 slice_reduce_fusion.2
  563.3 0.6 slice.28
  563.9 1.7 copy.38
  565.6 1.4 copy-done.1
  567.0 1.7 copy.39
  568.6 0.0 copy-done.5
  568.6 0.7 copy.40
  569.3 0.0 copy-done.4
  569.3 0.7 copy.41
  570.0 0.7 copy.42
  570.8 0.7 copy.43
  (12 shorter events, 0.0 us)
Async XLA Ops:
  497.3 65.3 %copy-start.6 = (f32[24,896]{1,0:T(8,128)S(1)}, f32[24,896]{1,0:T(8,128)}, u32[]{:S(2)}) copy-start(f32[24,896]{1,0:T(8,128)} %get-tuple-element.87) | copy-start | bytes 258052
  497.3 66.6 %copy-start = (bf16[2,1024,768]{2,1,0:T(8,128)(2,1)S(1)}, bf16[2,1024,768]{2,1,0:T(8,128)(2,1)}, u32[]{:S(2)}) copy-start(bf16[2,1024,768]{2,1,0:T(8,128)(2,1)} %get-tuple-element.104) | copy-start | bytes 9437188
  563.9 3.0 copy-start.1
  567.0 1.7 copy-start.5
  567.0 2.4 copy-start.4
  567.0 3.1 copy-start.3
  567.0 3.8 copy-start.2

commit v5 on v4

--- a/solution.py
+++ b/solution.py
@@ -242,27 +242,46 @@
         ]
 
 
-def swap_copies(me, source, target, send, recv, local, slot):
-    other = moved(me, "y", 1)
-    y = me["y"]
-    keep = pltpu.make_async_copy(source.at[y], target.at[y], local)
-    give = pltpu.make_async_remote_copy(
-        src_ref=source.at[1 - y],
-        dst_ref=target.at[y],
-        send_sem=send.at[slot],
-        recv_sem=recv.at[slot],
-        device_id=device(other),
-        device_id_type=MESH,
-    )
-    take = pltpu.make_async_remote_copy(
-        src_ref=target.at[1 - y],
-        dst_ref=target.at[1 - y],
-        send_sem=send.at[slot],
-        recv_sem=recv.at[slot],
-        device_id=device(other),
-        device_id_type=MESH,
-    )
-    return keep, give, take
+class Swap:
+    def __init__(self, me, source, target, bounce, send, recv, local, slots, parts):
+        self.me, self.source, self.target, self.bounce = me, source, target, bounce
+        self.send, self.recv, self.local, self.slots, self.parts = send, recv, local, slots, parts
+
+    def copy(self, n, row, half):
+        begin, size = self.parts[n]
+        part = pl.ds(begin, size)
+        return pltpu.make_async_remote_copy(
+            src_ref=self.source.at[row, part],
+            dst_ref=self.target.at[half, part],
+            send_sem=self.send.at[self.slots + n],
+            recv_sem=self.recv.at[self.slots + n],
+            device_id=device(moved(self.me, "y", 1)),
+            device_id_type=MESH,
+        )
+
+    def give(self, n):
+        y = self.me["y"]
+        self.copy(n, 1 - y, y).start()
+
+    def keep_in(self):
+        return pltpu.make_async_copy(self.source.at[self.me["y"]], self.bounce, self.local)
+
+    def keep_out(self):
+        return pltpu.make_async_copy(self.bounce, self.target.at[self.me["y"]], self.local)
+
+    def keep_begin(self):
+        self.keep_in().start()
+
+    def keep_turn(self):
+        self.keep_in().wait()
+        self.keep_out().start()
+
+    def finish(self):
+        y = self.me["y"]
+        for n in range(len(self.parts)):
+            self.copy(n, 1 - y, 1 - y).wait_recv()
+            self.copy(n, 1 - y, y).wait_send()
+        self.keep_out().wait()
 
 
 OPENING_ORDERS = ("yzxc", "zyxc", "z", "z", "z")
@@ -271,14 +290,15 @@
 def opening_kernel(tok_ref, qkv_ref, *rest):
     early, rest = rest[:3], rest[3:]
     x_ref, full_ref, rest = rest[0], rest[1], rest[2:]
-    early_out, (send, recv, local) = rest[:3], rest[3:]
+    early_out, (bounce, send, recv, local) = rest[:3], rest[3:]
     me = place()
     greet(me)
-    keep, give, take = swap_copies(me, tok_ref, x_ref, send, recv, local.at[0], 0)
+    rows = tok_ref.shape[1]
+    swap = Swap(me, tok_ref, x_ref, bounce, send, recv, local.at[0], 0, ((0, rows // 8), (rows // 8, rows - rows // 8)))
     half = qkv_ref.shape[-1] // 2
     sources = [(qkv_ref, full_ref, (0, half)), (qkv_ref, full_ref, (half, half))]
     sources += [(a, b, None) for a, b in zip(early, early_out)]
-    gathers, base = [], 1
+    gathers, base = [], 2
     for i, (source, full, columns) in enumerate(sources):
         order = OPENING_ORDERS[i]
         gathers.append(
@@ -288,10 +308,12 @@
     first, second, later = gathers[0], gathers[1], gathers[2:]
     first.start()
     second.start()
-    give.start()
-    keep.start()
+    swap.give(0)
+    swap.keep_begin()
     first.step(1)
     second.step(1)
+    swap.give(1)
+    swap.keep_turn()
     first.step(2)
     for g in later:
         g.start()
@@ -304,17 +326,15 @@
         g.step(1)
     for g in gathers:
         g.finish()
-    take.wait_recv()
-    give.wait_send()
-    keep.wait()
+    swap.finish()
 
 
 def opening_call(tokens, w_qkv, early):
     hbm = pl.BlockSpec(memory_space=pl.ANY)
-    sems = 1 + sum(map(Gather.sems, OPENING_ORDERS))
+    sems = 2 + sum(map(Gather.sems, OPENING_ORDERS))
     return pl.pallas_call(
         opening_kernel,
-        in_specs=[hbm] * 5,
+        in_specs=[hbm] + [pl.BlockSpec(memory_space=pltpu.VMEM)] * 4,
         out_specs=[hbm] * 5,
         out_shape=[
             jax.ShapeDtypeStruct(tokens.shape, BF),
@@ -322,11 +342,14 @@
         ]
         + [jax.ShapeDtypeStruct((4,) + a.shape, BF) for a in early],
         scratch_shapes=[
+            pltpu.VMEM(tokens.shape[1:], BF),
             pltpu.SemaphoreType.DMA((sems,)),
             pltpu.SemaphoreType.DMA((sems,)),
             pltpu.SemaphoreType.DMA((6,)),
         ],
-        compiler_params=pltpu.CompilerParams(collective_id=0, has_side_effects=True),
+        compiler_params=pltpu.CompilerParams(
+            vmem_limit_bytes=VMEM_LIMIT, collective_id=0, has_side_effects=True
+        ),
         name="opening",
     )(tokens, w_qkv, *early)
 
@@ -467,16 +490,17 @@
         self.setdefault(at, []).extend(acts)
 
 
-ATTEND_ORDERS = ("xyc", "xyc", "yxc", "yzxc")
+ATTEND_ORDERS = ("yxc", "xyc", "yxc", "yzxc")
 ATTEND_PLAN = (
-    (3, 3, 1), (7, 1, 1), (7, 2, 1), (8, 0, 1), (13, 3, 2), (16, 0, 2), (17, 1, 2), (18, 2, 2),
+    (3, 3, 1), (4, 0, 1), (6, 1, 1), (8, 2, 1), (9, 0, 2), (12, 3, 2), (17, 1, 2), (18, 2, 2),
 )
-ATTEND_SWAP = 9
-
-
-def attend_events(inputs, outputs, send, recv, local):
+ATTEND_SWAP = 8
+
+
+def attend_events(inputs, outputs, bounce, send, recv, local):
     me = place()
-    keep, give, take = swap_copies(me, inputs[0], outputs[0], send, recv, local.at[0], 0)
+    rows = inputs[0].shape[1]
+    swap = Swap(me, inputs[0], outputs[0], bounce, send, recv, local.at[0], 0, ((0, rows),))
     gathers, base = [], 1
     for i, (shard, full) in enumerate(zip(inputs[1:], outputs[1:])):
         held = "z" if i < 3 else ""
@@ -485,17 +509,18 @@
         )
         base += Gather.sems(ATTEND_ORDERS[i])
     events = Events()
-    events.put(0, functools.partial(greet, me), *(gathers[i].start for i in (3, 1, 2, 0)))
-    events.put(ATTEND_SWAP, give.start, keep.start)
+    events.put(0, functools.partial(greet, me), *(gathers[i].start for i in (3, 0, 2, 1)))
     done = [1] * len(gathers)
     for at, i, stage in ATTEND_PLAN:
         events.put(at, functools.partial(gathers[i].step, stage))
         done[i] = stage + 1
+    events.put(ATTEND_SWAP, functools.partial(swap.give, 0), swap.keep_begin)
+    events.put(ATTEND_SWAP + 3, swap.keep_turn)
     for stage in range(1, 5):
         for i, g in enumerate(gathers):
             if done[i] <= stage <= len(ATTEND_ORDERS[i]):
                 events.last.append(functools.partial(g.step, stage))
-    events.last += [g.finish for g in gathers] + [take.wait_recv, give.wait_send, keep.wait]
+    events.last += [g.finish for g in gathers] + [swap.finish]
     return events
 
 
@@ -522,12 +547,19 @@
         jax.ShapeDtypeStruct((4, 2, 2, 2) + a.shape[-2:], a.dtype) for a in moving[1:]
     ]
     sems = 1 + sum(map(Gather.sems, ATTEND_ORDERS))
-    extra = [pltpu.SemaphoreType.DMA((sems,))] * 2 + [pltpu.SemaphoreType.DMA((moves,))]
+    extra = [pltpu.VMEM(moving[0].shape[1:], BF)] if moves else []
+    extra += [pltpu.SemaphoreType.DMA((sems,))] * 2 + [pltpu.SemaphoreType.DMA((moves,))]
+    held = [
+        pl.BlockSpec(a.shape, lambda r, p, n=a.ndim: (0,) * n, pipeline_mode=pl.Buffered(1))
+        for a in moving[1:]
+    ]
     more = dict(collective_id=1, has_side_effects=True) if moves else {}
     return pl.pallas_call(
         functools.partial(attend_kernel, tile, chunk, moves),
         grid=(rows, width // PAIR),
-        in_specs=[qs, ks, ks, pl.BlockSpec((1, keys, PAIR), lambda r, p: (r, 0, 0))] + [hbm] * moves,
+        in_specs=[qs, ks, ks, pl.BlockSpec((1, keys, PAIR), lambda r, p: (r, 0, 0))]
+        + [hbm] * min(moves, 1)
+        + held,
         out_specs=[qs, qs] + [hbm] * moves,
         out_shape=[jax.ShapeDtypeStruct(q.shape, BF)] * 2 + moved_shapes,
         scratch_shapes=[
@@ -543,17 +575,17 @@
 
 
 def attend_back_kernel(
-    tk, tq, moves, q_ref, k_ref, v_ref, bias_ref, o_ref, do_ref, aug_ref, cos_ref, sin_ref, *rest
+    tq, moves, q_ref, k_ref, v_ref, bias_ref, o_ref, do_ref, aug_ref, cos_ref, sin_ref, *rest
 ):
     inputs, rest = rest[:moves], rest[moves:]
     dq_ref, dk_ref, dv_ref, rest = rest[0], rest[1], rest[2], rest[3:]
     outputs, rest = rest[:moves], rest[moves:]
-    qa, da, ka, va, kt, dqt, dk_acc, dv_acc = rest[:8]
+    qa, da, ka, va, kt, dk_acc, dv_acc = rest[:7]
     keys, span = k_ref.shape[1], q_ref.shape[1]
-    nq, nk = span // tq, keys // tk
+    tiles = span // tq
     events = {}
     if moves:
-        events = back_events(inputs, outputs, *rest[8:])
+        events = back_events(inputs, outputs, *rest[7:])
 
     @pl.when(pl.program_id(1) == 0)
     def _():
@@ -579,10 +611,11 @@
     for h in range(2):
         qa[h] = jnp.where(side == h, q_both, jnp.zeros_like(q_both))
         da[h] = jnp.where(side == h, d_both, jnp.zeros_like(d_both))
-    dqt[...] = jnp.zeros_like(dqt)
-
-    def key_step(j, _):
-        now = pl.program_id(1) * nk + j
+    dk_acc[...] = jnp.zeros_like(dk_acc)
+    dv_acc[...] = jnp.zeros_like(dv_acc)
+
+    def query_step(i, _):
+        now = pl.program_id(1) * tiles + i
         for at_step, acts in events.items():
 
             @pl.when(now == at_step)
@@ -590,39 +623,30 @@
                 for act in acts:
                     act()
 
-        at_k = pl.ds(pl.multiple_of(j * tk, tk), tk)
-        dk_acc[...] = jnp.zeros_like(dk_acc)
-        dv_acc[...] = jnp.zeros_like(dv_acc)
-
-        def query_step(i, _):
-            at_q = pl.ds(pl.multiple_of(i * tq, tq), tq)
-            dv, dk = None, None
-            for h in range(2):
-                st = dot_nt(ka[at_k, :], qa[h, at_q, :])
-                dpt = dot_nt(va[at_k, :], da[h, at_q, :])
-                p = jnp.exp2(st)
-                ds = (p * dpt).astype(BF)
-                pv = dot(p.astype(BF), da[h, at_q, :PAIR])
-                pk = dot(ds, qa[h, at_q, :PAIR])
-                dv = pv if dv is None else dv + pv
-                dk = pk if dk is None else dk + pk
-                head = slice(h * HEAD, (h + 1) * HEAD)
-                dqt[head, at_q] += dot(kt[head, at_k], ds)
-            dv_acc[...] += dv
-            dk_acc[...] += dk
-            return 0
-
-        lax.fori_loop(0, nq, query_step, 0, unroll=True)
-        dv_ref[0, at_k, :] = dv_acc[...].astype(dv_ref.dtype)
-        g = dk_acc[...] * LN2
-        if dk_ref.dtype == BF:
-            g = back_turn(g, cos_ref[at_k, :], sin_ref[at_k, :])
-        dk_ref[0, at_k, :] = g.astype(dk_ref.dtype)
+        at_q = pl.ds(pl.multiple_of(i * tq, tq), tq)
+        dv, dk, dq = None, None, []
+        for h in range(2):
+            st = dot_nt(ka[...], qa[h, at_q, :])
+            dpt = dot_nt(va[...], da[h, at_q, :])
+            p = jnp.exp2(st)
+            ds = (p * dpt).astype(BF)
+            pv = dot(p.astype(BF), da[h, at_q, :PAIR])
+            pk = dot(ds, qa[h, at_q, :PAIR])
+            dv = pv if dv is None else dv + pv
+            dk = pk if dk is None else dk + pk
+            dq.append(dot(kt[h * HEAD : (h + 1) * HEAD, :], ds))
+        dv_acc[...] += dv
+        dk_acc[...] += dk
+        g = jnp.concatenate(dq, axis=0).T * 0.125
+        dq_ref[0, at_q, :] = back_turn(g, cos_ref[at_q, :], sin_ref[at_q, :]).astype(BF)
         return 0
 
-    lax.fori_loop(0, nk, key_step, 0)
-    g = dqt[...].T * 0.125
-    dq_ref[0] = back_turn(g, cos_ref[...], sin_ref[...]).astype(BF)
+    lax.fori_loop(0, tiles, query_step, 0)
+    dv_ref[0] = dv_acc[...].astype(dv_ref.dtype)
+    g = dk_acc[...] * LN2
+    if dk_ref.dtype == BF:
+        g = back_turn(g, cos_ref[...], sin_ref[...])
+    dk_ref[0] = g.astype(dk_ref.dtype)
     if moves:
 
         @pl.when(pl.program_id(1) == pl.num_programs(1) - 1)
@@ -645,39 +669,34 @@
 
 BACK_ORDERS = ("yx", "yx", "xy", "xy")
 BACK_PLAN = (
-    (1, 0, 1), (1, 2, 1), (4, 0, 2), (4, 1, 1), (5, 3, 1), (5, 0, 3), (7, 1, 2), (7, 2, 2),
-    (8, 3, 2), (9, 1, 3), (9, 2, 3), (10, 3, 3),
+    (2, 0, 1), (2, 2, 1), (3, 1, 1), (3, 3, 1), (7, 0, 2), (7, 2, 2), (10, 3, 2), (12, 0, 3), (12, 1, 2),
+    (14, 2, 3), (15, 1, 3), (16, 3, 3), (18, 0, 4), (19, 2, 4), (20, 1, 4), (21, 3, 4),
 )
-BACK_SWAP = 8
 
 
 def back_events(inputs, outputs, send, recv, local, *bufs):
     me = place()
-    keep, give, take = swap_copies(me, inputs[0], outputs[0], send, recv, local.at[0], 0)
     reduces = []
-    for i, (source, out) in enumerate(zip(inputs[1:], outputs[1:])):
+    for i, (source, out) in enumerate(zip(inputs, outputs)):
         piece = wide_piece(source, source.shape[-1] // 2) if len(source.shape) == 5 else tall_piece(source)
         reduces.append(
             Reduce(
                 me, piece, bufs[5 * i : 5 * i + 5], out, send, recv,
-                local.at[pl.ds(1 + 2 * i, 2)], 1 + i * Reduce.SEMS, BACK_ORDERS[i],
+                local.at[pl.ds(2 * i, 2)], i * Reduce.SEMS, BACK_ORDERS[i],
             )
         )
     events = Events()
     events.put(0, functools.partial(greet, me), *(reduces[i].start for i in (0, 2, 1, 3)))
     for at, i, stage in BACK_PLAN:
         events.put(at, functools.partial(reduces[i].step, stage))
-    events.put(BACK_SWAP, give.start, keep.start)
-    events.last += [functools.partial(r.step, 4) for r in reduces] + [r.finish for r in reduces]
-    events.last += [take.wait_recv, give.wait_send, keep.wait]
+    events.last += [r.finish for r in reduces]
     return events
 
 
-def attend_back_call(q, k, v, bias, o, do, aug, cosine, sine, whole, moving=(), tk=1024, tq=512):
+def attend_back_call(q, k, v, bias, o, do, aug, cosine, sine, whole, moving=(), tq=512):
     rows, span, width = q.shape
     keys = k.shape[1]
     tq = min(tq, span)
-    tk = min(tk, keys)
     moves = len(moving)
     qs = pl.BlockSpec((1, span, PAIR), lambda r, p: (r, 0, p))
     ks = pl.BlockSpec((1, keys, PAIR), lambda r, p: (r, 0, p))
@@ -686,21 +705,21 @@
     kv_type = BF if whole else F32
     results, result_specs, extra, more = [], [], [], {}
     if moves:
-        results.append(jax.ShapeDtypeStruct(moving[0].shape, BF))
-        result_specs.append(hbm)
-        sems = 1 + Reduce.SEMS * (moves - 1)
-        extra = [pltpu.SemaphoreType.DMA((sems,))] * 2 + [pltpu.SemaphoreType.DMA((2 * moves - 1,))]
-        for a, order in zip(moving[1:], BACK_ORDERS):
+        extra = [pltpu.SemaphoreType.DMA((Reduce.SEMS * moves,))] * 2
+        extra += [pltpu.SemaphoreType.DMA((2 * moves,))]
+        for a, order in zip(moving, BACK_ORDERS):
             block = (a.shape[-2], a.shape[-1] // (2 if a.ndim == 5 else 1))
             results.append(jax.ShapeDtypeStruct(block, F32))
-            result_specs.append(pl.BlockSpec(block, lambda r, p: (0, 0)))
+            result_specs.append(pl.BlockSpec(block, lambda r, p: (0, 0), pipeline_mode=pl.Buffered(1)))
             extra += Reduce.scratch(*block, a.dtype, order)
         more = dict(collective_id=2, has_side_effects=True)
     return pl.pallas_call(
-        functools.partial(attend_back_kernel, tk, tq, moves),
+        functools.partial(attend_back_kernel, tq, moves),
         grid=(rows, width // PAIR),
         in_specs=[
-            qs, ks, ks, pl.BlockSpec((1, keys, PAIR), lambda r, p: (r, 0, 0)), qs, qs, qs, table, table,
+            qs, ks, ks,
+            pl.BlockSpec((1, keys, PAIR), lambda r, p: (r, 0, 0), pipeline_mode=pl.Buffered(1)),
+            qs, qs, qs, table, table,
         ]
         + [hbm] * moves,
         out_specs=[qs, ks, ks] + result_specs,
@@ -716,9 +735,8 @@
             pltpu.VMEM((keys, 2 * PAIR), BF),
             pltpu.VMEM((keys, 2 * PAIR), BF),
             pltpu.VMEM((PAIR, keys), BF),
-            pltpu.VMEM((PAIR, span), F32),
-            pltpu.VMEM((tk, PAIR), F32),
-            pltpu.VMEM((tk, PAIR), F32),
+            pltpu.VMEM((keys, PAIR), F32),
+            pltpu.VMEM((keys, PAIR), F32),
         ]
         + extra,
         compiler_params=pltpu.CompilerParams(vmem_limit_bytes=VMEM_LIMIT, **more),
@@ -839,8 +857,23 @@
     )(a, b)
 
 
-def outers_kernel(steps, a1_ref, a2_ref, a3_ref, b1_ref, b2_ref, b3_ref, b4_ref, gains_ref, o1_ref, o2_ref, o3_ref, o4_ref):
+def outers_kernel(steps, moves, a1_ref, a2_ref, a3_ref, b1_ref, b2_ref, b3_ref, b4_ref, gains_ref, *rest):
+    source, rest = rest[:moves], rest[moves:]
+    o1_ref, o2_ref, o3_ref, o4_ref, rest = rest[0], rest[1], rest[2], rest[3], rest[4:]
     now = pl.program_id(0)
+    if moves:
+        target, bounce, send, recv, local = rest
+        me = place()
+        swap = Swap(me, source[0], target, bounce, send, recv, local.at[0], 0, ((0, target.shape[1]),))
+
+        @pl.when(now == 0)
+        def _():
+            greet(me)
+            swap.give(0)
+            swap.keep_begin()
+
+        pl.when(now == 3)(swap.keep_turn)
+        pl.when(now == 3 * steps)(swap.finish)
 
     @pl.when(now < steps)
     def _():
@@ -861,7 +894,7 @@
         o4_ref[:, width:] = gains_ref[...]
 
 
-def outers_call(h_t, df_t, att_t, d_gate, d_up, act, d_first, gains, tile=512):
+def outers_call(h_t, df_t, att_t, d_gate, d_up, act, d_first, gains, moving=(), tile=512):
     width, tokens = h_t.shape
     hidden = d_gate.shape[1]
     steps = hidden // tile
@@ -872,22 +905,31 @@
     def part(rows, n):
         return pl.BlockSpec((rows, tile), lambda i: (0, jnp.clip(i - n * steps, 0, steps - 1)))
 
+    moves = len(moving)
+    hbm = pl.BlockSpec(memory_space=pl.ANY)
+    extra = [pltpu.VMEM(a.shape[1:], BF) for a in moving]
+    extra += [pltpu.SemaphoreType.DMA((1,))] * (3 * moves)
+    more = dict(collective_id=4, has_side_effects=True) if moves else {}
     return pl.pallas_call(
-        functools.partial(outers_kernel, steps),
+        functools.partial(outers_kernel, steps, moves),
         grid=(3 * steps + 1,),
         in_specs=[whole(h_t), whole(df_t), whole(att_t)]
         + [part(tokens, n) for n in range(3)]
-        + [whole(d_first), whole(gains)],
+        + [whole(d_first), whole(gains)]
+        + [hbm] * moves,
         out_specs=[part(width, n) for n in range(3)]
-        + [pl.BlockSpec((width, width + gains.shape[1]), lambda i: (0, 0), pipeline_mode=pl.Buffered(1))],
+        + [pl.BlockSpec((width, width + gains.shape[1]), lambda i: (0, 0), pipeline_mode=pl.Buffered(1))]
+        + [hbm] * moves,
         out_shape=[jax.ShapeDtypeStruct((width, hidden), BF)] * 3
-        + [jax.ShapeDtypeStruct((width, width + gains.shape[1]), F32)],
-        compiler_params=params(),
+        + [jax.ShapeDtypeStruct((width, width + gains.shape[1]), F32)]
+        + [jax.ShapeDtypeStruct(a.shape, BF) for a in moving],
+        scratch_shapes=extra,
+        compiler_params=pltpu.CompilerParams(vmem_limit_bytes=VMEM_LIMIT, **more),
         name="outers",
-    )(h_t, df_t, att_t, d_gate, d_up, act, d_first, gains)
-
-
-CLOSING_ORDERS = ("xy", "yx", "xy")
+    )(h_t, df_t, att_t, d_gate, d_up, act, d_first, gains, *moving)
+
+
+CLOSING_ORDERS = ("xy", "xy", "xy")
 
 
 def closing_kernel(
@@ -918,21 +960,23 @@
 
     for load in loads[:5]:
         load.wait()
-    gives = []
-    for t in range(2):
-        rows_of(1 - y, t)
-        part = pl.ds(t * tile, tile)
-        gives.append(
-            pltpu.make_async_remote_copy(
-                src_ref=g.at[1 - y, part],
-                dst_ref=g_out.at[y, part],
-                send_sem=send.at[t],
-                recv_sem=recv.at[t],
-                device_id=device(moved(me, "y", 1)),
-                device_id_type=MESH,
-            )
+    quarter = half // 4
+
+    def give(n, target_half):
+        part = pl.ds(n * quarter, quarter)
+        return pltpu.make_async_remote_copy(
+            src_ref=g.at[1 - y, part],
+            dst_ref=g_out.at[target_half, part],
+            send_sem=send.at[n],
+            recv_sem=recv.at[n],
+            device_id=device(moved(me, "y", 1)),
+            device_id_type=MESH,
         )
-        gives[-1].start()
+
+    rows_of(1 - y, 0)
+    give(0, y).start()
+    give(1, y).start()
+    rows_of(1 - y, 1)
     for t in range(2):
         rows_of(y, t)
     keep = pltpu.make_async_copy(g.at[y], g_out.at[y], local.at[0])
@@ -943,7 +987,7 @@
         reduces.append(
             Reduce(
                 me, tall_piece(target), bufs[5 * n : 5 * n + 5], sum_ref.at[:, pl.ds(n * width, width)],
-                send, recv, mine_sem.at[pl.ds(2 * n, 2)], 2 + n * Reduce.SEMS, CLOSING_ORDERS[n],
+                send, recv, mine_sem.at[pl.ds(2 * n, 2)], 4 + n * Reduce.SEMS, CLOSING_ORDERS[n],
             )
         )
 
@@ -960,6 +1004,7 @@
 
     products(0, dq, w0)
     reduces[0].start()
+    give(2, y).start()
     products(1, dk, w1)
     reduces[1].start()
     reduces[0].step(1)
@@ -971,6 +1016,7 @@
     reduces[1].step(2)
     reduces[0].step(3)
     reduces[2].step(2)
+    give(3, y).start()
     reduces[1].step(3)
     reduces[0].step(4)
     reduces[2].step(3)
@@ -978,17 +1024,9 @@
     reduces[2].step(4)
     for r in reduces:
         r.finish()
-    for t in range(2):
-        part = pl.ds(t * tile, tile)
-        pltpu.make_async_remote_copy(
-            src_ref=g.at[1 - y, part],
-            dst_ref=g_out.at[1 - y, part],
-            send_sem=send.at[t],
-            recv_sem=recv.at[t],
-            device_id=device(moved(me, "y", 1)),
-            device_id_type=MESH,
-        ).wait_recv()
-        gives[t].wait_send()
+    for n in range(4):
+        give(n, 1 - y).wait_recv()
+        give(n, y).wait_send()
     keep.wait()
 
 
@@ -999,7 +1037,7 @@
     full = pltpu.VMEM((4, 2, 2, 2) + block, BF)
     scratch = [pltpu.VMEM(a.shape, BF) for a in (dq, dk, dv, first, xt, w)]
     scratch += [pltpu.VMEM((2, tokens // 2, width), BF), full, full, full]
-    sems = 2 + 3 * Reduce.SEMS
+    sems = 4 + 3 * Reduce.SEMS
     scratch += [pltpu.SemaphoreType.DMA((sems,))] * 2
     scratch += [pltpu.SemaphoreType.DMA((6,)), pltpu.SemaphoreType.DMA((6,))]
     for order in CLOSING_ORDERS:
@@ -1106,13 +1144,17 @@
         flat, att.reshape(n * t, width), cot.reshape(n * t, width), f_out, f_gate, f_up, f_down, g1, g2
     )
     gains = jnp.pad(jnp.concatenate([gg1, gg2]).T, ((0, 0), (0, PAIR - 2)))
-    gw_gate, gw_up, gw_down_t, gw_out = outers_call(h_t, df_t, att_t, d_gate, d_up, act, d_first, gains)
+    moving = (out.reshape(2, span, width),) if own else ()
+    gw_gate, gw_up, gw_down_t, gw_out, *moving = outers_call(
+        h_t, df_t, att_t, d_gate, d_up, act, d_first, gains, moving
+    )
     d_att = d_att.reshape(n, t, width)
     if own:
         wide = tuple(g.reshape(4, 2, 2, width // 16, -1) for g in (gw_gate, gw_up, gw_down_t))
-        dq, dk, dv, out, s_gate, s_up, s_down_t, s_out = attend_back_call(
+        out = moving[0]
+        dq, dk, dv, s_gate, s_up, s_down_t, s_out = attend_back_call(
             q, k, v, bias, att, d_att, aug, cq, sq, True,
-            (out.reshape(2, span, width),) + wide + (gw_out.reshape(4, 2, 2, 2, width // 32, -1),),
+            wide + (gw_out.reshape(4, 2, 2, 2, width // 32, -1),),
         )
     else:
 

time: 578 us -> 538 us (0.931)
  Pallas kernels: 549 us -> 509 us
    pallas_call x1, Pallas kernels: 104 us -> 87.3 us  [attend_call(): pl.pallas_call(functools.partial(attend_kernel, tile, chunk, moves), grid...]
    pallas_call x3, Pallas kernels: 273 us -> 259 us  [the longest x1 159 us: attend_back_call(): pl.pallas_call(functools.partial(attend_back_kernel, tq, moves), grid=(ro...]
    pallas_call x1, Pallas kernels: 65.3 us -> 56.5 us  [closing_call(): pl.pallas_call(closing_kernel, in_specs=[hbm] * 6, out_specs=[hbm, pl.Blo...]
where the time goes in v5:
time: 538 us; the launch traced here: 532 us
  Pallas kernels  509 us (95%)
  local copies, waits for them, and re-layouts  16.5 us (3%)
    pallas_call x1, Pallas kernels, attend_back_call(): pl.pallas_call(functools.partial(attend_back_kernel, tq, moves), grid=(ro...  159 us
    pallas_call x1, Pallas kernels, middle_call(): pl.pallas_call(functools.partial(middle_kernel, chunk), grid=(tokens // t...  93.2 us
    pallas_call x1, Pallas kernels, attend_call(): pl.pallas_call(functools.partial(attend_kernel, tile, chunk, moves), grid...  87.3 us
    pallas_call x1, Pallas kernels, closing_call(): pl.pallas_call(closing_kernel, in_specs=[hbm] * 6, out_specs=[hbm, pl.Blo...  56.5 us
    pallas_call x1, Pallas kernels, outers_call(): pl.pallas_call(functools.partial(outers_kernel, steps, moves), grid=(3 *...  51.1 us
    pallas_call x1, Pallas kernels, opening_call(): pl.pallas_call(opening_kernel, in_specs=[hbm] + [pl.BlockSpec(memory_spac...  49.4 us
    pallas_call x1, Pallas kernels, qkv_call(): pl.pallas_call(qkv_kernel, grid=(tokens // tile,), in_specs=[row, pl.Bloc...  13.3 us

profile of v5, /device:TPU:0, one launch (start us, length us, event | category | flops | bytes accessed | tf_op | source)
XLA Modules:
  0.0 532.0 jit_solution(11070585250888253469)
XLA Ops:
  0.6 1.2 dynamic_slice.3
  1.9 0.7 iota_compare_fusion.1
  2.6 0.7 copy.29
  3.3 0.7 copy.30
  4.0 1.5 fusion.4.rest_0_
  5.5 1.2 select_convert_fusion.bias_ref
  6.7 49.4 %opening.1 = (bf16[2,1024,768]{2,1,0:T(8,128)(2,1)}, bf16[4,2,2,2,24,2304]{5,4,3,2,1,0:T(8,128)(2,1)}, bf16[4,24,896]{2,1,0:T(8,128)(2,1)}, bf16[4,24,3072]{2,1,0:T(8,128)(2,1)}, bf16[4,24,3072]{2,1,0:T(8,128)(2,1)}) custom-call(bf16[2,1024,768]{2,1,0:T(8,128)(2,1)} %tok_ref.1, bf16[24,2304]{1,0:T(8,128)(2,1)} %qkv_ref.1, bf16[24,896]{1,0:T(8,128)(2,1)} %fusion.4.rest_0_, ...), custom_call_target="tpu_custom_call" | custom-call | tf_op jit(solution)/shard_map/opening/pallas_call | solution.py:335
  56.0 13.3 %qkv.1 = (bf16[2048,768]{1,0:T(8,128)(2,1)}, bf16[2048,768]{1,0:T(8,128)(2,1)}, bf16[2048,768]{1,0:T(8,128)(2,1)}, bf16[768,2048]{1,0:T(8,128)(2,1)}) custom-call(bf16[2048,768]{1,0:T(8,128)(2,1)} %bitcast.34, bf16[768,2304]{1,0:T(8,128)(2,1)} %bitcast.25, f32[2048,128]{1,0:T(8,128)} %constant.36.clone.cos_ref, f32[2048,128]{1,0:T(8,128)} %constant.37.clone.sin_ref), custom_call_target="tpu_custom_call" | custom-call | tf_op jit(solution)/shard_map/qkv/pallas_call | solution.py:381
  69.3 87.3 %attend.1 = (bf16[1,2048,768]{2,1,0:T(8,128)(2,1)}, bf16[1,2048,768]{2,1,0:T(8,128)(2,1)}, bf16[2,1024,768]{2,1,0:T(8,128)(2,1)}, bf16[4,2,2,2,24,896]{5,4,3,2,1...) custom-call(bf16[1,2048,768]{2,1,0:T(8,128)(2,1)} %bitcast.27, ...), custom_call_target="tpu_custom_call" | custom-call | tf_op jit(solution)/shard_map/attend/pallas_call | solution.py:557
  156.6 1.0 slice_convert_fusion
  157.6 0.4 slice_reduce_fusion
  158.0 2.4 slice.31.wo_ref
  160.3 0.6 broadcast_in_dim_squeeze.7.g2_ref
  160.9 0.6 broadcast_in_dim_squeeze.6.g1_ref
  161.5 93.2 %middle.1 = (bf16[2048,768]{1,0:T(8,128)(2,1)}, bf16[2048,768]{1,0:T(8,128)(2,1)}, bf16[2048,768]{1,0:T(8,128)(2,1)}, bf16[2048,3072]{1,0:T(8,128)(2,1)}, bf16[2...) custom-call(bf16[2048,768]{1,0:T(8,128)(2,1)} %bitcast.35, ...), custom_call_target="tpu_custom_call" | custom-call | tf_op jit(solution)/shard_map/middle/pallas_call | solution.py:823
  254.7 0.7 pad_maximum_fusion
  255.4 0.2 copy.31
  255.6 0.8 pad.9.gains_ref
  256.4 51.1 %outers.1 = (bf16[768,3072]{1,0:T(8,128)(2,1)}, bf16[768,3072]{1,0:T(8,128)(2,1)}, bf16[768,3072]{1,0:T(8,128)(2,1)}, f32[768,896]{1,0:T(8,128)}, bf16[2,1024,768]{2,1,0:T(8,128)(2,1)}) custom-call(bf16[768,2048]{1,0:T(8,128)(2,1)} %get-tuple-element.64.a1_ref, bf16[768,2048]{1,0:T(8,128)(2,1)} %get-tuple-element.65.a2_ref, ...), custom_call_target="tpu_custom_call" | custom-call | tf_op jit(solution)/shard_map/outers/pallas_call | solution.py:913
  307.6 158.5 %attend_back.1 = (bf16[1,2048,768]{2,1,0:T(8,128)(2,1)}, bf16[1,2048,768]{2,1,0:T(8,128)(2,1)}, bf16[1,2048,768]{2,1,0:T(8,128)(2,1)}, f32[48,1536]{1,0:T(8,128)...) custom-call(bf16[1,2048,768]{2,1,0:T(8,128)(2,1)} %bitcast.28, bf16[1,2048,768]{2,1,0:T(8,128)(2,1)} %bitcast.30, ...), custom_call_target="tpu_custom_call" | custom-call | tf_op jit(solution)/shard_map/attend_back/pallas_call | solution.py:716
  466.2 56.5 %closing.1 = (bf16[2,1024,768]{2,1,0:T(8,128)(2,1)}, f32[24,2304]{1,0:T(8,128)}) custom-call(bf16[2048,768]{1,0:T(8,128)(2,1)} %bitcast.44, bf16[2048,768]{1,0:T(8,128)(2,1)} %bitcast.45, bf16[2048,768]{1,0:T(8,128)(2,1)} %bitcast.46, bf16[2048,768]{1,0:T(8,128)(2,1)} %get-tuple-element.70.b4_ref.first_hbm, bf16[768,2048]{1,0:T(8,128)(2,1)} %get-tuple-element.84.xt_hbm, ...), custom_call_target="tpu_custom_call" | custom-call | tf_op jit(solution)/shard_map/closing/pallas_call | solution.py:1045
  522.7 0.7 slice_reduce_fusion.2
  523.4 0.6 slice.28
  524.0 1.7 copy.38
  525.7 1.4 copy-done.1
  527.0 1.7 copy.39
  528.7 0.7 copy.40
  529.4 0.0 copy-done.4
  529.4 0.7 copy.41
  530.1 0.0 copy-done.3
  530.1 0.7 copy.42
  530.8 0.7 copy.43
  (12 shorter events, 0.0 us)
Async XLA Ops:
  466.1 56.5 %copy-start.6 = (f32[24,896]{1,0:T(8,128)S(1)}, f32[24,896]{1,0:T(8,128)}, u32[]{:S(2)}) copy-start(f32[24,896]{1,0:T(8,128)} %get-tuple-element.87) | copy-start | bytes 258052
  466.1 57.8 %copy-start = (bf16[2,1024,768]{2,1,0:T(8,128)(2,1)S(1)}, bf16[2,1024,768]{2,1,0:T(8,128)(2,1)}, u32[]{:S(2)}) copy-start(bf16[2,1024,768]{2,1,0:T(8,128)(2,1)} %get-tuple-element.104) | copy-start | bytes 9437188
  524.0 3.0 copy-start.1
  527.0 1.7 copy-start.5
  527.0 2.4 copy-start.4
  527.0 3.1 copy-start.3
  527.0 3.8 copy-start.2

commit v6 on v5

--- a/solution.py
+++ b/solution.py
@@ -71,10 +71,9 @@
 
 class Gather:
     def __init__(self, me, shard, full, send, recv, local, base, order, held="", columns=None):
-        self.me, self.full, self.held = me, full, held
+        self.me, self.shard, self.full, self.held = me, shard, full, held
         self.part = () if columns is None else (slice(None), pl.ds(*columns))
-        lead = (slice(None),) * len(held)
-        self.shard = shard.at[lead + self.part] if self.part else shard
+        self.spans = [a for a in AXES if a in held + order]
         self.send, self.recv, self.local, self.base, self.order = send, recv, local, base, order
 
     @staticmethod
@@ -82,10 +81,7 @@
         return sum(SIZE[a] - 1 for a in order)
 
     def view(self, at, got):
-        return self.full.at[tuple(slice(None) if a in got else at[a] for a in AXES if a in self.axes()) + self.part]
-
-    def axes(self):
-        return AXES if len(self.full.shape) == 6 else "z"
+        return self.full.at[tuple(slice(None) if a in got else at[a] for a in self.spans) + self.part]
 
     def at_stage(self, stage):
         got = self.held + self.order[:stage]
@@ -284,19 +280,19 @@
         self.keep_out().wait()
 
 
-OPENING_ORDERS = ("yzxc", "zyxc", "z", "z", "z")
+OPENING_ORDERS = ("yzxc", "zyxc", "z", "z")
 
 
 def opening_kernel(tok_ref, qkv_ref, *rest):
-    early, rest = rest[:3], rest[3:]
+    early, rest = rest[:2], rest[2:]
     x_ref, full_ref, rest = rest[0], rest[1], rest[2:]
-    early_out, (bounce, send, recv, local) = rest[:3], rest[3:]
+    early_out, (bounce, send, recv, local) = rest[:2], rest[2:]
     me = place()
     greet(me)
     rows = tok_ref.shape[1]
     swap = Swap(me, tok_ref, x_ref, bounce, send, recv, local.at[0], 0, ((0, rows // 8), (rows // 8, rows - rows // 8)))
     half = qkv_ref.shape[-1] // 2
-    sources = [(qkv_ref, full_ref, (0, half)), (qkv_ref, full_ref, (half, half))]
+    sources = [(qkv_ref.at[:, pl.ds(n * half, half)], full_ref, (n * half, half)) for n in range(2)]
     sources += [(a, b, None) for a, b in zip(early, early_out)]
     gathers, base = [], 2
     for i, (source, full, columns) in enumerate(sources):
@@ -334,8 +330,8 @@
     sems = 2 + sum(map(Gather.sems, OPENING_ORDERS))
     return pl.pallas_call(
         opening_kernel,
-        in_specs=[hbm] + [pl.BlockSpec(memory_space=pltpu.VMEM)] * 4,
-        out_specs=[hbm] * 5,
+        in_specs=[hbm] + [pl.BlockSpec(memory_space=pltpu.VMEM)] * 3,
+        out_specs=[hbm] * 4,
         out_shape=[
             jax.ShapeDtypeStruct(tokens.shape, BF),
             jax.ShapeDtypeStruct((4, 2, 2, 2) + w_qkv.shape, BF),
@@ -345,7 +341,7 @@
             pltpu.VMEM(tokens.shape[1:], BF),
             pltpu.SemaphoreType.DMA((sems,)),
             pltpu.SemaphoreType.DMA((sems,)),
-            pltpu.SemaphoreType.DMA((6,)),
+            pltpu.SemaphoreType.DMA((5,)),
         ],
         compiler_params=pltpu.CompilerParams(
             vmem_limit_bytes=VMEM_LIMIT, collective_id=0, has_side_effects=True
@@ -354,7 +350,40 @@
     )(tokens, w_qkv, *early)
 
 
-def qkv_kernel(x_ref, w_ref, cos_ref, sin_ref, q_ref, k_ref, v_ref, xt_ref):
+QKV_ORDERS = ("y", "x", "z", "y", "x")
+QKV_HELD = ("z", "z", "", "", "")
+
+
+def halves(ref):
+    half = ref.shape[-1] // 2
+    return [ref.at[:, pl.ds(n * half, half)] for n in range(2)]
+
+
+def stages(me, shards, fulls, orders, held, columns, send, recv, local):
+    out, base = [], 0
+    for i, order in enumerate(orders):
+        out.append(
+            Gather(me, shards[i], fulls[i], send, recv, local.at[i], base, order, held[i], columns[i])
+        )
+        base += Gather.sems(order)
+    return out
+
+
+def qkv_kernel(moves, x_ref, w_ref, cos_ref, sin_ref, *rest):
+    shards, rest = rest[:moves], rest[moves:]
+    q_ref, k_ref, v_ref, xt_ref, rest = rest[0], rest[1], rest[2], rest[3], rest[4:]
+    if moves:
+        fulls, (send, recv, local) = rest[:5], rest[5:]
+        me = place()
+        shards = list(shards[:3]) + halves(shards[3])
+        gathers = stages(me, shards, fulls, QKV_ORDERS, QKV_HELD, (None,) * 5, send, recv, local)
+
+        @pl.when(pl.program_id(0) == 0)
+        def _():
+            greet(me)
+            for i in (3, 4, 0, 1, 2):
+                gathers[i].start()
+
     x = x_ref[...]
     width = x.shape[1]
     cosine, sine = cos_ref[...], sin_ref[...]
@@ -370,35 +399,62 @@
                 u = u * (0.125 * LOG2E)
             out[:, pair * PAIR : (pair + 1) * PAIR] = u.astype(BF)
     xt_ref[...] = x.T
-
-
-def qkv_call(x, w, cosine, sine, tile=512):
+    if moves:
+
+        @pl.when(pl.program_id(0) == pl.num_programs(0) - 1)
+        def _():
+            for g in gathers:
+                g.step(1)
+            for g in gathers:
+                g.finish()
+
+
+def qkv_call(x, w, cosine, sine, moving=(), tile=512):
     tokens, width = x.shape
     span = cosine.shape[0]
     tile = min(tile, span)
+    moves = len(moving)
     row = pl.BlockSpec((tile, width), lambda i: (i, 0))
     table = pl.BlockSpec((tile, PAIR), lambda i: (i % (span // tile), 0))
+    results, extra, more = [], [], {}
+    if moves:
+        for i, order in enumerate(QKV_ORDERS):
+            a = moving[min(i, 3)]
+            spans = tuple(SIZE[n] for n in AXES if n in QKV_HELD[i] + order)
+            block = (a.shape[-2], a.shape[-1] // (2 if i >= 3 else 1))
+            results.append(jax.ShapeDtypeStruct(spans + block, BF))
+        sems = sum(map(Gather.sems, QKV_ORDERS))
+        extra = [pltpu.SemaphoreType.DMA((n,)) for n in (sems, sems, len(QKV_ORDERS))]
+        more = dict(collective_id=6, has_side_effects=True)
     return pl.pallas_call(
-        qkv_kernel,
+        functools.partial(qkv_kernel, moves),
         grid=(tokens // tile,),
         in_specs=[
             row,
             pl.BlockSpec(w.shape, lambda i: (0, 0), pipeline_mode=pl.Buffered(1)),
             table,
             table,
+        ]
+        + [
+            pl.BlockSpec(a.shape, lambda i, n=a.ndim: (0,) * n, pipeline_mode=pl.Buffered(1))
+            for a in moving
         ],
-        out_specs=[row, row, row, pl.BlockSpec((width, tile), lambda i: (0, i))],
+        out_specs=[row, row, row, pl.BlockSpec((width, tile), lambda i: (0, i))]
+        + [pl.BlockSpec(memory_space=pl.ANY)] * len(results),
         out_shape=[jax.ShapeDtypeStruct((tokens, width), BF)] * 3
-        + [jax.ShapeDtypeStruct((width, tokens), BF)],
-        compiler_params=params(),
+        + [jax.ShapeDtypeStruct((width, tokens), BF)]
+        + results,
+        scratch_shapes=extra,
+        compiler_params=pltpu.CompilerParams(vmem_limit_bytes=VMEM_LIMIT, **more),
         name="qkv",
-    )(x, w, cosine, sine)
+    )(x, w, cosine, sine, *moving)
 
 
 def attend_kernel(tile, chunk, moves, q_ref, k_ref, v_ref, bias_ref, *rest):
-    inputs, rest = rest[: moves], rest[moves:]
+    inputs, rest = rest[:moves], rest[moves:]
     o_ref, aug_ref, rest = rest[0], rest[1], rest[2:]
-    outputs, rest = rest[: moves], rest[moves:]
+    results = max(moves - 1, 0)
+    outputs, rest = rest[:results], rest[results:]
     ka, va, s_scr, m_scr = rest[:4]
     keys, span = k_ref.shape[1], q_ref.shape[1]
     tiles = span // tile
@@ -453,14 +509,6 @@
     close(0, top)
 
     def step(i, _):
-        now = pl.program_id(1) * tiles + i
-        for at_step, acts in events.items():
-
-            @pl.when(now == at_step)
-            def _():
-                for act in acts:
-                    act()
-
         acc0, top, m0 = unit(0, i, 1)
         close(1, top)
         acc1, top, m1 = unit(1, jnp.minimum(i + 1, tiles - 1), 0)
@@ -473,7 +521,22 @@
         aug_ref[0, at, :] = spread(lse, jnp.where(lane % HEAD == 3, 1.0, 0.0))
         return 0
 
-    lax.fori_loop(0, tiles, step, 0)
+    unroll = 2 if tiles % 2 == 0 else 1
+
+    def group(n, _):
+        now = pl.program_id(1) * (tiles // unroll) + n
+        for at_step, acts in events.items():
+
+            @pl.when(now == at_step)
+            def _():
+                for act in acts:
+                    act()
+
+        for j in range(unroll):
+            step(n * unroll + j, 0)
+        return 0
+
+    lax.fori_loop(0, tiles // unroll, group, 0)
     if moves:
 
         @pl.when(pl.program_id(1) == pl.num_programs(1) - 1)
@@ -490,37 +553,29 @@
         self.setdefault(at, []).extend(acts)
 
 
-ATTEND_ORDERS = ("yxc", "xyc", "yxc", "yzxc")
-ATTEND_PLAN = (
-    (3, 3, 1), (4, 0, 1), (6, 1, 1), (8, 2, 1), (9, 0, 2), (12, 3, 2), (17, 1, 2), (18, 2, 2),
-)
-ATTEND_SWAP = 8
-
-
-def attend_events(inputs, outputs, bounce, send, recv, local):
+ATTEND_HELD = ("zy", "zx", "z", "y", "x")
+ATTEND_ORDERS = ("xc", "yc", "yxc", "zxc", "zyc")
+ATTEND_PLAN = ((2, 0, 1), (4, 2, 1), (4, 3, 1), (7, 4, 1), (10, 1, 1), (10, 2, 2))
+ATTEND_FIRST = (2, 1, 0, 3, 4)
+
+
+def attend_events(inputs, outputs, send, recv, local):
     me = place()
-    rows = inputs[0].shape[1]
-    swap = Swap(me, inputs[0], outputs[0], bounce, send, recv, local.at[0], 0, ((0, rows),))
-    gathers, base = [], 1
-    for i, (shard, full) in enumerate(zip(inputs[1:], outputs[1:])):
-        held = "z" if i < 3 else ""
-        gathers.append(
-            Gather(me, shard, full, send, recv, local.at[1 + i], base, ATTEND_ORDERS[i], held)
-        )
-        base += Gather.sems(ATTEND_ORDERS[i])
+    half = inputs[3].shape[-1]
+    columns = (None, None, None, (0, half), (half, half))
+    fulls = tuple(outputs) + (outputs[3],)
+    gathers = stages(me, inputs, fulls, ATTEND_ORDERS, ATTEND_HELD, columns, send, recv, local)
     events = Events()
-    events.put(0, functools.partial(greet, me), *(gathers[i].start for i in (3, 0, 2, 1)))
+    events.put(0, functools.partial(greet, me), *(gathers[i].start for i in ATTEND_FIRST))
     done = [1] * len(gathers)
     for at, i, stage in ATTEND_PLAN:
         events.put(at, functools.partial(gathers[i].step, stage))
         done[i] = stage + 1
-    events.put(ATTEND_SWAP, functools.partial(swap.give, 0), swap.keep_begin)
-    events.put(ATTEND_SWAP + 3, swap.keep_turn)
-    for stage in range(1, 5):
+    for stage in range(1, 4):
         for i, g in enumerate(gathers):
             if done[i] <= stage <= len(ATTEND_ORDERS[i]):
                 events.last.append(functools.partial(g.step, stage))
-    events.last += [g.finish for g in gathers] + [swap.finish]
+    events.last += [g.finish for g in gathers]
     return events
 
 
@@ -543,24 +598,22 @@
     qs = pl.BlockSpec((1, span, PAIR), lambda r, p: (r, 0, p))
     ks = pl.BlockSpec((1, keys, PAIR), lambda r, p: (r, 0, p))
     hbm = pl.BlockSpec(memory_space=pl.ANY)
-    moved_shapes = [jax.ShapeDtypeStruct(a.shape, a.dtype) for a in moving[:1]] + [
-        jax.ShapeDtypeStruct((4, 2, 2, 2) + a.shape[-2:], a.dtype) for a in moving[1:]
-    ]
-    sems = 1 + sum(map(Gather.sems, ATTEND_ORDERS))
-    extra = [pltpu.VMEM(moving[0].shape[1:], BF)] if moves else []
-    extra += [pltpu.SemaphoreType.DMA((sems,))] * 2 + [pltpu.SemaphoreType.DMA((moves,))]
+    moved_shapes = [jax.ShapeDtypeStruct((4, 2, 2, 2) + a.shape[-2:], a.dtype) for a in moving[:3]]
+    for a in moving[3:4]:
+        moved_shapes.append(jax.ShapeDtypeStruct((4, 2, 2, 2, a.shape[-2], 2 * a.shape[-1]), a.dtype))
+    sems = sum(map(Gather.sems, ATTEND_ORDERS))
+    extra = [pltpu.SemaphoreType.DMA((sems,))] * 2 + [pltpu.SemaphoreType.DMA((len(ATTEND_ORDERS),))]
     held = [
         pl.BlockSpec(a.shape, lambda r, p, n=a.ndim: (0,) * n, pipeline_mode=pl.Buffered(1))
-        for a in moving[1:]
+        for a in moving
     ]
     more = dict(collective_id=1, has_side_effects=True) if moves else {}
     return pl.pallas_call(
         functools.partial(attend_kernel, tile, chunk, moves),
         grid=(rows, width // PAIR),
         in_specs=[qs, ks, ks, pl.BlockSpec((1, keys, PAIR), lambda r, p: (r, 0, 0))]
-        + [hbm] * min(moves, 1)
         + held,
-        out_specs=[qs, qs] + [hbm] * moves,
+        out_specs=[qs, qs] + [hbm] * len(moved_shapes),
         out_shape=[jax.ShapeDtypeStruct(q.shape, BF)] * 2 + moved_shapes,
         scratch_shapes=[
             pltpu.VMEM((keys, 2 * PAIR), BF),
@@ -575,7 +628,7 @@
 
 
 def attend_back_kernel(
-    tq, moves, q_ref, k_ref, v_ref, bias_ref, o_ref, do_ref, aug_ref, cos_ref, sin_ref, *rest
+    tq, unroll, moves, q_ref, k_ref, v_ref, bias_ref, o_ref, do_ref, aug_ref, cos_ref, sin_ref, *rest
 ):
     inputs, rest = rest[:moves], rest[moves:]
     dq_ref, dk_ref, dv_ref, rest = rest[0], rest[1], rest[2], rest[3:]
@@ -615,14 +668,6 @@
     dv_acc[...] = jnp.zeros_like(dv_acc)
 
     def query_step(i, _):
-        now = pl.program_id(1) * tiles + i
-        for at_step, acts in events.items():
-
-            @pl.when(now == at_step)
-            def _():
-                for act in acts:
-                    act()
-
         at_q = pl.ds(pl.multiple_of(i * tq, tq), tq)
         dv, dk, dq = None, None, []
         for h in range(2):
@@ -641,7 +686,20 @@
         dq_ref[0, at_q, :] = back_turn(g, cos_ref[at_q, :], sin_ref[at_q, :]).astype(BF)
         return 0
 
-    lax.fori_loop(0, tiles, query_step, 0)
+    def group(n, _):
+        now = pl.program_id(1) * (tiles // unroll) + n
+        for at_step, acts in events.items():
+
+            @pl.when(now == at_step)
+            def _():
+                for act in acts:
+                    act()
+
+        for j in range(unroll):
+            query_step(n * unroll + j, 0)
+        return 0
+
+    lax.fori_loop(0, tiles // unroll, group, 0)
     dv_ref[0] = dv_acc[...].astype(dv_ref.dtype)
     g = dk_acc[...] * LN2
     if dk_ref.dtype == BF:
@@ -669,8 +727,8 @@
 
 BACK_ORDERS = ("yx", "yx", "xy", "xy")
 BACK_PLAN = (
-    (2, 0, 1), (2, 2, 1), (3, 1, 1), (3, 3, 1), (7, 0, 2), (7, 2, 2), (10, 3, 2), (12, 0, 3), (12, 1, 2),
-    (14, 2, 3), (15, 1, 3), (16, 3, 3), (18, 0, 4), (19, 2, 4), (20, 1, 4), (21, 3, 4),
+    (1, 0, 1), (1, 2, 1), (1, 1, 1), (1, 3, 1), (3, 0, 2), (3, 2, 2), (3, 3, 2), (4, 0, 3), (4, 2, 3), (4, 1, 2),
+    (5, 1, 3), (5, 3, 3), (5, 0, 4),
 )
 
 
@@ -689,14 +747,16 @@
     events.put(0, functools.partial(greet, me), *(reduces[i].start for i in (0, 2, 1, 3)))
     for at, i, stage in BACK_PLAN:
         events.put(at, functools.partial(reduces[i].step, stage))
+    events.last += [functools.partial(reduces[i].step, 4) for i in (2, 1, 3)]
     events.last += [r.finish for r in reduces]
     return events
 
 
-def attend_back_call(q, k, v, bias, o, do, aug, cosine, sine, whole, moving=(), tq=512):
+def attend_back_call(q, k, v, bias, o, do, aug, cosine, sine, whole, moving=(), tq=512, unroll=4):
     rows, span, width = q.shape
     keys = k.shape[1]
     tq = min(tq, span)
+    unroll = min(unroll, span // tq)
     moves = len(moving)
     qs = pl.BlockSpec((1, span, PAIR), lambda r, p: (r, 0, p))
     ks = pl.BlockSpec((1, keys, PAIR), lambda r, p: (r, 0, p))
@@ -714,7 +774,7 @@
             extra += Reduce.scratch(*block, a.dtype, order)
         more = dict(collective_id=2, has_side_effects=True)
     return pl.pallas_call(
-        functools.partial(attend_back_kernel, tq, moves),
+        functools.partial(attend_back_kernel, tq, unroll, moves),
         grid=(rows, width // PAIR),
         in_specs=[
             qs, ks, ks,
@@ -745,10 +805,43 @@
 
 
 def middle_kernel(
-    chunk, x_ref, att_ref, cot_ref, wo_ref, wg_ref, wu_ref, wd_ref, g1_ref, g2_ref,
-    out_ref, dfirst_ref, datt_ref, act_ref, dg_ref, du_ref, ht_ref, dft_ref, at_ref, gg1_ref, gg2_ref,
-    ca, cb,
+    chunk, moves, x_ref, att_ref, cot_ref, wo_ref, wg_ref, wu_ref, wd_ref, g1_ref, g2_ref, *rest
 ):
+    source, rest = rest[:moves], rest[moves:]
+    (out_ref, dfirst_ref, datt_ref, act_ref, dg_ref, du_ref, ht_ref, dft_ref, at_ref, gg1_ref, gg2_ref) = rest[:11]
+    ca, cb = rest[11:13]
+    if moves:
+        arrived, dy_ref, send, recv = rest[13:]
+        me = place()
+        now, per = pl.program_id(0), pl.num_programs(0) // 2
+        tile = dy_ref.shape[0]
+        give = pltpu.make_async_remote_copy(
+            src_ref=source[0].at[1 - me["y"]],
+            dst_ref=arrived,
+            send_sem=send.at[0],
+            recv_sem=recv.at[0],
+            device_id=device(moved(me, "y", 1)),
+            device_id_type=MESH,
+        )
+
+        @pl.when(now == 0)
+        def _():
+            greet(me)
+            give.start()
+
+        pl.when(now == per)(give.wait)
+
+        @pl.when(now < per)
+        def _():
+            dy_ref[...] = cot_ref[...]
+
+        @pl.when(now >= per)
+        def _():
+            dy_ref[...] = arrived[pl.ds(pl.multiple_of((now - per) * tile, tile), tile), :]
+
+    else:
+        dy_ref = cot_ref
+
     @pl.when(pl.program_id(0) == 0)
     def _():
         gg1_ref[...] = jnp.zeros_like(gg1_ref)
@@ -757,7 +850,7 @@
     gain1, gain2 = g1_ref[...], g2_ref[...]
     att = att_ref[...]
     at_ref[...] = att.T
-    first = x_ref[...].astype(F32) + dot(att, wo_ref[...])
+    first = x_ref[...].astype(F32) + dot(att, wo_ref[:, : att.shape[1]])
     centered = first - jnp.mean(first, axis=1, keepdims=True)
     s1 = lax.rsqrt(jnp.mean(centered * centered, axis=1, keepdims=True) + EPS)
     n1 = centered * s1
@@ -781,7 +874,7 @@
     s2 = lax.rsqrt(jnp.mean(centered * centered, axis=1, keepdims=True) + EPS)
     n2 = centered * s2
     out_ref[...] = (n2 * gain2).astype(BF)
-    dy = cot_ref[...].astype(F32)
+    dy = dy_ref[...].astype(F32)
     gg2_ref[...] += jnp.sum(dy * n2, axis=0, keepdims=True)
     inner = dy * gain2
     d_second = s2 * (
@@ -805,34 +898,51 @@
     )
     low = d_first.astype(BF)
     dfirst_ref[...] = low
-    datt_ref[...] = dot_nt(low, wo_ref[...]).astype(BF)
+    datt_ref[...] = dot_nt(low, wo_ref[:, : low.shape[1]]).astype(BF)
 
 
 def middle_call(x, att, cot, wo, wg, wu, wd, g1, g2, tile=256, chunk=768):
     tokens, width = x.shape
     hidden_width = wg.shape[1]
     tile = min(tile, tokens)
-    row = pl.BlockSpec((tile, width), lambda i: (i, 0))
-    wide = pl.BlockSpec((tile, hidden_width), lambda i: (i, 0))
-    column = pl.BlockSpec((width, tile), lambda i: (0, i))
+    moves = cot.ndim - 2
+    per = tokens // tile // 2
+
+    def place_of(i):
+        if not moves:
+            return i
+        return lax.rem(lax.axis_index("blk") + i // per, 2) * per + lax.rem(i, per)
+
+    row = pl.BlockSpec((tile, width), lambda i: (place_of(i), 0))
+    wide = pl.BlockSpec((tile, hidden_width), lambda i: (place_of(i), 0))
+    column = pl.BlockSpec((width, tile), lambda i: (0, place_of(i)))
+    cot_row, extra, more = row, [], {}
+    if moves:
+        cot_row = pl.BlockSpec(
+            (None, tile, width), lambda i: (lax.axis_index("blk"), jnp.minimum(i, per - 1), 0)
+        )
+        extra = [pltpu.VMEM((tokens // 2, width), BF), pltpu.VMEM((tile, width), BF)]
+        extra += [pltpu.SemaphoreType.DMA((1,))] * 2
+        more = dict(collective_id=5, has_side_effects=True)
 
     def whole(a):
         return pl.BlockSpec(a.shape, lambda i: (0, 0), pipeline_mode=pl.Buffered(1))
 
     gain = pl.BlockSpec((1, width), lambda i: (0, 0))
     return pl.pallas_call(
-        functools.partial(middle_kernel, chunk),
+        functools.partial(middle_kernel, chunk, moves),
         grid=(tokens // tile,),
-        in_specs=[row, row, row, whole(wo), whole(wg), whole(wu), whole(wd), gain, gain],
+        in_specs=[row, row, cot_row, whole(wo), whole(wg), whole(wu), whole(wd), gain, gain]
+        + [pl.BlockSpec(memory_space=pl.ANY)] * moves,
         out_specs=[row, row, row, wide, wide, wide, column, column, column, gain, gain],
         out_shape=[jax.ShapeDtypeStruct((tokens, width), BF)] * 3
         + [jax.ShapeDtypeStruct((tokens, hidden_width), BF)] * 3
         + [jax.ShapeDtypeStruct((width, tokens), BF)] * 3
         + [jax.ShapeDtypeStruct((1, width), F32)] * 2,
-        scratch_shapes=[pltpu.VMEM((tile, hidden_width), F32)] * 2,
-        compiler_params=params(),
+        scratch_shapes=[pltpu.VMEM((tile, hidden_width), F32)] * 2 + extra,
+        compiler_params=pltpu.CompilerParams(vmem_limit_bytes=VMEM_LIMIT, **more),
         name="middle",
-    )(x, att, cot, wo, wg, wu, wd, g1, g2)
+    )(x, att, cot, wo, wg, wu, wd, g1, g2, *([cot] * moves))
 
 
 def outer_kernel(a_ref, b_ref, o_ref):
@@ -977,10 +1087,6 @@
     give(0, y).start()
     give(1, y).start()
     rows_of(1 - y, 1)
-    for t in range(2):
-        rows_of(y, t)
-    keep = pltpu.make_async_copy(g.at[y], g_out.at[y], local.at[0])
-    keep.start()
     loads[5].wait()
     reduces = []
     for n, (a, target) in enumerate(((dq, w0), (dk, w1), (dv, w2))):
@@ -1013,8 +1119,12 @@
     reduces[1].step(1)
     reduces[0].step(2)
     reduces[2].step(1)
+    rows_of(y, 0)
     reduces[1].step(2)
     reduces[0].step(3)
+    rows_of(y, 1)
+    keep = pltpu.make_async_copy(g.at[y], g_out.at[y], local.at[0])
+    keep.start()
     reduces[2].step(2)
     give(3, y).start()
     reduces[1].step(3)
@@ -1108,7 +1218,7 @@
     gains = jnp.stack([gain_one, gain_two], 1)
     if own:
         w_out = jnp.pad(jnp.concatenate([w_out, gains], 1), ((0, 0), (0, PAIR - 2)))
-        x, f_qkv, w_out, w_gate, w_up = opening_call(tokens, w_qkv, (w_out, w_gate, w_up))
+        x, f_qkv, w_out, w_gate = opening_call(tokens, w_qkv, (w_out, w_gate))
         x = x.reshape(1, seq, width)
         f_qkv = f_qkv.reshape(width, -1)
         length = lax.dynamic_slice_in_dim(lengths, mine, 1, 0)
@@ -1116,12 +1226,14 @@
     else:
         f_qkv, f_out, f_gate, f_up, f_down = map(gather, (w_qkv, w_out, w_gate, w_up, w_down))
         f_gains = gather(gains).astype(F32)
-        x, cot, length = tokens, cotangent, lengths
+        x, cot, length = tokens, cotangent.reshape(rows * span, width), lengths
         cq = lax.dynamic_slice_in_dim(cosine, mine * span, span, 0)
         sq = lax.dynamic_slice_in_dim(sine, mine * span, span, 0)
     n, t = x.shape[:2]
     flat = x.reshape(n * t, width)
-    q, k, v, xt = qkv_call(flat, f_qkv, cq, sq)
+    q, k, v, xt, *moving = qkv_call(
+        flat, f_qkv, cq, sq, (w_out, w_gate, w_up, w_down) if own else ()
+    )
     q, k, v = (a.reshape(n, t, width) for a in (q, k, v))
     if not own:
         k = lax.all_gather(k, "blk", axis=1, tiled=True)
@@ -1130,18 +1242,19 @@
     lane = jnp.arange(PAIR, dtype=jnp.int32)[None, None, :]
     bias = jnp.where((lane % HEAD == 3) & (position >= length[:, None, None]), NEG, 0.0).astype(BF)
     if own:
-        att, aug, cot, f_out, f_gate, f_up, f_down = attend_call(
-            q, k, v, bias, (cotangent, w_out, w_gate, w_up, w_down)
+        att, aug, f_out, f_gate, f_up, f_down = attend_call(
+            q, k, v, bias, moving
         )
         f_out = f_out.reshape(width, -1)
-        f_out, f_gains = f_out[:, :width], f_out[:, width : width + 2].astype(F32)
+        f_gains = f_out[:, width : width + 2].astype(F32)
+        cot = cotangent
         f_gate, f_up = f_gate.reshape(width, -1), f_up.reshape(width, -1)
         f_down = f_down.reshape(-1, width)
     else:
         att, aug = attend_call(q, k, v, bias)
     g1, g2 = f_gains[:, 0][None], f_gains[:, 1][None]
     out, d_first, d_att, act, d_gate, d_up, h_t, df_t, att_t, gg1, gg2 = middle_call(
-        flat, att.reshape(n * t, width), cot.reshape(n * t, width), f_out, f_gate, f_up, f_down, g1, g2
+        flat, att.reshape(n * t, width), cot, f_out, f_gate, f_up, f_down, g1, g2
     )
     gains = jnp.pad(jnp.concatenate([gg1, gg2]).T, ((0, 0), (0, PAIR - 2)))
     moving = (out.reshape(2, span, width),) if own else ()

time: 538 us -> 527 us (0.980)
  Pallas kernels: 509 us -> 499 us
    pallas_call x1, Pallas kernels: 87.3 us -> 76.6 us  [attend_call(): pl.pallas_call(functools.partial(attend_kernel, tile, chunk, moves), grid...]
where the time goes in v6:
time: 527 us; the launch traced here: 519 us
  Pallas kernels  499 us (95%)
  local copies, waits for them, and re-layouts  14.1 us (3%)
    pallas_call x1, Pallas kernels, attend_back_call(): pl.pallas_call(functools.partial(attend_back_kernel, tq, unroll, moves),...  149 us
    pallas_call x1, Pallas kernels, middle_call(): pl.pallas_call(functools.partial(middle_kernel, chunk, moves), grid=(toke...  97.6 us
    pallas_call x1, Pallas kernels, attend_call(): pl.pallas_call(functools.partial(attend_kernel, tile, chunk, moves), grid...  76.6 us
    pallas_call x1, Pallas kernels, closing_call(): pl.pallas_call(closing_kernel, in_specs=[hbm] * 6, out_specs=[hbm, pl.Blo...  56.5 us
    pallas_call x1, Pallas kernels, outers_call(): pl.pallas_call(functools.partial(outers_kernel, steps, moves), grid=(3 *...  48.8 us
    pallas_call x1, Pallas kernels, opening_call(): pl.pallas_call(opening_kernel, in_specs=[hbm] + [pl.BlockSpec(memory_spac...  48.1 us
    pallas_call x1, Pallas kernels, qkv_call(): pl.pallas_call(functools.partial(qkv_kernel, moves), grid=(tokens // tile...  22.6 us

profile of v6, /device:TPU:0, one launch (start us, length us, event | category | flops | bytes accessed | tf_op | source)
XLA Modules:
  0.0 519.1 jit_solution(9877555960526325804)
XLA Ops:
  0.6 1.2 dynamic_slice.3
  1.9 0.7 iota_compare_fusion.1
  2.6 0.7 copy.29
  3.3 0.7 copy.30
  4.0 1.5 fusion.4.rest_0_
  5.5 1.1 select_convert_fusion.bias_ref
  6.6 48.1 %opening.1 = (bf16[2,1024,768]{2,1,0:T(8,128)(2,1)}, bf16[4,2,2,2,24,2304]{5,4,3,2,1,0:T(8,128)(2,1)}, bf16[4,24,896]{2,1,0:T(8,128)(2,1)}, bf16[4,24,3072]{2,1,0:T(8,128)(2,1)}) custom-call(bf16[2,1024,768]{2,1,0:T(8,128)(2,1)} %tok_ref.1, bf16[24,2304]{1,0:T(8,128)(2,1)} %qkv_ref.1, bf16[24,896]{1,0:T(8,128)(2,1)} %fusion.4.rest_0_, bf16[24,3072]{1,0:T(8,128)(2,1)} %rest_1_.1), custom_call_target="tpu_custom_call" | custom-call | tf_op jit(solution)/shard_map/opening/pallas_call | solution.py:331
  54.8 22.6 %qkv.1 = (bf16[2048,768]{1,0:T(8,128)(2,1)}, bf16[2048,768]{1,0:T(8,128)(2,1)}, bf16[2048,768]{1,0:T(8,128)(2,1)}, bf16[768,2048]{1,0:T(8,128)(2,1)}, bf16[4,2,2...) custom-call(bf16[2048,768]{1,0:T(8,128)(2,1)} %bitcast.33, ...), custom_call_target="tpu_custom_call" | custom-call | tf_op jit(solution)/shard_map/qkv/pallas_call | solution.py:429
  77.3 76.6 %attend.1 = (bf16[1,2048,768]{2,1,0:T(8,128)(2,1)}, bf16[1,2048,768]{2,1,0:T(8,128)(2,1)}, bf16[4,2,2,2,24,896]{5,4,3,2,1,0:T(8,128)(2,1)}, bf16[4,2,2,2,24,3072...) custom-call(bf16[1,2048,768]{2,1,0:T(8,128)(2,1)} %bitcast.27, ...), custom_call_target="tpu_custom_call" | custom-call | tf_op jit(solution)/shard_map/attend/pallas_call | solution.py:611
  154.0 1.0 slice_convert_fusion
  154.9 0.4 slice_reduce_fusion
  155.3 0.6 broadcast_in_dim_squeeze.7.g2_ref
  155.9 0.6 broadcast_in_dim_squeeze.6.g1_ref
  156.5 97.6 %middle.1 = (bf16[2048,768]{1,0:T(8,128)(2,1)}, bf16[2048,768]{1,0:T(8,128)(2,1)}, bf16[2048,768]{1,0:T(8,128)(2,1)}, bf16[2048,3072]{1,0:T(8,128)(2,1)}, bf16[2...) custom-call(bf16[2048,768]{1,0:T(8,128)(2,1)} %bitcast.34, ...), custom_call_target="tpu_custom_call" | custom-call | tf_op jit(solution)/shard_map/middle/pallas_call | solution.py:932
  254.2 0.7 pad_maximum_fusion
  254.8 0.2 copy.31
  255.0 0.8 pad.9.gains_ref
  255.8 48.8 %outers.1 = (bf16[768,3072]{1,0:T(8,128)(2,1)}, bf16[768,3072]{1,0:T(8,128)(2,1)}, bf16[768,3072]{1,0:T(8,128)(2,1)}, f32[768,896]{1,0:T(8,128)}, bf16[2,1024,768]{2,1,0:T(8,128)(2,1)}) custom-call(bf16[768,2048]{1,0:T(8,128)(2,1)} %get-tuple-element.70.a1_ref, bf16[768,2048]{1,0:T(8,128)(2,1)} %get-tuple-element.71.a2_ref, ...), custom_call_target="tpu_custom_call" | custom-call | tf_op jit(solution)/shard_map/outers/pallas_call | solution.py:1023
  304.7 148.7 %attend_back.1 = (bf16[1,2048,768]{2,1,0:T(8,128)(2,1)}, bf16[1,2048,768]{2,1,0:T(8,128)(2,1)}, bf16[1,2048,768]{2,1,0:T(8,128)(2,1)}, f32[48,1536]{1,0:T(8,128)...) custom-call(bf16[1,2048,768]{2,1,0:T(8,128)(2,1)} %bitcast.28, bf16[1,2048,768]{2,1,0:T(8,128)(2,1)} %bitcast.30, ...), custom_call_target="tpu_custom_call" | custom-call | tf_op jit(solution)/shard_map/attend_back/pallas_call | solution.py:776
  453.4 56.5 %closing.1 = (bf16[2,1024,768]{2,1,0:T(8,128)(2,1)}, f32[24,2304]{1,0:T(8,128)}) custom-call(bf16[2048,768]{1,0:T(8,128)(2,1)} %bitcast.43, bf16[2048,768]{1,0:T(8,128)(2,1)} %bitcast.44, bf16[2048,768]{1,0:T(8,128)(2,1)} %bitcast.45, bf16[2048,768]{1,0:T(8,128)(2,1)} %get-tuple-element.76.b4_ref.first_hbm, bf16[768,2048]{1,0:T(8,128)(2,1)} %get-tuple-element.90.xt_hbm, ...), custom_call_target="tpu_custom_call" | custom-call | tf_op jit(solution)/shard_map/closing/pallas_call | solution.py:1155
  509.8 0.7 slice_reduce_fusion.2
  510.5 0.6 slice.24
  511.2 1.7 copy.38
  512.9 1.4 copy-done.1
  514.2 1.7 copy.39
  515.9 0.0 copy-done.5
  515.9 0.7 copy.40
  516.6 0.0 copy-done.4
  516.6 0.7 copy.41
  517.3 0.0 copy-done.3
  517.3 0.7 copy.42
  518.0 0.7 copy.43
  (11 shorter events, 0.0 us)
Async XLA Ops:
  453.3 56.5 %copy-start.6 = (f32[24,896]{1,0:T(8,128)S(1)}, f32[24,896]{1,0:T(8,128)}, u32[]{:S(2)}) copy-start(f32[24,896]{1,0:T(8,128)} %get-tuple-element.93) | copy-start | bytes 258052
  453.4 57.8 %copy-start = (bf16[2,1024,768]{2,1,0:T(8,128)(2,1)S(1)}, bf16[2,1024,768]{2,1,0:T(8,128)(2,1)}, u32[]{:S(2)}) copy-start(bf16[2,1024,768]{2,1,0:T(8,128)(2,1)} %get-tuple-element.110) | copy-start | bytes 9437188
  511.2 3.0 copy-start.1
  514.2 1.7 copy-start.5
  514.2 2.4 copy-start.4
  514.2 3.1 copy-start.3
  514.2 3.8 copy-start.2

commit v7 on v6

--- a/solution.py
+++ b/solution.py
@@ -185,14 +185,14 @@
         x, y, z = self.me["x"], self.me["y"], self.me["z"]
         for copy in self.copies(stage - 1):
             copy.wait_recv()
-        b, kind = self.b, self.b.dtype
+        b = self.b
         if stage == 1:
             for copy in self.mine():
                 copy.wait()
 
             def add(i, _):
                 at = (i // 4, i % 4)
-                b[at] = (b[at].astype(F32) + self.r0[at].astype(F32)).astype(kind)
+                b[at] = b[at] + self.r0[at]
                 return 0
 
             lax.fori_loop(0, 8, add, 0)
@@ -201,17 +201,17 @@
             def add(i, _):
                 if self.order[0] == "y":
                     for j in range(2):
-                        b[y, i, j] = (b[y, i, j].astype(F32) + self.r1[i, j].astype(F32)).astype(kind)
+                        b[y, i, j] = b[y, i, j] + self.r1[i, j]
                 else:
                     for j in range(2):
-                        b[j, i, x] = (b[j, i, x].astype(F32) + self.r1[j, i].astype(F32)).astype(kind)
+                        b[j, i, x] = b[j, i, x] + self.r1[j, i]
                 return 0
 
             lax.fori_loop(0, 4, add, 0)
         if stage == 3:
 
             def add(i, _):
-                b[y, i, x] = (b[y, i, x].astype(F32) + self.r2[i].astype(F32)).astype(kind)
+                b[y, i, x] = b[y, i, x] + self.r2[i]
                 return 0
 
             lax.fori_loop(0, 4, add, 0)
@@ -280,87 +280,13 @@
         self.keep_out().wait()
 
 
-OPENING_ORDERS = ("yzxc", "zyxc", "z", "z")
-
-
-def opening_kernel(tok_ref, qkv_ref, *rest):
-    early, rest = rest[:2], rest[2:]
-    x_ref, full_ref, rest = rest[0], rest[1], rest[2:]
-    early_out, (bounce, send, recv, local) = rest[:2], rest[2:]
-    me = place()
-    greet(me)
-    rows = tok_ref.shape[1]
-    swap = Swap(me, tok_ref, x_ref, bounce, send, recv, local.at[0], 0, ((0, rows // 8), (rows // 8, rows - rows // 8)))
-    half = qkv_ref.shape[-1] // 2
-    sources = [(qkv_ref.at[:, pl.ds(n * half, half)], full_ref, (n * half, half)) for n in range(2)]
-    sources += [(a, b, None) for a, b in zip(early, early_out)]
-    gathers, base = [], 2
-    for i, (source, full, columns) in enumerate(sources):
-        order = OPENING_ORDERS[i]
-        gathers.append(
-            Gather(me, source, full, send, recv, local.at[1 + i], base, order, "", columns)
-        )
-        base += Gather.sems(order)
-    first, second, later = gathers[0], gathers[1], gathers[2:]
-    first.start()
-    second.start()
-    swap.give(0)
-    swap.keep_begin()
-    first.step(1)
-    second.step(1)
-    swap.give(1)
-    swap.keep_turn()
-    first.step(2)
-    for g in later:
-        g.start()
-    second.step(2)
-    first.step(3)
-    second.step(3)
-    first.step(4)
-    second.step(4)
-    for g in later:
-        g.step(1)
-    for g in gathers:
-        g.finish()
-    swap.finish()
-
-
-def opening_call(tokens, w_qkv, early):
-    hbm = pl.BlockSpec(memory_space=pl.ANY)
-    sems = 2 + sum(map(Gather.sems, OPENING_ORDERS))
-    return pl.pallas_call(
-        opening_kernel,
-        in_specs=[hbm] + [pl.BlockSpec(memory_space=pltpu.VMEM)] * 3,
-        out_specs=[hbm] * 4,
-        out_shape=[
-            jax.ShapeDtypeStruct(tokens.shape, BF),
-            jax.ShapeDtypeStruct((4, 2, 2, 2) + w_qkv.shape, BF),
-        ]
-        + [jax.ShapeDtypeStruct((4,) + a.shape, BF) for a in early],
-        scratch_shapes=[
-            pltpu.VMEM(tokens.shape[1:], BF),
-            pltpu.SemaphoreType.DMA((sems,)),
-            pltpu.SemaphoreType.DMA((sems,)),
-            pltpu.SemaphoreType.DMA((5,)),
-        ],
-        compiler_params=pltpu.CompilerParams(
-            vmem_limit_bytes=VMEM_LIMIT, collective_id=0, has_side_effects=True
-        ),
-        name="opening",
-    )(tokens, w_qkv, *early)
-
-
-QKV_ORDERS = ("y", "x", "z", "y", "x")
-QKV_HELD = ("z", "z", "", "", "")
-
-
 def halves(ref):
     half = ref.shape[-1] // 2
-    return [ref.at[:, pl.ds(n * half, half)] for n in range(2)]
-
-
-def stages(me, shards, fulls, orders, held, columns, send, recv, local):
-    out, base = [], 0
+    return [ref.at[(slice(None),) * (len(ref.shape) - 1) + (pl.ds(n * half, half),)] for n in range(2)]
+
+
+def stages(me, shards, fulls, orders, held, columns, send, recv, local, base=0):
+    out = []
     for i, order in enumerate(orders):
         out.append(
             Gather(me, shards[i], fulls[i], send, recv, local.at[i], base, order, held[i], columns[i])
@@ -369,25 +295,9 @@
     return out
 
 
-def qkv_kernel(moves, x_ref, w_ref, cos_ref, sin_ref, *rest):
-    shards, rest = rest[:moves], rest[moves:]
-    q_ref, k_ref, v_ref, xt_ref, rest = rest[0], rest[1], rest[2], rest[3], rest[4:]
-    if moves:
-        fulls, (send, recv, local) = rest[:5], rest[5:]
-        me = place()
-        shards = list(shards[:3]) + halves(shards[3])
-        gathers = stages(me, shards, fulls, QKV_ORDERS, QKV_HELD, (None,) * 5, send, recv, local)
-
-        @pl.when(pl.program_id(0) == 0)
-        def _():
-            greet(me)
-            for i in (3, 4, 0, 1, 2):
-                gathers[i].start()
-
-    x = x_ref[...]
+def project(x, w_ref, cosine, sine, put):
     width = x.shape[1]
-    cosine, sine = cos_ref[...], sin_ref[...]
-    for part, out in ((0, q_ref), (1, k_ref), (2, v_ref)):
+    for part in range(3):
         for pair in range(width // PAIR):
             at = part * width + pair * PAIR
             if pair % 2 == 0:
@@ -397,57 +307,188 @@
                 u = u * cosine + turn(u) * sine
             if part == 0:
                 u = u * (0.125 * LOG2E)
-            out[:, pair * PAIR : (pair + 1) * PAIR] = u.astype(BF)
+            put(part, slice(pair * PAIR, (pair + 1) * PAIR), u.astype(BF))
+
+
+def qkv_kernel(x_ref, w_ref, cos_ref, sin_ref, q_ref, k_ref, v_ref, xt_ref):
+    x = x_ref[...]
+
+    def put(part, columns, value):
+        (q_ref, k_ref, v_ref)[part][:, columns] = value
+
+    project(x, w_ref, cos_ref[...], sin_ref[...], put)
     xt_ref[...] = x.T
-    if moves:
-
-        @pl.when(pl.program_id(0) == pl.num_programs(0) - 1)
-        def _():
-            for g in gathers:
-                g.step(1)
-            for g in gathers:
-                g.finish()
-
-
-def qkv_call(x, w, cosine, sine, moving=(), tile=512):
+
+
+def qkv_call(x, w, cosine, sine, tile=512):
     tokens, width = x.shape
     span = cosine.shape[0]
     tile = min(tile, span)
-    moves = len(moving)
     row = pl.BlockSpec((tile, width), lambda i: (i, 0))
     table = pl.BlockSpec((tile, PAIR), lambda i: (i % (span // tile), 0))
-    results, extra, more = [], [], {}
-    if moves:
-        for i, order in enumerate(QKV_ORDERS):
-            a = moving[min(i, 3)]
-            spans = tuple(SIZE[n] for n in AXES if n in QKV_HELD[i] + order)
-            block = (a.shape[-2], a.shape[-1] // (2 if i >= 3 else 1))
-            results.append(jax.ShapeDtypeStruct(spans + block, BF))
-        sems = sum(map(Gather.sems, QKV_ORDERS))
-        extra = [pltpu.SemaphoreType.DMA((n,)) for n in (sems, sems, len(QKV_ORDERS))]
-        more = dict(collective_id=6, has_side_effects=True)
     return pl.pallas_call(
-        functools.partial(qkv_kernel, moves),
+        qkv_kernel,
         grid=(tokens // tile,),
         in_specs=[
             row,
             pl.BlockSpec(w.shape, lambda i: (0, 0), pipeline_mode=pl.Buffered(1)),
             table,
             table,
-        ]
-        + [
-            pl.BlockSpec(a.shape, lambda i, n=a.ndim: (0,) * n, pipeline_mode=pl.Buffered(1))
-            for a in moving
         ],
-        out_specs=[row, row, row, pl.BlockSpec((width, tile), lambda i: (0, i))]
-        + [pl.BlockSpec(memory_space=pl.ANY)] * len(results),
+        out_specs=[row, row, row, pl.BlockSpec((width, tile), lambda i: (0, i))],
         out_shape=[jax.ShapeDtypeStruct((tokens, width), BF)] * 3
-        + [jax.ShapeDtypeStruct((width, tokens), BF)]
-        + results,
-        scratch_shapes=extra,
-        compiler_params=pltpu.CompilerParams(vmem_limit_bytes=VMEM_LIMIT, **more),
+        + [jax.ShapeDtypeStruct((width, tokens), BF)],
+        compiler_params=params(),
         name="qkv",
-    )(x, w, cosine, sine, *moving)
+    )(x, w, cosine, sine)
+
+
+OPENING_ORDERS = ("yzxc", "zyxc", "zy", "zx", "z", "y", "x")
+
+
+def opening_kernel(
+    tok_hbm, w_shard, out_shard, gate_shard, up_shard, down_shard, cos_ref, sin_ref,
+    x_hbm, w_hbm, q_hbm, k_hbm, v_hbm, xt_hbm, out_part, gate_part, up_part, left_part, right_part,
+    x, w_blocks, w, q, k, v, xt, send, recv, local, load, store,
+):
+    me = place()
+    y = me["y"]
+    greet(me)
+    rows = x.shape[1]
+    begin = rows // 8
+    parts = ((0, begin), (begin, rows - begin))
+
+    def token_copy(n, row, half):
+        part = pl.ds(*parts[n])
+        return pltpu.make_async_remote_copy(
+            src_ref=tok_hbm.at[row, part],
+            dst_ref=x.at[half, part],
+            send_sem=send.at[n],
+            recv_sem=recv.at[n],
+            device_id=device(moved(me, "y", 1)),
+            device_id_type=MESH,
+        )
+
+    width = w.shape[1] // 2
+    g = stages(
+        me,
+        halves(w_shard) + [out_shard, gate_shard, up_shard] + halves(down_shard),
+        [w_blocks, w_blocks, out_part, gate_part, up_part, left_part, right_part],
+        OPENING_ORDERS,
+        ("",) * 7,
+        ((0, width), (width, width)) + (None,) * 5,
+        send, recv, local, 2,
+    )
+    mine = pltpu.make_async_copy(tok_hbm.at[y], x.at[y], load.at[0])
+    g[0].start()
+    g[1].start()
+    token_copy(0, 1 - y, y).start()
+    mine.start()
+    g[0].step(1)
+    g[1].step(1)
+    token_copy(1, 1 - y, y).start()
+    g[0].step(2)
+    for n in (2, 3, 4):
+        g[n].start()
+    g[1].step(2)
+    g[6].start()
+    g[5].start()
+    g[0].step(3)
+    g[1].step(3)
+    g[0].step(4)
+    g[1].step(4)
+    g[2].step(1)
+    g[3].step(1)
+    for n in range(3):
+        part = slice(n * w.shape[0], (n + 1) * w.shape[0])
+        block = w_blocks[:, :, :, :, :, part].astype(F32)
+        w[:, part] = block.reshape(w.shape[0], w.shape[0]).astype(BF)
+    keep_w = pltpu.make_async_copy(w, w_hbm, load.at[1])
+    keep_w.start()
+    mine.wait()
+    tile = 512
+
+    def stores(n):
+        half = lax.rem(y + n // 2, 2)
+        at = pl.ds(pl.multiple_of(half * rows + lax.rem(n, 2) * tile, tile), tile)
+        pairs = [(a.at[at], b.at[at]) for a, b in ((q, q_hbm), (k, k_hbm), (v, v_hbm))]
+        pairs.append((xt.at[:, at], xt_hbm.at[:, at]))
+        return [pltpu.make_async_copy(a, b, store.at[n, i]) for i, (a, b) in enumerate(pairs)]
+
+    def tile_step(n, _):
+        half = lax.rem(y + n // 2, 2)
+        start = pl.multiple_of(half * rows + lax.rem(n, 2) * tile, tile)
+        at = pl.ds(start, tile)
+
+        @pl.when(n == 2)
+        def _():
+            for m in range(2):
+                token_copy(m, 1 - y, 1 - y).wait_recv()
+
+        value = x[half, pl.ds(pl.multiple_of(lax.rem(n, 2) * tile, tile), tile), :]
+
+        def put(part, columns, u):
+            (q, k, v)[part][at, columns] = u
+
+        project(value, w, cos_ref[at, :], sin_ref[at, :], put)
+        xt[:, at] = value.T
+        for copy in stores(n):
+            copy.start()
+        return 0
+
+    lax.fori_loop(0, 4, tile_step, 0)
+    keep_x = pltpu.make_async_copy(x, x_hbm, load.at[2])
+    keep_x.start()
+    g[2].step(2)
+    g[3].step(2)
+    for n in (4, 5, 6):
+        g[n].step(1)
+    for gather in g:
+        gather.finish()
+    for m in range(2):
+        token_copy(m, 1 - y, y).wait_send()
+    for n in range(4):
+        for copy in stores(n):
+            copy.wait()
+    keep_w.wait()
+    keep_x.wait()
+
+
+def opening_call(tokens, w_qkv, w_out, w_gate, w_up, w_down, cosine, sine):
+    rows, span, width = tokens.shape
+    total = rows * span
+    hbm = pl.BlockSpec(memory_space=pl.ANY)
+    held = pl.BlockSpec(memory_space=pltpu.VMEM)
+    whole = (width, w_qkv.shape[1])
+    flat = (total, width)
+    shapes = [tokens.shape, whole, flat, flat, flat, (width, total)]
+    shapes += [(4, 2) + w_out.shape, (4, 2) + w_gate.shape, (4,) + w_up.shape]
+    shapes += [(2, w_down.shape[0], w_down.shape[1] // 2)] * 2
+    sems = 2 + sum(map(Gather.sems, OPENING_ORDERS))
+    return pl.pallas_call(
+        opening_kernel,
+        in_specs=[hbm] + [held] * 7,
+        out_specs=[hbm] * len(shapes),
+        out_shape=[jax.ShapeDtypeStruct(shape, BF) for shape in shapes],
+        scratch_shapes=[
+            pltpu.VMEM(tokens.shape, BF),
+            pltpu.VMEM((4, 2, 2, 2) + w_qkv.shape, BF),
+            pltpu.VMEM(whole, BF),
+            pltpu.VMEM(flat, BF),
+            pltpu.VMEM(flat, BF),
+            pltpu.VMEM(flat, BF),
+            pltpu.VMEM((width, total), BF),
+            pltpu.SemaphoreType.DMA((sems,)),
+            pltpu.SemaphoreType.DMA((sems,)),
+            pltpu.SemaphoreType.DMA((len(OPENING_ORDERS),)),
+            pltpu.SemaphoreType.DMA((3,)),
+            pltpu.SemaphoreType.DMA((4, 4)),
+        ],
+        compiler_params=pltpu.CompilerParams(
+            vmem_limit_bytes=VMEM_LIMIT, collective_id=0, has_side_effects=True
+        ),
+        name="opening",
+    )(tokens, w_qkv, w_out, w_gate, w_up, w_down, cosine, sine)
 
 
 def attend_kernel(tile, chunk, moves, q_ref, k_ref, v_ref, bias_ref, *rest):
@@ -555,7 +596,7 @@
 
 ATTEND_HELD = ("zy", "zx", "z", "y", "x")
 ATTEND_ORDERS = ("xc", "yc", "yxc", "zxc", "zyc")
-ATTEND_PLAN = ((2, 0, 1), (4, 2, 1), (4, 3, 1), (7, 4, 1), (10, 1, 1), (10, 2, 2))
+ATTEND_PLAN = ((2, 0, 1), (4, 2, 1), (4, 3, 1), (7, 4, 1), (10, 1, 1), (10, 2, 2), (11, 3, 2), (11, 4, 2))
 ATTEND_FIRST = (2, 1, 0, 3, 4)
 
 
@@ -967,12 +1008,29 @@
     )(a, b)
 
 
-def outers_kernel(steps, moves, a1_ref, a2_ref, a3_ref, b1_ref, b2_ref, b3_ref, b4_ref, gains_ref, *rest):
+def outers_kernel(steps, moves, a1_ref, a2_hbm, a3_hbm, b1_ref, b2_ref, b3_ref, b4_hbm, gains_ref, *rest):
     source, rest = rest[:moves], rest[moves:]
     o1_ref, o2_ref, o3_ref, o4_ref, rest = rest[0], rest[1], rest[2], rest[3], rest[4:]
     now = pl.program_id(0)
+    target, rest = rest[:moves], rest[moves:]
+    a2_ref, a3_ref, b4_ref, load, rest = rest[0], rest[1], rest[2], rest[3], rest[4:]
+    late = [
+        pltpu.make_async_copy(a, b, load.at[i])
+        for i, (a, b) in enumerate(((a2_hbm, a2_ref), (a3_hbm, a3_ref), (b4_hbm, b4_ref)))
+    ]
+
+    @pl.when(now == 0)
+    def _():
+        for copy in late:
+            copy.start()
+
+    @pl.when(now == 2 * steps)
+    def _():
+        for copy in late:
+            copy.wait()
+
     if moves:
-        target, bounce, send, recv, local = rest
+        target, (bounce, send, recv, local) = target[0], rest
         me = place()
         swap = Swap(me, source[0], target, bounce, send, recv, local.at[0], 0, ((0, target.shape[1]),))
 
@@ -1017,15 +1075,14 @@
 
     moves = len(moving)
     hbm = pl.BlockSpec(memory_space=pl.ANY)
-    extra = [pltpu.VMEM(a.shape[1:], BF) for a in moving]
+    extra = [pltpu.VMEM(a.shape, BF) for a in (df_t, att_t, d_first)] + [pltpu.SemaphoreType.DMA((3,))]
+    extra += [pltpu.VMEM(a.shape[1:], BF) for a in moving]
     extra += [pltpu.SemaphoreType.DMA((1,))] * (3 * moves)
     more = dict(collective_id=4, has_side_effects=True) if moves else {}
     return pl.pallas_call(
         functools.partial(outers_kernel, steps, moves),
         grid=(3 * steps + 1,),
-        in_specs=[whole(h_t), whole(df_t), whole(att_t)]
-        + [part(tokens, n) for n in range(3)]
-        + [whole(d_first), whole(gains)]
+        in_specs=[whole(h_t), hbm, hbm] + [part(tokens, n) for n in range(3)] + [hbm, whole(gains)]
         + [hbm] * moves,
         out_specs=[part(width, n) for n in range(3)]
         + [pl.BlockSpec((width, width + gains.shape[1]), lambda i: (0, 0), pipeline_mode=pl.Buffered(1))]
@@ -1218,9 +1275,10 @@
     gains = jnp.stack([gain_one, gain_two], 1)
     if own:
         w_out = jnp.pad(jnp.concatenate([w_out, gains], 1), ((0, 0), (0, PAIR - 2)))
-        x, f_qkv, w_out, w_gate = opening_call(tokens, w_qkv, (w_out, w_gate))
+        x, f_qkv, q, k, v, xt, *moving = opening_call(
+            tokens, w_qkv, w_out, w_gate, w_up, w_down, cosine, sine
+        )
         x = x.reshape(1, seq, width)
-        f_qkv = f_qkv.reshape(width, -1)
         length = lax.dynamic_slice_in_dim(lengths, mine, 1, 0)
         cq, sq = cosine, sine
     else:
@@ -1231,9 +1289,8 @@
         sq = lax.dynamic_slice_in_dim(sine, mine * span, span, 0)
     n, t = x.shape[:2]
     flat = x.reshape(n * t, width)
-    q, k, v, xt, *moving = qkv_call(
-        flat, f_qkv, cq, sq, (w_out, w_gate, w_up, w_down) if own else ()
-    )
+    if not own:
+        q, k, v, xt = qkv_call(flat, f_qkv, cq, sq)
     q, k, v = (a.reshape(n, t, width) for a in (q, k, v))
     if not own:
         k = lax.all_gather(k, "blk", axis=1, tiled=True)

time: 527 us -> 508 us (0.964)
  Pallas kernels: 499 us -> 480 us
    pallas_call x2 -> x1, Pallas kernels: 70.7 us -> 58.9 us  [opening_call(): pl.pallas_call(opening_kernel, in_specs=[hbm] + [held] * 7, out_specs=[hb...]
where the time goes in v7:
time: 508 us; the launch traced here: 500 us
  Pallas kernels  480 us (94%)
  local copies, waits for them, and re-layouts  14.1 us (3%)
    pallas_call x1, Pallas kernels, attend_back_call(): pl.pallas_call(functools.partial(attend_back_kernel, tq, unroll, moves),...  147 us
    pallas_call x1, Pallas kernels, middle_call(): pl.pallas_call(functools.partial(middle_kernel, chunk, moves), grid=(toke...  97 us
    pallas_call x1, Pallas kernels, attend_call(): pl.pallas_call(functools.partial(attend_kernel, tile, chunk, moves), grid...  75.1 us
    pallas_call x1, Pallas kernels, opening_call(): pl.pallas_call(opening_kernel, in_specs=[hbm] + [held] * 7, out_specs=[hb...  58.9 us
    pallas_call x1, Pallas kernels, closing_call(): pl.pallas_call(closing_kernel, in_specs=[hbm] * 6, out_specs=[hbm, pl.Blo...  55.2 us
    pallas_call x1, Pallas kernels, outers_call(): pl.pallas_call(functools.partial(outers_kernel, steps, moves), grid=(3 *...  47 us

profile of v7, /device:TPU:0, one launch (start us, length us, event | category | flops | bytes accessed | tf_op | source)
XLA Modules:
  0.0 500.2 jit_solution(3058733250631918501)
XLA Ops:
  0.6 1.2 dynamic_slice.3
  1.9 0.7 iota_compare_fusion.1
  2.6 0.7 copy.29
  3.3 0.7 copy.30
  4.0 1.5 fusion.4.out_shard
  5.5 1.1 select_convert_fusion.bias_ref
  6.6 58.9 %opening.1 = (bf16[2,1024,768]{2,1,0:T(8,128)(2,1)}, bf16[768,2304]{1,0:T(8,128)(2,1)}, bf16[2048,768]{1,0:T(8,128)(2,1)}, bf16[2048,768]{1,0:T(8,128)(2,1)}, bf...) custom-call(bf16[2,1024,768]{2,1,0:T(8,128)(2,1)} %tok_hbm.1, ...), custom_call_target="tpu_custom_call" | custom-call | tf_op jit(solution)/shard_map/opening/pallas_call | solution.py:468
  65.5 75.1 %attend.1 = (bf16[1,2048,768]{2,1,0:T(8,128)(2,1)}, bf16[1,2048,768]{2,1,0:T(8,128)(2,1)}, bf16[4,2,2,2,24,896]{5,4,3,2,1,0:T(8,128)(2,1)}, bf16[4,2,2,2,24,3072...) custom-call(bf16[1,2048,768]{2,1,0:T(8,128)(2,1)} %bitcast.24, ...), custom_call_target="tpu_custom_call" | custom-call | tf_op jit(solution)/shard_map/attend/pallas_call | solution.py:652
  140.7 1.0 slice_convert_fusion
  141.6 0.4 slice_reduce_fusion
  142.0 0.6 broadcast_in_dim_squeeze.7.g2_ref
  142.6 0.6 broadcast_in_dim_squeeze.6.g1_ref
  143.2 97.0 %middle.1 = (bf16[2048,768]{1,0:T(8,128)(2,1)}, bf16[2048,768]{1,0:T(8,128)(2,1)}, bf16[2048,768]{1,0:T(8,128)(2,1)}, bf16[2048,3072]{1,0:T(8,128)(2,1)}, bf16[2...) custom-call(bf16[2048,768]{1,0:T(8,128)(2,1)} %bitcast.37, ...), custom_call_target="tpu_custom_call" | custom-call | tf_op jit(solution)/shard_map/middle/pallas_call | solution.py:973
  240.1 0.7 pad_maximum_fusion
  240.8 0.2 copy.31
  241.0 0.8 pad.9.gains_ref
  241.8 47.0 %outers.1 = (bf16[768,3072]{1,0:T(8,128)(2,1)}, bf16[768,3072]{1,0:T(8,128)(2,1)}, bf16[768,3072]{1,0:T(8,128)(2,1)}, f32[768,896]{1,0:T(8,128)}, bf16[2,1024,768]{2,1,0:T(8,128)(2,1)}) custom-call(bf16[768,2048]{1,0:T(8,128)(2,1)} %get-tuple-element.65.a1_ref, bf16[768,2048]{1,0:T(8,128)(2,1)} %get-tuple-element.66.a2_hbm, ...), custom_call_target="tpu_custom_call" | custom-call | tf_op jit(solution)/shard_map/outers/pallas_call | solution.py:1082
  288.8 146.9 %attend_back.1 = (bf16[1,2048,768]{2,1,0:T(8,128)(2,1)}, bf16[1,2048,768]{2,1,0:T(8,128)(2,1)}, bf16[1,2048,768]{2,1,0:T(8,128)(2,1)}, f32[48,1536]{1,0:T(8,128)...) custom-call(bf16[1,2048,768]{2,1,0:T(8,128)(2,1)} %bitcast.25, bf16[1,2048,768]{2,1,0:T(8,128)(2,1)} %bitcast.27, ...), custom_call_target="tpu_custom_call" | custom-call | tf_op jit(solution)/shard_map/attend_back/pallas_call | solution.py:817
  435.7 0.0 copy-start.6
  435.8 0.0 copy-start
  435.8 55.2 %closing.1 = (bf16[2,1024,768]{2,1,0:T(8,128)(2,1)}, f32[24,2304]{1,0:T(8,128)}) custom-call(bf16[2048,768]{1,0:T(8,128)(2,1)} %bitcast.39, bf16[2048,768]{1,0:T(8,128)(2,1)} %bitcast.40, bf16[2048,768]{1,0:T(8,128)(2,1)} %bitcast.41, bf16[2048,768]{1,0:T(8,128)(2,1)} %get-tuple-element.71.b4_hbm.first_hbm, bf16[768,2048]{1,0:T(8,128)(2,1)} %get-tuple-element.85.xt_hbm, ...), custom_call_target="tpu_custom_call" | custom-call | tf_op jit(solution)/shard_map/closing/pallas_call | solution.py:1212
  490.9 0.0 copy-done.6
  490.9 0.7 slice_reduce_fusion.2
  491.6 0.6 slice.24
  492.3 0.0 copy-done
  492.3 1.7 copy.38
  493.9 1.4 copy-done.1
  495.3 1.7 copy.39
  497.0 0.7 copy.40
  497.7 0.7 copy.41
  498.4 0.7 copy.42
  499.1 0.7 copy.43
  (10 shorter events, 0.0 us)
Async XLA Ops:
  435.7 55.2 %copy-start.6 = (f32[24,896]{1,0:T(8,128)S(1)}, f32[24,896]{1,0:T(8,128)}, u32[]{:S(2)}) copy-start(f32[24,896]{1,0:T(8,128)} %get-tuple-element.89) | copy-start | bytes 258052
  435.8 56.5 %copy-start = (bf16[2,1024,768]{2,1,0:T(8,128)(2,1)S(1)}, bf16[2,1024,768]{2,1,0:T(8,128)(2,1)}, u32[]{:S(2)}) copy-start(bf16[2,1024,768]{2,1,0:T(8,128)(2,1)} %get-tuple-element.106) | copy-start | bytes 9437188
  492.3 3.0 copy-start.1
  495.3 1.7 copy-start.5
  495.3 2.4 copy-start.4
  495.3 3.1 copy-start.3
  495.3 3.8 copy-start.2

commit v8 on v7

--- a/solution.py
+++ b/solution.py
@@ -166,6 +166,15 @@
         if stage == 0:
             other = 1 - self.me["c"]
             return [self.copy(self.piece(other, i), self.r0.at[i], i, "c") for i in range(2)]
+        if self.order[0] == "z":
+            if stage == 1:
+                return [
+                    self.copy(self.b.at[:, lax.rem(z + d, 4)], self.r1.at[d - 1], 3 + d, "z", d)
+                    for d in range(1, 4)
+                ]
+            if stage == 2:
+                return [self.copy(self.b.at[1 - y, z], self.r2, 2, "y")]
+            return [self.copy(self.b.at[y, z, 1 - x], self.r3, 3, "x")]
         if stage == 1:
             source = self.b.at[1 - y] if self.order[0] == "y" else self.b.at[:, :, 1 - x]
             return [self.copy(source, self.r1, 2, self.order[0])]
@@ -196,6 +205,27 @@
                 return 0
 
             lax.fori_loop(0, 8, add, 0)
+        if self.order[0] == "z" and stage > 1:
+            if stage == 2:
+
+                def add(i, _):
+                    at = (i // 2, i % 2)
+                    total = b[at[0], z, at[1]].astype(F32)
+                    for d in range(3):
+                        total = total + self.r1[d, at[0], at[1]].astype(F32)
+                    b[at[0], z, at[1]] = total.astype(b.dtype)
+                    return 0
+
+                lax.fori_loop(0, 4, add, 0)
+            if stage == 3:
+                for i in range(2):
+                    b[y, z, i] = b[y, z, i] + self.r2[i]
+            if stage == 4:
+                self.out[...] = b[y, z, x].astype(F32) + self.r3[...].astype(F32)
+                return
+            for copy in self.copies(stage):
+                copy.start()
+            return
         if stage == 2:
 
             def add(i, _):
@@ -231,6 +261,11 @@
 
     @staticmethod
     def scratch(rows, columns, kind, order):
+        if order[0] == "z":
+            return [
+                pltpu.VMEM(shape + (rows, columns), kind)
+                for shape in ((2, 4, 2), (2, 4, 2), (3, 2, 2), (2,), ())
+            ]
         lead = (4, 2) if order[0] == "y" else (2, 4)
         return [
             pltpu.VMEM(shape + (rows, columns), kind)
@@ -491,7 +526,14 @@
     )(tokens, w_qkv, w_out, w_gate, w_up, w_down, cosine, sine)
 
 
-def attend_kernel(tile, chunk, moves, q_ref, k_ref, v_ref, bias_ref, *rest):
+def key_mask(len_ref, own, keys, other):
+    length = len_ref[lax.axis_index("blk") if own else pl.program_id(0)]
+    sub = lanes((keys, PAIR)) % HEAD
+    past = lax.broadcasted_iota(jnp.int32, (keys, PAIR), 0) >= length
+    return jnp.where(sub < 3, other, jnp.where((sub == 3) & past, NEG, 0.0))
+
+
+def attend_kernel(tile, chunk, moves, len_ref, q_ref, k_ref, v_ref, *rest):
     inputs, rest = rest[:moves], rest[moves:]
     o_ref, aug_ref, rest = rest[0], rest[1], rest[2:]
     results = max(moves - 1, 0)
@@ -505,7 +547,7 @@
 
     @pl.when(pl.program_id(1) == 0)
     def _():
-        ka[:, PAIR:] = bias_ref[0]
+        ka[:, PAIR:] = key_mask(len_ref, moves, keys, 0.0).astype(BF)
         va[:, PAIR:] = jnp.ones((keys, PAIR), BF)
 
     ka[:, :PAIR] = k_ref[0]
@@ -631,7 +673,7 @@
     ).astype(BF)
 
 
-def attend_call(q, k, v, bias, moving=(), tile=512, chunk=512):
+def attend_call(q, k, v, lengths, moving=(), tile=512, chunk=512):
     rows, span, width = q.shape
     keys = k.shape[1]
     tile = min(tile, span)
@@ -652,8 +694,7 @@
     return pl.pallas_call(
         functools.partial(attend_kernel, tile, chunk, moves),
         grid=(rows, width // PAIR),
-        in_specs=[qs, ks, ks, pl.BlockSpec((1, keys, PAIR), lambda r, p: (r, 0, 0))]
-        + held,
+        in_specs=[pl.BlockSpec(memory_space=pltpu.SMEM), qs, ks, ks] + held,
         out_specs=[qs, qs] + [hbm] * len(moved_shapes),
         out_shape=[jax.ShapeDtypeStruct(q.shape, BF)] * 2 + moved_shapes,
         scratch_shapes=[
@@ -665,11 +706,11 @@
         + (extra if moves else []),
         compiler_params=pltpu.CompilerParams(vmem_limit_bytes=VMEM_LIMIT, **more),
         name="attend",
-    )(q, k, v, bias, *moving)
+    )(lengths, q, k, v, *moving)
 
 
 def attend_back_kernel(
-    tq, unroll, moves, q_ref, k_ref, v_ref, bias_ref, o_ref, do_ref, aug_ref, cos_ref, sin_ref, *rest
+    tq, unroll, moves, len_ref, q_ref, k_ref, v_ref, o_ref, do_ref, aug_ref, cos_ref, sin_ref, *rest
 ):
     inputs, rest = rest[:moves], rest[moves:]
     dq_ref, dk_ref, dv_ref, rest = rest[0], rest[1], rest[2], rest[3:]
@@ -683,9 +724,8 @@
 
     @pl.when(pl.program_id(1) == 0)
     def _():
-        minus = jnp.where(lanes((keys, PAIR)) % HEAD < 3, -1.0, 0.0)
-        ka[:, PAIR:] = (minus + bias_ref[0].astype(F32)).astype(BF)
-        va[:, PAIR:] = minus.astype(BF)
+        ka[:, PAIR:] = key_mask(len_ref, moves, keys, -1.0).astype(BF)
+        va[:, PAIR:] = jnp.where(lanes((keys, PAIR)) % HEAD < 3, -1.0, 0.0).astype(BF)
 
     k, do = k_ref[0], do_ref[0]
     ka[:, :PAIR] = k
@@ -766,11 +806,12 @@
     return lambda c, y: source.at[:, :, c, y]
 
 
-BACK_ORDERS = ("yx", "yx", "xy", "xy")
+BACK_ORDERS = ("yx", "xy", "zyx", "xy")
 BACK_PLAN = (
-    (1, 0, 1), (1, 2, 1), (1, 1, 1), (1, 3, 1), (3, 0, 2), (3, 2, 2), (3, 3, 2), (4, 0, 3), (4, 2, 3), (4, 1, 2),
-    (5, 1, 3), (5, 3, 3), (5, 0, 4),
+    (1, 0, 1), (1, 1, 1), (1, 2, 1), (1, 3, 1), (3, 0, 2), (3, 1, 2), (3, 3, 2), (4, 0, 3), (4, 1, 3), (4, 2, 2),
+    (4, 3, 3), (5, 0, 4), (5, 2, 3),
 )
+BACK_LAST = (2, 1, 3)
 
 
 def back_events(inputs, outputs, send, recv, local, *bufs):
@@ -785,15 +826,15 @@
             )
         )
     events = Events()
-    events.put(0, functools.partial(greet, me), *(reduces[i].start for i in (0, 2, 1, 3)))
+    events.put(0, functools.partial(greet, me), *(reduces[i].start for i in (2, 0, 1, 3)))
     for at, i, stage in BACK_PLAN:
         events.put(at, functools.partial(reduces[i].step, stage))
-    events.last += [functools.partial(reduces[i].step, 4) for i in (2, 1, 3)]
+    events.last += [functools.partial(reduces[i].step, 4) for i in BACK_LAST]
     events.last += [r.finish for r in reduces]
     return events
 
 
-def attend_back_call(q, k, v, bias, o, do, aug, cosine, sine, whole, moving=(), tq=512, unroll=4):
+def attend_back_call(q, k, v, lengths, o, do, aug, cosine, sine, whole, moving=(), tq=512, unroll=4):
     rows, span, width = q.shape
     keys = k.shape[1]
     tq = min(tq, span)
@@ -817,11 +858,7 @@
     return pl.pallas_call(
         functools.partial(attend_back_kernel, tq, unroll, moves),
         grid=(rows, width // PAIR),
-        in_specs=[
-            qs, ks, ks,
-            pl.BlockSpec((1, keys, PAIR), lambda r, p: (r, 0, 0), pipeline_mode=pl.Buffered(1)),
-            qs, qs, qs, table, table,
-        ]
+        in_specs=[pl.BlockSpec(memory_space=pltpu.SMEM), qs, ks, ks, qs, qs, qs, table, table]
         + [hbm] * moves,
         out_specs=[qs, ks, ks] + result_specs,
         out_shape=[
@@ -842,15 +879,15 @@
         + extra,
         compiler_params=pltpu.CompilerParams(vmem_limit_bytes=VMEM_LIMIT, **more),
         name="attend_back",
-    )(q, k, v, bias, o, do, aug, cosine, sine, *moving)
+    )(lengths, q, k, v, o, do, aug, cosine, sine, *moving)
 
 
 def middle_kernel(
-    chunk, moves, x_ref, att_ref, cot_ref, wo_ref, wg_ref, wu_ref, wd_ref, g1_ref, g2_ref, *rest
+    chunk, moves, x_ref, att_ref, cot_ref, wo_ref, wg_ref, wu_ref, wd_ref, *rest
 ):
     source, rest = rest[:moves], rest[moves:]
-    (out_ref, dfirst_ref, datt_ref, act_ref, dg_ref, du_ref, ht_ref, dft_ref, at_ref, gg1_ref, gg2_ref) = rest[:11]
-    ca, cb = rest[11:13]
+    (out_ref, dfirst_ref, datt_ref, act_ref, dg_ref, du_ref, ht_ref, dft_ref, at_ref, gg_ref) = rest[:10]
+    ca, cb, gains = rest[10:13]
     if moves:
         arrived, dy_ref, send, recv = rest[13:]
         me = place()
@@ -885,10 +922,10 @@
 
     @pl.when(pl.program_id(0) == 0)
     def _():
-        gg1_ref[...] = jnp.zeros_like(gg1_ref)
-        gg2_ref[...] = jnp.zeros_like(gg2_ref)
-
-    gain1, gain2 = g1_ref[...], g2_ref[...]
+        gg_ref[...] = jnp.zeros_like(gg_ref)
+        gains[...] = wo_ref[:, x_ref.shape[1] :].astype(F32).T[:8]
+
+    gain1, gain2 = gains[0:1, :], gains[1:2, :]
     att = att_ref[...]
     at_ref[...] = att.T
     first = x_ref[...].astype(F32) + dot(att, wo_ref[:, : att.shape[1]])
@@ -916,7 +953,7 @@
     n2 = centered * s2
     out_ref[...] = (n2 * gain2).astype(BF)
     dy = dy_ref[...].astype(F32)
-    gg2_ref[...] += jnp.sum(dy * n2, axis=0, keepdims=True)
+    gg_ref[1:2, :] += jnp.sum(dy * n2, axis=0, keepdims=True)
     inner = dy * gain2
     d_second = s2 * (
         inner - jnp.mean(inner, axis=1, keepdims=True) - n2 * jnp.mean(inner * n2, axis=1, keepdims=True)
@@ -932,7 +969,7 @@
         dg_ref[:, at] = dg
         du_ref[:, at] = du
         d_hidden = d_hidden + dot_nt(dg, wg_ref[:, at]) + dot_nt(du, wu_ref[:, at])
-    gg1_ref[...] += jnp.sum(d_hidden * n1, axis=0, keepdims=True)
+    gg_ref[0:1, :] += jnp.sum(d_hidden * n1, axis=0, keepdims=True)
     inner = d_hidden * gain1
     d_first = s1 * (
         inner - jnp.mean(inner, axis=1, keepdims=True) - n1 * jnp.mean(inner * n1, axis=1, keepdims=True)
@@ -942,7 +979,7 @@
     datt_ref[...] = dot_nt(low, wo_ref[:, : low.shape[1]]).astype(BF)
 
 
-def middle_call(x, att, cot, wo, wg, wu, wd, g1, g2, tile=256, chunk=768):
+def middle_call(x, att, cot, wo, wg, wu, wd, tile=256, chunk=768):
     tokens, width = x.shape
     hidden_width = wg.shape[1]
     tile = min(tile, tokens)
@@ -969,21 +1006,21 @@
     def whole(a):
         return pl.BlockSpec(a.shape, lambda i: (0, 0), pipeline_mode=pl.Buffered(1))
 
-    gain = pl.BlockSpec((1, width), lambda i: (0, 0))
     return pl.pallas_call(
         functools.partial(middle_kernel, chunk, moves),
         grid=(tokens // tile,),
-        in_specs=[row, row, cot_row, whole(wo), whole(wg), whole(wu), whole(wd), gain, gain]
+        in_specs=[row, row, cot_row, whole(wo), whole(wg), whole(wu), whole(wd)]
         + [pl.BlockSpec(memory_space=pl.ANY)] * moves,
-        out_specs=[row, row, row, wide, wide, wide, column, column, column, gain, gain],
+        out_specs=[row, row, row, wide, wide, wide, column, column, column]
+        + [pl.BlockSpec((PAIR, width), lambda i: (0, 0))],
         out_shape=[jax.ShapeDtypeStruct((tokens, width), BF)] * 3
         + [jax.ShapeDtypeStruct((tokens, hidden_width), BF)] * 3
         + [jax.ShapeDtypeStruct((width, tokens), BF)] * 3
-        + [jax.ShapeDtypeStruct((1, width), F32)] * 2,
-        scratch_shapes=[pltpu.VMEM((tile, hidden_width), F32)] * 2 + extra,
+        + [jax.ShapeDtypeStruct((PAIR, width), F32)],
+        scratch_shapes=[pltpu.VMEM((tile, hidden_width), F32)] * 2 + [pltpu.VMEM((8, width), F32)] + extra,
         compiler_params=pltpu.CompilerParams(vmem_limit_bytes=VMEM_LIMIT, **more),
         name="middle",
-    )(x, att, cot, wo, wg, wu, wd, g1, g2, *([cot] * moves))
+    )(x, att, cot, wo, wg, wu, wd, *([cot] * moves))
 
 
 def outer_kernel(a_ref, b_ref, o_ref):
@@ -1059,7 +1096,7 @@
     def _():
         width = b4_ref.shape[1]
         o4_ref[:, :width] = dot(a3_ref[...], b4_ref[...])
-        o4_ref[:, width:] = gains_ref[...]
+        o4_ref[:, width:] = gains_ref[...].T
 
 
 def outers_call(h_t, df_t, att_t, d_gate, d_up, act, d_first, gains, moving=(), tile=512):
@@ -1085,10 +1122,10 @@
         in_specs=[whole(h_t), hbm, hbm] + [part(tokens, n) for n in range(3)] + [hbm, whole(gains)]
         + [hbm] * moves,
         out_specs=[part(width, n) for n in range(3)]
-        + [pl.BlockSpec((width, width + gains.shape[1]), lambda i: (0, 0), pipeline_mode=pl.Buffered(1))]
+        + [pl.BlockSpec((width, width + PAIR), lambda i: (0, 0), pipeline_mode=pl.Buffered(1))]
         + [hbm] * moves,
         out_shape=[jax.ShapeDtypeStruct((width, hidden), BF)] * 3
-        + [jax.ShapeDtypeStruct((width, width + gains.shape[1]), F32)]
+        + [jax.ShapeDtypeStruct((width, width + PAIR), F32)]
         + [jax.ShapeDtypeStruct(a.shape, BF) for a in moving],
         scratch_shapes=extra,
         compiler_params=pltpu.CompilerParams(vmem_limit_bytes=VMEM_LIMIT, **more),
@@ -1105,18 +1142,22 @@
 ):
     me = place()
     y = me["y"]
-    loads = [
-        pltpu.make_async_copy(a, b, local.at[i])
-        for i, (a, b) in enumerate(
-            ((w_hbm, w), (dq_hbm, dq), (dk_hbm, dk), (dv_hbm, dv), (first_hbm, first), (xt_hbm, xt))
-        )
-    ]
-    for load in loads:
-        load.start()
+    half = g.shape[1]
+
+    def load(n, a, b, which=None):
+        if which is not None:
+            at = pl.ds(pl.multiple_of(which * half, half), half)
+            a, b = a.at[at], b.at[at]
+        return pltpu.make_async_copy(a, b, local.at[n])
+
+    rows_hbm = ((dq_hbm, dq), (dk_hbm, dk), (dv_hbm, dv), (first_hbm, first))
+    early = [load(0, w_hbm, w)] + [load(1 + n, a, b, 1 - y) for n, (a, b) in enumerate(rows_hbm)]
+    later = [load(5, xt_hbm, xt)] + [load(6 + n, a, b, y) for n, (a, b) in enumerate(rows_hbm)]
+    for copy in early + later:
+        copy.start()
     greet(me)
     width = dq.shape[1]
-    half = g.shape[1]
-    tile = half // 2
+    tile = half // 4
 
     def rows_of(which, t):
         at = pl.ds(pl.multiple_of(which * half + t * tile, tile), tile)
@@ -1125,8 +1166,8 @@
             total += dot_nt(a[at, :], w[:, n * width : (n + 1) * width])
         g[which, pl.ds(t * tile, tile), :] = total.astype(BF)
 
-    for load in loads[:5]:
-        load.wait()
+    for copy in early:
+        copy.wait()
     quarter = half // 4
 
     def give(n, target_half):
@@ -1140,11 +1181,12 @@
             device_id_type=MESH,
         )
 
-    rows_of(1 - y, 0)
-    give(0, y).start()
-    give(1, y).start()
-    rows_of(1 - y, 1)
-    loads[5].wait()
+    for t in range(4):
+        rows_of(1 - y, t)
+        if t < 2:
+            give(t, y).start()
+    for copy in later:
+        copy.wait()
     reduces = []
     for n, (a, target) in enumerate(((dq, w0), (dk, w1), (dv, w2))):
         reduces.append(
@@ -1177,9 +1219,11 @@
     reduces[0].step(2)
     reduces[2].step(1)
     rows_of(y, 0)
+    rows_of(y, 1)
     reduces[1].step(2)
     reduces[0].step(3)
-    rows_of(y, 1)
+    rows_of(y, 2)
+    rows_of(y, 3)
     keep = pltpu.make_async_copy(g.at[y], g_out.at[y], local.at[0])
     keep.start()
     reduces[2].step(2)
@@ -1206,7 +1250,7 @@
     scratch += [pltpu.VMEM((2, tokens // 2, width), BF), full, full, full]
     sems = 4 + 3 * Reduce.SEMS
     scratch += [pltpu.SemaphoreType.DMA((sems,))] * 2
-    scratch += [pltpu.SemaphoreType.DMA((6,)), pltpu.SemaphoreType.DMA((6,))]
+    scratch += [pltpu.SemaphoreType.DMA((10,)), pltpu.SemaphoreType.DMA((6,))]
     for order in CLOSING_ORDERS:
         scratch += Reduce.scratch(*block, BF, order)
     return pl.pallas_call(
@@ -1273,18 +1317,16 @@
 
     cosine, sine = map(jnp.asarray, angle_tables(seq))
     gains = jnp.stack([gain_one, gain_two], 1)
+    w_out = jnp.pad(jnp.concatenate([w_out, gains], 1), ((0, 0), (0, PAIR - 2)))
     if own:
-        w_out = jnp.pad(jnp.concatenate([w_out, gains], 1), ((0, 0), (0, PAIR - 2)))
         x, f_qkv, q, k, v, xt, *moving = opening_call(
             tokens, w_qkv, w_out, w_gate, w_up, w_down, cosine, sine
         )
         x = x.reshape(1, seq, width)
-        length = lax.dynamic_slice_in_dim(lengths, mine, 1, 0)
         cq, sq = cosine, sine
     else:
         f_qkv, f_out, f_gate, f_up, f_down = map(gather, (w_qkv, w_out, w_gate, w_up, w_down))
-        f_gains = gather(gains).astype(F32)
-        x, cot, length = tokens, cotangent.reshape(rows * span, width), lengths
+        x, cot = tokens, cotangent.reshape(rows * span, width)
         cq = lax.dynamic_slice_in_dim(cosine, mine * span, span, 0)
         sq = lax.dynamic_slice_in_dim(sine, mine * span, span, 0)
     n, t = x.shape[:2]
@@ -1295,25 +1337,19 @@
     if not own:
         k = lax.all_gather(k, "blk", axis=1, tiled=True)
         v = lax.all_gather(v, "blk", axis=1, tiled=True)
-    position = jnp.arange(seq, dtype=jnp.int32)[None, :, None]
-    lane = jnp.arange(PAIR, dtype=jnp.int32)[None, None, :]
-    bias = jnp.where((lane % HEAD == 3) & (position >= length[:, None, None]), NEG, 0.0).astype(BF)
     if own:
         att, aug, f_out, f_gate, f_up, f_down = attend_call(
-            q, k, v, bias, moving
+            q, k, v, lengths, moving
         )
         f_out = f_out.reshape(width, -1)
-        f_gains = f_out[:, width : width + 2].astype(F32)
         cot = cotangent
         f_gate, f_up = f_gate.reshape(width, -1), f_up.reshape(width, -1)
         f_down = f_down.reshape(-1, width)
     else:
-        att, aug = attend_call(q, k, v, bias)
-    g1, g2 = f_gains[:, 0][None], f_gains[:, 1][None]
-    out, d_first, d_att, act, d_gate, d_up, h_t, df_t, att_t, gg1, gg2 = middle_call(
-        flat, att.reshape(n * t, width), cot, f_out, f_gate, f_up, f_down, g1, g2
+        att, aug = attend_call(q, k, v, lengths)
+    out, d_first, d_att, act, d_gate, d_up, h_t, df_t, att_t, gains = middle_call(
+        flat, att.reshape(n * t, width), cot, f_out, f_gate, f_up, f_down
     )
-    gains = jnp.pad(jnp.concatenate([gg1, gg2]).T, ((0, 0), (0, PAIR - 2)))
     moving = (out.reshape(2, span, width),) if own else ()
     gw_gate, gw_up, gw_down_t, gw_out, *moving = outers_call(
         h_t, df_t, att_t, d_gate, d_up, act, d_first, gains, moving
@@ -1323,7 +1359,7 @@
         wide = tuple(g.reshape(4, 2, 2, width // 16, -1) for g in (gw_gate, gw_up, gw_down_t))
         out = moving[0]
         dq, dk, dv, s_gate, s_up, s_down_t, s_out = attend_back_call(
-            q, k, v, bias, att, d_att, aug, cq, sq, True,
+            q, k, v, lengths, att, d_att, aug, cq, sq, True,
             wide + (gw_out.reshape(4, 2, 2, 2, width // 32, -1),),
         )
     else:
@@ -1334,7 +1370,7 @@
 
         s_gate, s_up, s_down_t = map(scatter_wide, (gw_gate, gw_up, gw_down_t))
         s_out = lax.psum_scatter(gw_out, axes, scatter_dimension=0, tiled=True)
-        dq, dk, dv = attend_back_call(q, k, v, bias, att, d_att, aug, cq, sq, False)
+        dq, dk, dv = attend_back_call(q, k, v, lengths, att, d_att, aug, cq, sq, False)
         dk = lax.psum_scatter(dk, "blk", scatter_dimension=1, tiled=True)
         dv = lax.psum_scatter(dv, "blk", scatter_dimension=1, tiled=True)
         heads = (dk * jnp.tile(sq, (1, width // PAIR))).reshape(n, t, HEADS, HEAD)

time: 508 us -> 497 us (0.978)
  no operation moved by 1% of the time
where the time goes in v8:
time: 497 us; the launch traced here: 489 us
  Pallas kernels  477 us (96%)
  local copies, waits for them, and re-layouts  10.4 us (2%)
    pallas_call x1, Pallas kernels, attend_back_call(): pl.pallas_call(functools.partial(attend_back_kernel, tq, unroll, moves),...  146 us
    pallas_call x1, Pallas kernels, middle_call(): pl.pallas_call(functools.partial(middle_kernel, chunk, moves), grid=(toke...  97.7 us
    pallas_call x1, Pallas kernels, attend_call(): pl.pallas_call(functools.partial(attend_kernel, tile, chunk, moves), grid...  75 us
    pallas_call x1, Pallas kernels, opening_call(): pl.pallas_call(opening_kernel, in_specs=[hbm] + [held] * 7, out_specs=[hb...  58.9 us
    pallas_call x1, Pallas kernels, closing_call(): pl.pallas_call(closing_kernel, in_specs=[hbm] * 6, out_specs=[hbm, pl.Blo...  51.5 us
    pallas_call x1, Pallas kernels, outers_call(): pl.pallas_call(functools.partial(outers_kernel, steps, moves), grid=(3 *...  47.3 us

profile of v8, /device:TPU:0, one launch (start us, length us, event | category | flops | bytes accessed | tf_op | source)
XLA Modules:
  0.0 489.4 jit_solution(7591627287603973437)
XLA Ops:
  0.6 0.7 copy.23
  1.4 0.7 copy.24
  2.1 1.5 fusion.4.out_shard
  3.6 58.9 %opening.1 = (bf16[2,1024,768]{2,1,0:T(8,128)(2,1)}, bf16[768,2304]{1,0:T(8,128)(2,1)}, bf16[2048,768]{1,0:T(8,128)(2,1)}, bf16[2048,768]{1,0:T(8,128)(2,1)}, bf...) custom-call(bf16[2,1024,768]{2,1,0:T(8,128)(2,1)} %tok_hbm.1, ...), custom_call_target="tpu_custom_call" | custom-call | tf_op jit(solution)/shard_map/opening/pallas_call | solution.py:503
  62.5 75.0 %attend.1 = (bf16[1,2048,768]{2,1,0:T(8,128)(2,1)}, bf16[1,2048,768]{2,1,0:T(8,128)(2,1)}, bf16[4,2,2,2,24,896]{5,4,3,2,1,0:T(8,128)(2,1)}, bf16[4,2,2,2,24,3072...) custom-call(s32[2]{0:T(128)} %len_ref.3, ...), custom_call_target="tpu_custom_call" | custom-call | tf_op jit(solution)/shard_map/attend/pallas_call | solution.py:694
  137.6 97.7 %middle.1 = (bf16[2048,768]{1,0:T(8,128)(2,1)}, bf16[2048,768]{1,0:T(8,128)(2,1)}, bf16[2048,768]{1,0:T(8,128)(2,1)}, bf16[2048,3072]{1,0:T(8,128)(2,1)}, bf16[2...) custom-call(bf16[2048,768]{1,0:T(8,128)(2,1)} %bitcast.39, ...), custom_call_target="tpu_custom_call" | custom-call | tf_op jit(solution)/shard_map/middle/pallas_call | solution.py:1009
  235.2 47.3 %outers.1 = (bf16[768,3072]{1,0:T(8,128)(2,1)}, bf16[768,3072]{1,0:T(8,128)(2,1)}, bf16[768,3072]{1,0:T(8,128)(2,1)}, f32[768,896]{1,0:T(8,128)}, bf16[2,1024,768]{2,1,0:T(8,128)(2,1)}) custom-call(bf16[768,2048]{1,0:T(8,128)(2,1)} %get-tuple-element.64.a1_ref, bf16[768,2048]{1,0:T(8,128)(2,1)} %get-tuple-element.65.a2_hbm, ...), custom_call_target="tpu_custom_call" | custom-call | tf_op jit(solution)/shard_map/outers/pallas_call | solution.py:1119
  282.5 146.1 %attend_back.1 = (bf16[1,2048,768]{2,1,0:T(8,128)(2,1)}, bf16[1,2048,768]{2,1,0:T(8,128)(2,1)}, bf16[1,2048,768]{2,1,0:T(8,128)(2,1)}, f32[48,1536]{1,0:T(8,128)...) custom-call(s32[2]{0:T(128)} %len_ref.3, bf16[1,2048,768]{2,1,0:T(8,128)(2,1)} %bitcast.22, ...), custom_call_target="tpu_custom_call" | custom-call | tf_op jit(solution)/shard_map/attend_back/pallas_call | solution.py:858
  428.6 0.0 copy-start.6
  428.6 0.0 copy-start
  428.6 51.5 %closing.1 = (bf16[2,1024,768]{2,1,0:T(8,128)(2,1)}, f32[24,2304]{1,0:T(8,128)}) custom-call(bf16[2048,768]{1,0:T(8,128)(2,1)} %bitcast.35, bf16[2048,768]{1,0:T(8,128)(2,1)} %bitcast.36, bf16[2048,768]{1,0:T(8,128)(2,1)} %bitcast.37, bf16[2048,768]{1,0:T(8,128)(2,1)} %get-tuple-element.70.b4_hbm.first_hbm, bf16[768,2048]{1,0:T(8,128)(2,1)} %get-tuple-element.83.xt_hbm, ...), custom_call_target="tpu_custom_call" | custom-call | tf_op jit(solution)/shard_map/closing/pallas_call | solution.py:1256
  480.2 0.0 copy-done.6
  480.2 0.7 slice_reduce_fusion
  480.9 0.6 slice.12
  481.5 0.0 copy-done
  481.5 0.0 copy-start.1
  481.5 1.7 copy.31
  483.2 1.4 copy-done.1
  484.5 0.0 copy-start.5
  484.5 0.0 copy-start.4
  484.6 0.0 copy-start.3
  484.6 0.0 copy-start.2
  484.6 1.7 copy.32
  486.2 0.0 copy-done.5
  486.2 0.7 copy.33
  486.9 0.0 copy-done.4
  486.9 0.7 copy.34
  487.6 0.0 copy-done.3
  487.6 0.7 copy.35
  488.3 0.0 copy-done.2
  488.3 0.7 copy.36
Async XLA Ops:
  428.6 51.5 %copy-start.6 = (f32[24,896]{1,0:T(8,128)S(1)}, f32[24,896]{1,0:T(8,128)}, u32[]{:S(2)}) copy-start(f32[24,896]{1,0:T(8,128)} %get-tuple-element.87) | copy-start | bytes 258052
  428.6 52.9 %copy-start = (bf16[2,1024,768]{2,1,0:T(8,128)(2,1)S(1)}, bf16[2,1024,768]{2,1,0:T(8,128)(2,1)}, u32[]{:S(2)}) copy-start(bf16[2,1024,768]{2,1,0:T(8,128)(2,1)} %get-tuple-element.102) | copy-start | bytes 9437188
  481.5 3.0 copy-start.1
  484.5 1.7 copy-start.5
  484.5 2.4 copy-start.4
  484.6 3.1 copy-start.3
  484.6 3.8 copy-start.2

commit v9 on v8

--- a/solution.py
+++ b/solution.py
@@ -808,8 +808,8 @@
 
 BACK_ORDERS = ("yx", "xy", "zyx", "xy")
 BACK_PLAN = (
-    (1, 0, 1), (1, 1, 1), (1, 2, 1), (1, 3, 1), (3, 0, 2), (3, 1, 2), (3, 3, 2), (4, 0, 3), (4, 1, 3), (4, 2, 2),
-    (4, 3, 3), (5, 0, 4), (5, 2, 3),
+    (1, 0, 1), (1, 1, 1), (1, 2, 1), (1, 3, 1), (3, 0, 2), (3, 1, 2), (4, 0, 3), (4, 1, 3), (4, 2, 2), (4, 3, 2),
+    (5, 0, 4), (5, 2, 3), (5, 3, 3),
 )
 BACK_LAST = (2, 1, 3)
 
@@ -1164,14 +1164,14 @@
         total = first[at, :].astype(F32)
         for n, a in enumerate((dq, dk, dv)):
             total += dot_nt(a[at, :], w[:, n * width : (n + 1) * width])
-        g[which, pl.ds(t * tile, tile), :] = total.astype(BF)
+        g[which, pl.ds(pl.multiple_of(t * tile, tile), tile), :] = total.astype(BF)
 
     for copy in early:
         copy.wait()
     quarter = half // 4
 
     def give(n, target_half):
-        part = pl.ds(n * quarter, quarter)
+        part = pl.ds(n * quarter if isinstance(n, int) else pl.multiple_of(n * quarter, quarter), quarter)
         return pltpu.make_async_remote_copy(
             src_ref=g.at[1 - y, part],
             dst_ref=g_out.at[target_half, part],
@@ -1181,10 +1181,16 @@
             device_id_type=MESH,
         )
 
-    for t in range(4):
+    def away(t, _):
         rows_of(1 - y, t)
-        if t < 2:
-            give(t, y).start()
+        pl.when(t < 2)(lambda: give(t, y).start())
+        return 0
+
+    def home(t, _):
+        rows_of(y, t)
+        return 0
+
+    lax.fori_loop(0, 4, away, 0)
     for copy in later:
         copy.wait()
     reduces = []
@@ -1218,12 +1224,10 @@
     reduces[1].step(1)
     reduces[0].step(2)
     reduces[2].step(1)
-    rows_of(y, 0)
-    rows_of(y, 1)
+    lax.fori_loop(0, 2, home, 0)
     reduces[1].step(2)
     reduces[0].step(3)
-    rows_of(y, 2)
-    rows_of(y, 3)
+    lax.fori_loop(2, 4, home, 0)
     keep = pltpu.make_async_copy(g.at[y], g_out.at[y], local.at[0])
     keep.start()
     reduces[2].step(2)

time: 497 us -> 496 us (level)
  no operation moved by 1% of the time
where the time goes in v9:
time: 496 us; the launch traced here: 489 us
  Pallas kernels  476 us (96%)
  local copies, waits for them, and re-layouts  10.4 us (2%)
    pallas_call x1, Pallas kernels, attend_back_call(): pl.pallas_call(functools.partial(attend_back_kernel, tq, unroll, moves),...  146 us
    pallas_call x1, Pallas kernels, middle_call(): pl.pallas_call(functools.partial(middle_kernel, chunk, moves), grid=(toke...  97.7 us
    pallas_call x1, Pallas kernels, attend_call(): pl.pallas_call(functools.partial(attend_kernel, tile, chunk, moves), grid...  75 us
    pallas_call x1, Pallas kernels, opening_call(): pl.pallas_call(opening_kernel, in_specs=[hbm] + [held] * 7, out_specs=[hb...  58.9 us
    pallas_call x1, Pallas kernels, closing_call(): pl.pallas_call(closing_kernel, in_specs=[hbm] * 6, out_specs=[hbm, pl.Blo...  50.6 us
    pallas_call x1, Pallas kernels, outers_call(): pl.pallas_call(functools.partial(outers_kernel, steps, moves), grid=(3 *...  47.3 us

profile of v9, /device:TPU:0, one launch (start us, length us, event | category | flops | bytes accessed | tf_op | source)
XLA Modules:
  0.0 488.6 jit_solution(4631610938832644017)
XLA Ops:
  0.6 0.7 copy.23
  1.4 0.7 copy.24
  2.1 1.5 fusion.4.out_shard
  3.6 58.9 %opening.1 = (bf16[2,1024,768]{2,1,0:T(8,128)(2,1)}, bf16[768,2304]{1,0:T(8,128)(2,1)}, bf16[2048,768]{1,0:T(8,128)(2,1)}, bf16[2048,768]{1,0:T(8,128)(2,1)}, bf...) custom-call(bf16[2,1024,768]{2,1,0:T(8,128)(2,1)} %tok_hbm.1, ...), custom_call_target="tpu_custom_call" | custom-call | tf_op jit(solution)/shard_map/opening/pallas_call | solution.py:503
  62.5 75.0 %attend.1 = (bf16[1,2048,768]{2,1,0:T(8,128)(2,1)}, bf16[1,2048,768]{2,1,0:T(8,128)(2,1)}, bf16[4,2,2,2,24,896]{5,4,3,2,1,0:T(8,128)(2,1)}, bf16[4,2,2,2,24,3072...) custom-call(s32[2]{0:T(128)} %len_ref.3, ...), custom_call_target="tpu_custom_call" | custom-call | tf_op jit(solution)/shard_map/attend/pallas_call | solution.py:694
  137.6 97.7 %middle.1 = (bf16[2048,768]{1,0:T(8,128)(2,1)}, bf16[2048,768]{1,0:T(8,128)(2,1)}, bf16[2048,768]{1,0:T(8,128)(2,1)}, bf16[2048,3072]{1,0:T(8,128)(2,1)}, bf16[2...) custom-call(bf16[2048,768]{1,0:T(8,128)(2,1)} %bitcast.39, ...), custom_call_target="tpu_custom_call" | custom-call | tf_op jit(solution)/shard_map/middle/pallas_call | solution.py:1009
  235.2 47.3 %outers.1 = (bf16[768,3072]{1,0:T(8,128)(2,1)}, bf16[768,3072]{1,0:T(8,128)(2,1)}, bf16[768,3072]{1,0:T(8,128)(2,1)}, f32[768,896]{1,0:T(8,128)}, bf16[2,1024,768]{2,1,0:T(8,128)(2,1)}) custom-call(bf16[768,2048]{1,0:T(8,128)(2,1)} %get-tuple-element.64.a1_ref, bf16[768,2048]{1,0:T(8,128)(2,1)} %get-tuple-element.65.a2_hbm, ...), custom_call_target="tpu_custom_call" | custom-call | tf_op jit(solution)/shard_map/outers/pallas_call | solution.py:1119
  282.5 146.1 %attend_back.1 = (bf16[1,2048,768]{2,1,0:T(8,128)(2,1)}, bf16[1,2048,768]{2,1,0:T(8,128)(2,1)}, bf16[1,2048,768]{2,1,0:T(8,128)(2,1)}, f32[48,1536]{1,0:T(8,128)...) custom-call(s32[2]{0:T(128)} %len_ref.3, bf16[1,2048,768]{2,1,0:T(8,128)(2,1)} %bitcast.22, ...), custom_call_target="tpu_custom_call" | custom-call | tf_op jit(solution)/shard_map/attend_back/pallas_call | solution.py:858
  428.6 0.0 copy-start.6
  428.6 0.0 copy-start
  428.7 50.6 %closing.1 = (bf16[2,1024,768]{2,1,0:T(8,128)(2,1)}, f32[24,2304]{1,0:T(8,128)}) custom-call(bf16[2048,768]{1,0:T(8,128)(2,1)} %bitcast.35, bf16[2048,768]{1,0:T(8,128)(2,1)} %bitcast.36, bf16[2048,768]{1,0:T(8,128)(2,1)} %bitcast.37, bf16[2048,768]{1,0:T(8,128)(2,1)} %get-tuple-element.70.b4_hbm.first_hbm, bf16[768,2048]{1,0:T(8,128)(2,1)} %get-tuple-element.83.xt_hbm, ...), custom_call_target="tpu_custom_call" | custom-call | tf_op jit(solution)/shard_map/closing/pallas_call | solution.py:1260
  479.3 0.0 copy-done.6
  479.3 0.7 slice_reduce_fusion
  480.0 0.6 slice.12
  480.6 0.0 copy-done
  480.6 0.0 copy-start.1
  480.6 1.7 copy.31
  482.3 1.4 copy-done.1
  483.7 0.0 copy-start.5
  483.7 0.0 copy-start.4
  483.7 0.0 copy-start.3
  483.7 0.0 copy-start.2
  483.7 1.7 copy.32
  485.3 0.0 copy-done.5
  485.3 0.7 copy.33
  486.0 0.0 copy-done.4
  486.0 0.7 copy.34
  486.8 0.0 copy-done.3
  486.8 0.7 copy.35
  487.5 0.0 copy-done.2
  487.5 0.7 copy.36
Async XLA Ops:
  428.6 50.7 %copy-start.6 = (f32[24,896]{1,0:T(8,128)S(1)}, f32[24,896]{1,0:T(8,128)}, u32[]{:S(2)}) copy-start(f32[24,896]{1,0:T(8,128)} %get-tuple-element.87) | copy-start | bytes 258052
  428.6 52.0 %copy-start = (bf16[2,1024,768]{2,1,0:T(8,128)(2,1)S(1)}, bf16[2,1024,768]{2,1,0:T(8,128)(2,1)}, u32[]{:S(2)}) copy-start(bf16[2,1024,768]{2,1,0:T(8,128)(2,1)} %get-tuple-element.102) | copy-start | bytes 9437188
  480.6 3.0 copy-start.1
  483.7 1.7 copy-start.5
  483.7 2.4 copy-start.4
  483.7 3.1 copy-start.3
  483.7 3.8 copy-start.2

commit v10 on v8

--- a/solution.py
+++ b/solution.py
@@ -382,10 +382,19 @@
 
 
 def opening_kernel(
-    tok_hbm, w_shard, out_shard, gate_shard, up_shard, down_shard, cos_ref, sin_ref,
+    tok_hbm, w_shard, out_ref, one_ref, two_ref, gate_shard, up_shard, down_shard, cos_ref, sin_ref,
     x_hbm, w_hbm, q_hbm, k_hbm, v_hbm, xt_hbm, out_part, gate_part, up_part, left_part, right_part,
-    x, w_blocks, w, q, k, v, xt, send, recv, local, load, store,
+    x, w_blocks, w, q, k, v, xt, out_shard, send, recv, local, load, store,
 ):
+    count, columns = out_ref.shape
+    square = (count, count)
+    same = lax.broadcasted_iota(jnp.int32, square, 0) == lax.broadcasted_iota(jnp.int32, square, 1)
+    one, two = (
+        jnp.sum(jnp.where(same, ref[...].astype(F32), 0.0), axis=1, keepdims=True) for ref in (one_ref, two_ref)
+    )
+    lane = lanes((count, PAIR))
+    out_shard[:, :columns] = out_ref[...]
+    out_shard[:, columns:] = jnp.where(lane == 0, one, jnp.where(lane == 1, two, 0.0)).astype(BF)
     me = place()
     y = me["y"]
     greet(me)
@@ -489,7 +498,7 @@
     keep_x.wait()
 
 
-def opening_call(tokens, w_qkv, w_out, w_gate, w_up, w_down, cosine, sine):
+def opening_call(tokens, w_qkv, w_out, gain_one, gain_two, w_gate, w_up, w_down, cosine, sine):
     rows, span, width = tokens.shape
     total = rows * span
     hbm = pl.BlockSpec(memory_space=pl.ANY)
@@ -497,12 +506,13 @@
     whole = (width, w_qkv.shape[1])
     flat = (total, width)
     shapes = [tokens.shape, whole, flat, flat, flat, (width, total)]
-    shapes += [(4, 2) + w_out.shape, (4, 2) + w_gate.shape, (4,) + w_up.shape]
+    out_shape = (w_out.shape[0], width + PAIR)
+    shapes += [(4, 2) + out_shape, (4, 2) + w_gate.shape, (4,) + w_up.shape]
     shapes += [(2, w_down.shape[0], w_down.shape[1] // 2)] * 2
     sems = 2 + sum(map(Gather.sems, OPENING_ORDERS))
     return pl.pallas_call(
         opening_kernel,
-        in_specs=[hbm] + [held] * 7,
+        in_specs=[hbm] + [held] * 9,
         out_specs=[hbm] * len(shapes),
         out_shape=[jax.ShapeDtypeStruct(shape, BF) for shape in shapes],
         scratch_shapes=[
@@ -513,6 +523,7 @@
             pltpu.VMEM(flat, BF),
             pltpu.VMEM(flat, BF),
             pltpu.VMEM((width, total), BF),
+            pltpu.VMEM(out_shape, BF),
             pltpu.SemaphoreType.DMA((sems,)),
             pltpu.SemaphoreType.DMA((sems,)),
             pltpu.SemaphoreType.DMA((len(OPENING_ORDERS),)),
@@ -523,7 +534,7 @@
             vmem_limit_bytes=VMEM_LIMIT, collective_id=0, has_side_effects=True
         ),
         name="opening",
-    )(tokens, w_qkv, w_out, w_gate, w_up, w_down, cosine, sine)
+    )(tokens, w_qkv, w_out, gain_one[None], gain_two[None], w_gate, w_up, w_down, cosine, sine)
 
 
 def key_mask(len_ref, own, keys, other):
@@ -1316,15 +1327,15 @@
         return lax.all_gather(a, axes, axis=0, tiled=True)
 
     cosine, sine = map(jnp.asarray, angle_tables(seq))
-    gains = jnp.stack([gain_one, gain_two], 1)
-    w_out = jnp.pad(jnp.concatenate([w_out, gains], 1), ((0, 0), (0, PAIR - 2)))
     if own:
         x, f_qkv, q, k, v, xt, *moving = opening_call(
-            tokens, w_qkv, w_out, w_gate, w_up, w_down, cosine, sine
+            tokens, w_qkv, w_out, gain_one, gain_two, w_gate, w_up, w_down, cosine, sine
         )
         x = x.reshape(1, seq, width)
         cq, sq = cosine, sine
     else:
+        gains = jnp.stack([gain_one, gain_two], 1)
+        w_out = jnp.pad(jnp.concatenate([w_out, gains], 1), ((0, 0), (0, PAIR - 2)))
         f_qkv, f_out, f_gate, f_up, f_down = map(gather, (w_qkv, w_out, w_gate, w_up, w_down))
         x, cot = tokens, cotangent.reshape(rows * span, width)
         cq = lax.dynamic_slice_in_dim(cosine, mine * span, span, 0)

time: 497 us -> 494 us (level)
  no operation moved by 1% of the time
where the time goes in v10:
time: 494 us; the launch traced here: 487 us
  Pallas kernels  477 us (97%)
  local copies, waits for them, and re-layouts  8.88 us (2%)
    pallas_call x1, Pallas kernels, attend_back_call(): pl.pallas_call(functools.partial(attend_back_kernel, tq, unroll, moves),...  146 us
    pallas_call x1, Pallas kernels, middle_call(): pl.pallas_call(functools.partial(middle_kernel, chunk, moves), grid=(toke...  97.7 us
    pallas_call x1, Pallas kernels, attend_call(): pl.pallas_call(functools.partial(attend_kernel, tile, chunk, moves), grid...  75.1 us
    pallas_call x1, Pallas kernels, opening_call(): pl.pallas_call(opening_kernel, in_specs=[hbm] + [held] * 9, out_specs=[hb...  59 us
    pallas_call x1, Pallas kernels, closing_call(): pl.pallas_call(closing_kernel, in_specs=[hbm] * 6, out_specs=[hbm, pl.Blo...  51.5 us
    pallas_call x1, Pallas kernels, outers_call(): pl.pallas_call(functools.partial(outers_kernel, steps, moves), grid=(3 *...  47.2 us

profile of v10, /device:TPU:0, one launch (start us, length us, event | category | flops | bytes accessed | tf_op | source)
XLA Modules:
  0.0 486.6 jit_solution(3924105772850631951)
XLA Ops:
  0.6 59.0 %opening.1 = (bf16[2,1024,768]{2,1,0:T(8,128)(2,1)}, bf16[768,2304]{1,0:T(8,128)(2,1)}, bf16[2048,768]{1,0:T(8,128)(2,1)}, bf16[2048,768]{1,0:T(8,128)(2,1)}, bf...) custom-call(bf16[2,1024,768]{2,1,0:T(8,128)(2,1)} %tok_hbm.1, ...), custom_call_target="tpu_custom_call" | custom-call | tf_op jit(solution)/shard_map/opening/pallas_call | solution.py:513
  59.6 75.1 %attend.1 = (bf16[1,2048,768]{2,1,0:T(8,128)(2,1)}, bf16[1,2048,768]{2,1,0:T(8,128)(2,1)}, bf16[4,2,2,2,24,896]{5,4,3,2,1,0:T(8,128)(2,1)}, bf16[4,2,2,2,24,3072...) custom-call(s32[2]{0:T(128)} %len_ref.3, ...), custom_call_target="tpu_custom_call" | custom-call | tf_op jit(solution)/shard_map/attend/pallas_call | solution.py:705
  134.8 97.7 %middle.1 = (bf16[2048,768]{1,0:T(8,128)(2,1)}, bf16[2048,768]{1,0:T(8,128)(2,1)}, bf16[2048,768]{1,0:T(8,128)(2,1)}, bf16[2048,3072]{1,0:T(8,128)(2,1)}, bf16[2...) custom-call(bf16[2048,768]{1,0:T(8,128)(2,1)} %bitcast.39, ...), custom_call_target="tpu_custom_call" | custom-call | tf_op jit(solution)/shard_map/middle/pallas_call | solution.py:1020
  232.4 47.2 %outers.1 = (bf16[768,3072]{1,0:T(8,128)(2,1)}, bf16[768,3072]{1,0:T(8,128)(2,1)}, bf16[768,3072]{1,0:T(8,128)(2,1)}, f32[768,896]{1,0:T(8,128)}, bf16[2,1024,768]{2,1,0:T(8,128)(2,1)}) custom-call(bf16[768,2048]{1,0:T(8,128)(2,1)} %get-tuple-element.64.a1_ref, bf16[768,2048]{1,0:T(8,128)(2,1)} %get-tuple-element.65.a2_hbm, ...), custom_call_target="tpu_custom_call" | custom-call | tf_op jit(solution)/shard_map/outers/pallas_call | solution.py:1130
  279.7 146.2 %attend_back.1 = (bf16[1,2048,768]{2,1,0:T(8,128)(2,1)}, bf16[1,2048,768]{2,1,0:T(8,128)(2,1)}, bf16[1,2048,768]{2,1,0:T(8,128)(2,1)}, f32[48,1536]{1,0:T(8,128)...) custom-call(s32[2]{0:T(128)} %len_ref.3, bf16[1,2048,768]{2,1,0:T(8,128)(2,1)} %bitcast.22, ...), custom_call_target="tpu_custom_call" | custom-call | tf_op jit(solution)/shard_map/attend_back/pallas_call | solution.py:869
  425.8 0.0 copy-start.6
  425.9 0.0 copy-start
  425.9 51.5 %closing.1 = (bf16[2,1024,768]{2,1,0:T(8,128)(2,1)}, f32[24,2304]{1,0:T(8,128)}) custom-call(bf16[2048,768]{1,0:T(8,128)(2,1)} %bitcast.35, bf16[2048,768]{1,0:T(8,128)(2,1)} %bitcast.36, bf16[2048,768]{1,0:T(8,128)(2,1)} %bitcast.37, bf16[2048,768]{1,0:T(8,128)(2,1)} %get-tuple-element.70.b4_hbm.first_hbm, bf16[768,2048]{1,0:T(8,128)(2,1)} %get-tuple-element.83.xt_hbm, ...), custom_call_target="tpu_custom_call" | custom-call | tf_op jit(solution)/shard_map/closing/pallas_call | solution.py:1267
  477.4 0.0 copy-done.6
  477.4 0.7 slice_reduce_fusion
  478.1 0.6 slice.12
  478.7 0.0 copy-done
  478.7 0.0 copy-start.1
  478.7 1.7 copy.27
  480.4 1.4 copy-done.1
  481.7 0.0 copy-start.5
  481.7 0.0 copy-start.4
  481.7 0.0 copy-start.3
  481.7 0.0 copy-start.2
  481.8 1.7 copy.28
  483.4 0.0 copy-done.5
  483.4 0.7 copy.29
  484.1 0.0 copy-done.4
  484.1 0.7 copy.30
  484.8 0.0 copy-done.3
  484.8 0.7 copy.31
  485.5 0.0 copy-done.2
  485.5 0.7 copy.32
Async XLA Ops:
  425.8 51.5 %copy-start.6 = (f32[24,896]{1,0:T(8,128)S(1)}, f32[24,896]{1,0:T(8,128)}, u32[]{:S(2)}) copy-start(f32[24,896]{1,0:T(8,128)} %get-tuple-element.87) | copy-start | bytes 258052
  425.9 52.9 %copy-start = (bf16[2,1024,768]{2,1,0:T(8,128)(2,1)S(1)}, bf16[2,1024,768]{2,1,0:T(8,128)(2,1)}, u32[]{:S(2)}) copy-start(bf16[2,1024,768]{2,1,0:T(8,128)(2,1)} %get-tuple-element.102) | copy-start | bytes 9437188
  478.7 3.0 copy-start.1
  481.7 1.7 copy-start.5
  481.7 2.4 copy-start.4
  481.7 3.1 copy-start.3
  481.7 3.8 copy-start.2
